TPU v7x, 128 devices: a whole 4x4x4 slice. The times are simulated.
128 devices in a mesh: grid: 8 (over x, core), mesh: 16 (over y, z).
Axes of the slice: x: 4, y: 4, z: 4, core: 2. Of those that a mesh axis runs over, the one named last changes fastest.
Arguments:
- grid_inputs: bfloat16 [393216, 227], P(('grid', 'mesh')), may hold values from -6 to 6
- embed_weight: bfloat16 [227, 512], replicated, may hold values from -0.375 to 0.375
- send_weight: bfloat16 [512, 512], replicated, may hold values from -0.25 to 0.25
- g2m_dest: int32 [3072, 3], P(('grid', 'mesh')), may hold values from 0 to 63, all different within a row
- g2m_edges: bfloat16 [3072, 3, 128, 128], P(('grid', 'mesh')), may hold values from -0.3125 to 0.3125
- encode_weight: bfloat16 [512, 512], replicated, may hold values from -0.25 to 0.25
- adj_codes: int32 [16, 32, 4], P('grid', 'mesh'), may hold values from 0 to 8
- adj_count: int32 [16, 32], P('grid', 'mesh'), may hold values from 1 to 4
- couplings: bfloat16 [16, 32, 4, 128, 128], P('grid', 'mesh'), may hold values from -0.25 to 0.25
- message_weight: bfloat16 [2, 512, 512], replicated, may hold values from -0.25 to 0.25
- node_weight: bfloat16 [2, 512, 512], replicated, may hold values from -0.25 to 0.25
- decode_weight: bfloat16 [512, 512], replicated, may hold values from -0.25 to 0.25
- m2g_src: int32 [3072, 3], P(('grid', 'mesh')), may hold values from 0 to 63, all different within a row
- m2g_edges: bfloat16 [3072, 3, 128, 128], P(('grid', 'mesh')), may hold values from -0.3125 to 0.3125
- output_weight: bfloat16 [512, 227], replicated, may hold values from -0.25 to 0.25
Outputs:
- prediction: bfloat16 [393216, 227], P(('grid', 'mesh'))
Inputs may be any that keep to these rules, and one draw needn't show every extreme that they name: `g2m_dest`: each row names 3 different codes; code c is patch row c // 32 of the block's band and column c % 32. `m2g_src`: each row names 3 different codes, read as for g2m_dest. `adj_codes`: codes may repeat within a patch.
All inputs are finite; a program needn't handle non-finite values.
Results may differ from a plain program's by a relative error of at most 0.027.
Values may be sent and summed in bfloat16 or wider, within the bound.
No kernel may reach another device: no remote copies, remote signals or barrier semaphores. Data moves between devices by JAX's collectives and lax.ppermute only.
A program may use at most 128 MiB of HBM per device.

v0:
```python
import jax
import jax.numpy as jnp
from jax import lax
from jax.sharding import PartitionSpec as P

epsilon = 1e-05


def padded_2(value, sides, width):
    for axis, dim in sides:
        size, length = (lax.axis_size(axis), value.shape[dim])
        up = [(i, (i + 1) % size) for i in range(size - 1)]
        down = [(j, i) for i, j in up]
        last = lax.slice_in_dim(value, length - width, length, axis=dim)
        first = lax.slice_in_dim(value, 0, width, axis=dim)
        before = lax.ppermute(last, axis, up)
        after = lax.ppermute(first, axis, down)
        value = jnp.concatenate([before, value, after], axis=dim)
    return value


def per_device(
    grid_inputs,
    embed_weight,
    send_weight,
    g2m_dest,
    g2m_edges,
    encode_weight,
    adj_codes,
    adj_count,
    couplings,
    message_weight,
    node_weight,
    decode_weight,
    m2g_src,
    m2g_edges,
    output_weight,
):
    feat_width = embed_weight.shape[1]
    block_size = g2m_edges.shape[2]
    slot_count = couplings.shape[2]
    rows_dev, cols_dev = adj_count.shape
    columns = cols_dev * lax.axis_size("mesh")
    grid_latent = jax.nn.silu(
        jnp.dot(grid_inputs, embed_weight, preferred_element_type=jnp.float32)
    ).astype(jnp.bfloat16)
    grid_proj = jnp.dot(grid_latent, send_weight, preferred_element_type=jnp.float32).astype(
        jnp.bfloat16
    )
    grid_proj = grid_proj.reshape(-1, block_size, feat_width)
    messages = jnp.einsum(
        "bjmn,bmd->bjnd", g2m_edges, grid_proj, preferred_element_type=jnp.float32
    )
    messages = messages.reshape(-1, block_size, feat_width)
    dest_codes = g2m_dest.reshape(-1)
    band_row = dest_codes // columns
    column_all = dest_codes % columns
    slot_ids = (column_all // cols_dev * rows_dev + band_row) * cols_dev + column_all % cols_dev
    own_rows = rows_dev * cols_dev * block_size
    first_patch = 0 // block_size
    patch_total = own_rows * lax.axis_size("mesh") // block_size
    wanted = first_patch + lax.iota(jnp.int32, patch_total)
    select = (wanted[:, None] == slot_ids[None, :]).astype(jnp.float32)
    term_part = jnp.einsum("qk,knd->qnd", select, messages, precision=lax.Precision.HIGHEST)
    band_total = lax.psum(
        term_part.reshape(patch_total * block_size, feat_width).astype(jnp.bfloat16), "mesh"
    ).astype(jnp.float32)
    encoded = lax.dynamic_slice_in_dim(band_total, lax.axis_index("mesh") * own_rows, own_rows, 0)
    enc_act = jax.nn.silu(encoded).astype(jnp.bfloat16)
    mesh_state = jnp.dot(enc_act, encode_weight, preferred_element_type=jnp.float32).astype(
        jnp.bfloat16
    )
    patch_rows = lax.iota(jnp.int32, rows_dev)[:, None, None] + adj_codes // 3
    patch_cols = lax.iota(jnp.int32, cols_dev)[None, :, None] + adj_codes % 3
    neighbour_index = (patch_rows * (cols_dev + 2) + patch_cols).reshape(-1)
    live_mask = lax.iota(jnp.int32, slot_count)[None, None, :] < adj_count[:, :, None]
    live_couplings = couplings * live_mask[:, :, :, None, None].astype(jnp.bfloat16)
    live_couplings = live_couplings.reshape(rows_dev * cols_dev, slot_count, block_size, block_size)
    for layer_index in range(message_weight.shape[0]):
        sent_state = jnp.dot(
            mesh_state, message_weight[layer_index], preferred_element_type=jnp.float32
        ).astype(jnp.bfloat16)
        sent_state = sent_state.reshape(rows_dev, cols_dev, block_size, feat_width)
        padded = padded_2(sent_state, (("grid", 0), ("mesh", 1)), 1)
        padded = padded.reshape(-1, block_size, feat_width)
        neighbours = padded[neighbour_index].reshape(
            rows_dev * cols_dev, slot_count, block_size, feat_width
        )
        gathered_sum = jnp.einsum(
            "pamn,pamd->pnd", live_couplings, neighbours, preferred_element_type=jnp.float32
        )
        activated = jax.nn.silu(gathered_sum.reshape(-1, feat_width))
        normed = (
            activated * lax.rsqrt(jnp.mean(activated * activated, axis=-1, keepdims=True) + epsilon)
        ).astype(jnp.bfloat16)
        mesh_state = (
            mesh_state.astype(jnp.float32)
            + jnp.dot(normed, node_weight[layer_index], preferred_element_type=jnp.float32)
        ).astype(jnp.bfloat16)
    mesh_patches = mesh_state.reshape(rows_dev, cols_dev, block_size, feat_width)
    shard_piece = lax.all_gather(mesh_patches, "mesh", axis=1, tiled=True)
    flat_piece = shard_piece.reshape(-1, feat_width)
    projected = jnp.dot(flat_piece, decode_weight, preferred_element_type=jnp.float32).astype(
        jnp.bfloat16
    )
    band_proj = projected.reshape(shard_piece.shape)
    band_proj = band_proj.reshape(-1, block_size, feat_width)
    taken = band_proj[m2g_src]
    decoded = jnp.einsum("bjmn,bjmd->bnd", m2g_edges, taken, preferred_element_type=jnp.float32)
    grid_hidden = jax.nn.silu(decoded.reshape(-1, feat_width)).astype(jnp.bfloat16)
    prediction = grid_inputs.astype(jnp.float32) + jnp.dot(
        grid_hidden, output_weight, preferred_element_type=jnp.float32
    )
    return prediction.astype(jnp.bfloat16)


def solution(mesh):
    placed = (
        P(("grid", "mesh"), None),
        P(),
        P(),
        P(("grid", "mesh"), None),
        P(("grid", "mesh"), None, None, None),
        P(),
        P("grid", "mesh", None),
        P("grid", "mesh"),
        P("grid", "mesh", None, None, None),
        P(),
        P(),
        P(),
        P(("grid", "mesh"), None),
        P(("grid", "mesh"), None, None, None),
        P(),
    )
    return jax.shard_map(
        per_device, mesh=mesh, in_specs=placed, out_specs=P(("grid", "mesh"), None), check_vma=False
    )
```

profile of v0, /device:TPU:2, one launch (start us, length us, event | category | flops | bytes accessed | tf_op | source)
XLA Modules:
  0.0 404.5 jit_solution(7013693609545710749)
XLA Ops:
  6.5 6.8 %convolution_convert_fusion.2 = bf16[3072,512]{1,0:T(8,128)(2,1)} fusion(bf16[512,512]{1,0:T(8,128)(2,1)} %param.17, bf16[3072,227]{0,1:T(8,128)(2,1)} %param.15, bf16[227,512]{1,0:T(8,128)(2,1)} %param.16), kind=kOutput, calls=%fused_computation.12 | convolution fusion | flops 2334130176 | bytes 5297152 | tf_op jit(solution)/shard_map/dot_general | solution.py:47
  13.4 11.0 %fusion.38 = f32[24,512,3,128]{3,1,2,0:T(8,128)} fusion(bf16[24,128,512,1]{2,1,3,0:T(8,128)(2,1)} %bitcast.102, bf16[24,3,128,128]{3,2,1,0:T(8,128)(2,1)S(1)} %copy-done), kind=kOutput, calls=%fused_computation.85 | convolution fusion | flops 1207959552 | bytes 24379392 | tf_op jit(solution)/shard_map/bjmn,bmd->bjnd/dot_general | solution.py:51
  24.4 18.8 %copy.25 = f32[72,128,512]{2,0,1:T(8,128)} copy(f32[72,128,512]{1,2,0:T(8,128)} %bitcast.92) | data formatting | bytes 37748736 | tf_op jit(solution)/shard_map/reshape | solution.py:54
  43.4 16.1 %convolution_convert_fusion.1 = bf16[64,128,512]{2,0,1:T(8,128)(2,1)} fusion(f32[72,128,512]{2,0,1:T(8,128)} %copy.25, s32[72]{0:T(128)S(1)} %fusion.29), kind=kOutput, calls=%fused_computation.4 | convolution fusion | flops 3628077568 | bytes 27263264 | tf_op jit(solution)/shard_map/qk,knd->qnd/dot_general | solution.py:64
  59.4 11.3 %copy.26 = bf16[64,128,512]{2,1,0:T(8,128)(2,1)} copy(bf16[64,128,512]{2,0,1:T(8,128)(2,1)} %convolution_convert_fusion.1) | data formatting | bytes 16777216 | tf_op jit(solution)/shard_map/convert_element_type | solution.py:66
  70.9 144.3 %all-reduce.2.cloned.1.call-done = bf16[8192,512]{1,0:T(8,128)(2,1)} async-done(((bf16[8192,512]{1,0:T(8,128)(2,1)}), bf16[8192,512]{1,0:T(8,128)(2,1)}) %all-reduce.2.cloned.1.call-update) | async-done | bytes 8388624 | tf_op jit(solution)/shard_map/psum | solution.py:65
  217.5 1.5 convolution_convert_fusion.4
  219.1 1.9 collective-permute-start
  221.0 3.6 collective-permute-start.1
  224.8 2.0 collective-permute-done
  226.8 1.8 collective-permute-done.1
  228.8 2.2 collective-permute-start.2
  230.9 1.5 collective-permute-start.3
  233.5 9.0 %collective-permute-done.2 = bf16[4,1,128,512]{3,2,1,0:T(8,128)(2,1)S(1)} collective-permute-done((bf16[4,1,128,512]{3,2,1,0:T(8,128)(2,1)S(1)}, bf16[4,1,128,512]{3,2,1,0:T(8,128)(2,1)S(1)}, u32[]{:S(2)}, u32[]{:S(2)}) %collective-permute-start.2) | collective-permute-done | bytes 524320 | tf_op jit(solution)/shard_map/ppermute | solution.py:16
  242.5 4.7 %collective-permute-done.3 = bf16[4,1,128,512]{3,2,1,0:T(8,128)(2,1)S(1)} collective-permute-done((bf16[4,1,128,512]{3,2,1,0:T(8,128)(2,1)S(1)}, bf16[4,1,128,512]{3,2,1,0:T(8,128)(2,1)S(1)}, u32[]{:S(2)}, u32[]{:S(2)}) %collective-permute-start.3) | collective-permute-done | bytes 524320 | tf_op jit(solution)/shard_map/ppermute | solution.py:17
  247.5 2.0 gather_fusion
  249.5 2.4 multiply_reduce_fusion.1
  253.6 2.2 collective-permute-start.4
  255.8 3.4 collective-permute-start.5
  259.2 2.1 collective-permute-done.4
  261.3 1.8 collective-permute-done.5
  263.3 3.2 collective-permute-start.6
  267.8 10.0 %collective-permute-done.6 = bf16[4,1,128,512]{3,2,1,0:T(8,128)(2,1)S(1)} collective-permute-done((bf16[4,1,128,512]{3,2,1,0:T(8,128)(2,1)S(1)}, bf16[4,1,128,512]{3,2,1,0:T(8,128)(2,1)S(1)}, u32[]{:S(2)}, u32[]{:S(2)}) %collective-permute-start.6) | collective-permute-done | bytes 524320 | tf_op jit(solution)/shard_map/ppermute | solution.py:16
  277.8 4.7 %collective-permute-done.7 = bf16[4,1,128,512]{3,2,1,0:T(8,128)(2,1)S(1)} collective-permute-done((bf16[4,1,128,512]{3,2,1,0:T(8,128)(2,1)S(1)}, bf16[4,1,128,512]{3,2,1,0:T(8,128)(2,1)S(1)}, u32[]{:S(2)}, u32[]{:S(2)}) %collective-permute-start.7) | collective-permute-done | bytes 524320 | tf_op jit(solution)/shard_map/ppermute | solution.py:17
  282.8 2.0 gather_fusion.1
  284.8 2.3 multiply_reduce_fusion
  288.9 74.2 %all-gather.2.cloned.1.call-done = bf16[2,32,128,512]{3,2,1,0:T(8,128)(2,1)} async-done(((bf16[2,2,128,512]{3,2,1,0:T(8,128)(2,1)}), bf16[2,32,128,512]{3,2,1,0:T(8,128)(2,1)}) %all-gather.2.cloned.1.call-update) | async-done | bytes 8388624 | tf_op jit(solution)/shard_map/all_gather | solution.py:101
  363.1 10.1 %convolution_convert_fusion = bf16[8192,512]{1,0:T(8,128)(2,1)} fusion(bf16[8192,512]{1,0:T(8,128)(2,1)} %bitcast.114, bf16[512,512]{1,0:T(8,128)(2,1)S(1)} %copy-done.15), kind=kOutput, calls=%fused_computation.3 | convolution fusion | flops 4299161600 | bytes 17301504 | tf_op jit(solution)/shard_map/dot_general | solution.py:103
  373.2 9.5 %gather_fusion.2 = bf16[72,128,512]{2,1,0:T(8,128)(2,1)} fusion(bf16[64,128,512]{2,1,0:T(8,128)(2,1)} %bitcast.95, s32[1024]{0:T(1024)S(1)} %pad_clamp_fusion), kind=kCustom, calls=%fused_computation.2 | custom fusion | bytes 18874656 | tf_op jit(solution)/shard_map/gather | solution.py:108
  382.7 8.2 %fusion.39 = f32[24,512,128,1]{1,2,3,0:T(8,128)} fusion(bf16[24,3,128,512]{3,2,1,0:T(8,128)(2,1)} %bitcast.93, bf16[24,3,128,128]{3,2,1,0:T(8,128)(2,1)S(1)} %copy-done.3), kind=kOutput, calls=%fused_computation.86 | convolution fusion | flops 1207959552 | bytes 18087936 | tf_op jit(solution)/shard_map/bjmn,bjmd->bnd/dot_general | solution.py:109
  390.9 4.6 %fusion.3 = bf16[3072,512]{1,0:T(8,128)(2,1)S(1)} fusion(f32[24,512,128,1]{1,2,3,0:T(8,128)} %fusion.39), kind=kLoop, calls=%fused_computation.11 | loop fusion | flops 7864320 | bytes 9437184 | tf_op jit(solution)/shard_map/convert_element_type | solution.py:110
  395.5 2.1 fusion.4
  (74 shorter events, 9.3 us)
Async XLA Ops:
  6.5 6.9 %copy-start = (bf16[24,3,128,128]{3,2,1,0:T(8,128)(2,1)S(1)}, bf16[24,3,128,128]{3,2,1,0:T(8,128)(2,1)}, u32[]{:S(2)}) copy-start(bf16[24,3,128,128]{3,2,1,0:T(8,128)(2,1)} %param.19) | copy-start | bytes 7077892
  6.5 208.7 %all-reduce.2.cloned.1.call-start = ((), (), s32[]{:S(2)}) async-start(), calls=%async_computation | async-start | bytes 16777216 | tf_op jit(solution)/shard_map/psum | solution.py:65
  24.4 18.8 %copy-start.7 = (s32[24,3]{0,1:T(4,128)S(1)}, s32[24,3]{0,1:T(4,128)}, u32[]{:S(2)}) copy-start(s32[24,3]{0,1:T(4,128)} %param.18) | copy-start | bytes 868
  70.8 144.4 %copy-start.14 = (bf16[512,512]{1,0:T(8,128)(2,1)S(1)}, bf16[512,512]{1,0:T(8,128)(2,1)}, u32[]{:S(2)}) copy-start(bf16[512,512]{1,0:T(8,128)(2,1)} %param.20) | copy-start | bytes 1572868
  70.8 292.3 %all-gather.2.cloned.1.call-start = ((), (), s32[]{:S(2)}) async-start(), calls=%async_computation.1 | async-start | bytes 8912896 | tf_op jit(solution)/shard_map/all_gather | solution.py:101
  70.9 153.8 %copy-start.8 = (s32[2,2,4]{2,1,0:T(2,128)S(1)}, s32[2,2,4]{2,1,0:T(2,128)}, u32[]{:S(2)}) copy-start(s32[2,2,4]{2,1,0:T(2,128)} %param.21) | copy-start | bytes 196
  216.7 0.8 copy-start.16
  217.5 15.0 %copy-start.10 = (s32[2,2]{1,0:T(2,128)S(1)}, s32[2,2]{1,0:T(2,128)}, u32[]{:S(2)}) copy-start(s32[2,2]{1,0:T(2,128)} %param.22) | copy-start | bytes 52
  217.5 15.0 %copy-start.4 = (bf16[2,2,4,128,128]{4,3,2,1,0:T(8,128)(2,1)S(1)}, bf16[2,2,4,128,128]{4,3,2,1,0:T(8,128)(2,1)}, u32[]{:S(2)}) copy-start(bf16[2,2,4,128,128]{4,3,2,1,0:T(8,128)(2,1)} %param.23) | copy-start | bytes 1572868
  219.1 7.7 %collective-permute-start = (bf16[1,2,128,512]{3,2,1,0:T(8,128)(2,1)S(1)}, bf16[1,2,128,512]{3,2,1,0:T(8,128)(2,1)S(1)}, u32[]{:S(2)}, u32[]{:S(2)}) collective-permute-start(bf16[1,2,128,512]{3,2,1,0:T(8,128)(2,1)S(1)} %bitcast.111), channel_id=1, source_target_pairs={{0,16},{16,32},{32,48},{48,64},{64,80},{80,96},{96,112},{1,17},{17... | collective-permute-start | bytes 786440 | tf_op jit(solution)/shard_map/ppermute | solution.py:16
  221.0 7.5 %collective-permute-start.1 = (bf16[1,2,128,512]{3,2,1,0:T(8,128)(2,1)S(1)}, bf16[1,2,128,512]{3,2,1,0:T(8,128)(2,1)S(1)}, u32[]{:S(2)}, u32[]{:S(2)}) collective-permute-start(bf16[1,2,128,512]{3,2,1,0:T(8,128)(2,1)S(1)} %bitcast.110), channel_id=1, source_target_pairs={{16,0},{32,16},{48,32},{64,48},{80,64},{96,80},{112,96},{17,1},{33... | collective-permute-start | bytes 786440 | tf_op jit(solution)/shard_map/ppermute | solution.py:17
  228.8 13.7 %collective-permute-start.2 = (bf16[4,1,128,512]{3,2,1,0:T(8,128)(2,1)S(1)}, bf16[4,1,128,512]{3,2,1,0:T(8,128)(2,1)S(1)}, u32[]{:S(2)}, u32[]{:S(2)}) collective-permute-start(bf16[4,1,128,512]{3,2,1,0:T(8,128)(2,1)S(1)} %get-tuple-element.7), channel_id=1, source_target_pairs={{0,1},{1,2},{2,3},{3,4},{4,5},{5,6},{6,7},{7,8},{8,9},{9,10},{10,1... | collective-permute-start | bytes 1572872 | tf_op jit(solution)/shard_map/ppermute | solution.py:16
  230.9 16.3 %collective-permute-start.3 = (bf16[4,1,128,512]{3,2,1,0:T(8,128)(2,1)S(1)}, bf16[4,1,128,512]{3,2,1,0:T(8,128)(2,1)S(1)}, u32[]{:S(2)}, u32[]{:S(2)}) collective-permute-start(bf16[4,1,128,512]{3,2,1,0:T(8,128)(2,1)S(1)} %get-tuple-element.8), channel_id=1, source_target_pairs={{1,0},{2,1},{3,2},{4,3},{5,4},{6,5},{7,6},{8,7},{9,8},{10,9},{11,1... | collective-permute-start | bytes 1572872 | tf_op jit(solution)/shard_map/ppermute | solution.py:17
  247.5 2.0 copy-start.5
  249.5 2.5 copy-start.12
  249.5 2.5 copy-start.17
  251.9 1.2 copy-start.11
  253.1 9.9 %copy-start.18 = (bf16[512,512]{1,0:T(8,128)(2,1)}, bf16[512,512]{1,0:T(8,128)(2,1)S(1)}, u32[]{:S(2)}) copy-start(bf16[512,512]{1,0:T(8,128)(2,1)S(1)} %fusion.7) | copy-start | bytes 1572868
  253.6 7.7 %collective-permute-start.4 = (bf16[1,2,128,512]{3,2,1,0:T(8,128)(2,1)S(1)}, bf16[1,2,128,512]{3,2,1,0:T(8,128)(2,1)S(1)}, u32[]{:S(2)}, u32[]{:S(2)}) collective-permute-start(bf16[1,2,128,512]{3,2,1,0:T(8,128)(2,1)S(1)} %bitcast.113), channel_id=1, source_target_pairs={{0,16},{16,32},{32,48},{48,64},{64,80},{80,96},{96,112},{1,17},{17... | collective-permute-start | bytes 786440 | tf_op jit(solution)/shard_map/ppermute | solution.py:16
  255.8 7.3 %collective-permute-start.5 = (bf16[1,2,128,512]{3,2,1,0:T(8,128)(2,1)S(1)}, bf16[1,2,128,512]{3,2,1,0:T(8,128)(2,1)S(1)}, u32[]{:S(2)}, u32[]{:S(2)}) collective-permute-start(bf16[1,2,128,512]{3,2,1,0:T(8,128)(2,1)S(1)} %bitcast.112), channel_id=1, source_target_pairs={{16,0},{32,16},{48,32},{64,48},{80,64},{96,80},{112,96},{17,1},{33... | collective-permute-start | bytes 786440 | tf_op jit(solution)/shard_map/ppermute | solution.py:17
  263.3 14.5 %collective-permute-start.6 = (bf16[4,1,128,512]{3,2,1,0:T(8,128)(2,1)S(1)}, bf16[4,1,128,512]{3,2,1,0:T(8,128)(2,1)S(1)}, u32[]{:S(2)}, u32[]{:S(2)}) collective-permute-start(bf16[4,1,128,512]{3,2,1,0:T(8,128)(2,1)S(1)} %get-tuple-element.5), channel_id=1, source_target_pairs={{0,1},{1,2},{2,3},{3,4},{4,5},{5,6},{6,7},{7,8},{8,9},{9,10},{10,1... | collective-permute-start | bytes 1572872 | tf_op jit(solution)/shard_map/ppermute | solution.py:16
  266.5 16.1 %collective-permute-start.7 = (bf16[4,1,128,512]{3,2,1,0:T(8,128)(2,1)S(1)}, bf16[4,1,128,512]{3,2,1,0:T(8,128)(2,1)S(1)}, u32[]{:S(2)}, u32[]{:S(2)}) collective-permute-start(bf16[4,1,128,512]{3,2,1,0:T(8,128)(2,1)S(1)} %get-tuple-element.6), channel_id=1, source_target_pairs={{1,0},{2,1},{3,2},{4,3},{5,4},{6,5},{7,6},{8,7},{9,8},{10,9},{11,1... | collective-permute-start | bytes 1572872 | tf_op jit(solution)/shard_map/ppermute | solution.py:17
  284.8 2.5 copy-start.13
  284.8 2.5 copy-start.19
  287.2 1.5 copy-start.9
  287.2 75.9 %copy-start.15 = (bf16[512,512]{1,0:T(8,128)(2,1)S(1)}, bf16[512,512]{1,0:T(8,128)(2,1)}, u32[]{:S(2)}) copy-start(bf16[512,512]{1,0:T(8,128)(2,1)} %param.26) | copy-start | bytes 1572868
  373.2 9.5 %copy-start.3 = (bf16[24,3,128,128]{3,2,1,0:T(8,128)(2,1)S(1)}, bf16[24,3,128,128]{3,2,1,0:T(8,128)(2,1)}, u32[]{:S(2)}) copy-start(bf16[24,3,128,128]{3,2,1,0:T(8,128)(2,1)} %param.28) | copy-start | bytes 7077892
  390.9 4.6 %copy-start.2 = (bf16[3072,227]{0,1:T(8,128)(2,1)S(1)}, bf16[3072,227]{0,1:T(8,128)(2,1)}, u32[]{:S(2)}) copy-start(bf16[3072,227]{0,1:T(8,128)(2,1)} %param.15) | copy-start | bytes 4184068
  390.9 4.6 %copy-start.6 = (bf16[512,227]{0,1:T(8,128)(2,1)S(1)}, bf16[512,227]{0,1:T(8,128)(2,1)}, u32[]{:S(2)}) copy-start(bf16[512,227]{0,1:T(8,128)(2,1)} %param.29) | copy-start | bytes 697348
  390.9 6.7 %copy-start.1 = (bf16[24,3,128,128]{3,2,1,0:T(8,128)(2,1)S(1)}, bf16[24,3,128,128]{3,2,1,0:T(8,128)(2,1)}, u32[]{:S(2)}) copy-start(bf16[24,3,128,128]{3,2,1,0:T(8,128)(2,1)} %param.19) | copy-start | bytes 7077892
Sparse Core Ops, SparseCore 0:
  70.9 144.2 all-reduce.1
  288.8 74.2 all-gather.1
where the time goes:
time: 406 us; the launch traced here: 404 us
  waiting for transfers between devices  255 us (63%)
  matrix products  64.2 us (16%)
  local copies, waits for them, and re-layouts  45.8 us (11%)
  starting transfers between devices  19.3 us (5%)
  between operations  13.8 us (3%)
  other arithmetic  6.7 us (2%)
    psum x1, waiting for transfers between devices, per_device(): lax.psum(term_part.reshape(patch_total * block_size, feat_width).astype(j...  144 us
    all_gather x1, waiting for transfers between devices, per_device(): shard_piece = lax.all_gather(mesh_patches, 'mesh', axis=1, tiled=True)  74.2 us
    ppermute x4, waiting for transfers between devices, padded_2(): before = lax.ppermute(last, axis, up)  23.1 us
    reshape x1, local copies, waits for them, and re-layouts, per_device(): messages = messages.reshape(-1, block_size, feat_width)  18.8 us
    dot_general x1, matrix products, per_device(): jnp.einsum('qk,knd->qnd', select, messages, precision=lax.Precision.HIGHEST)  16.1 us
    ppermute x4, waiting for transfers between devices, padded_2(): after = lax.ppermute(first, axis, down)  13 us
    convert_element_type x1, local copies, waits for them, and re-layouts, per_device(): term_part.reshape(patch_total * block_size, feat_width).astype(jnp.bfloat16)  11.3 us
    dot_general x1, matrix products, per_device(): jnp.einsum('bjmn,bmd->bjnd', g2m_edges, grid_proj, preferred_element_type...  11 us
  transfers between devices with their start and end apart: 10, of which 10 were waited for; matrix products, arithmetic and copies ran while one was open for 0% of the time, Pallas kernels for 0%

commit v1 on v0

v1 whole, which is shorter than its diff:
```python
import functools

import jax
import jax.numpy as jnp
from jax import lax
from jax.experimental import pallas as pl
from jax.experimental.pallas import tpu as pltpu
from jax.sharding import PartitionSpec as P

epsilon = 1e-05
BF16 = jnp.bfloat16
F32 = jnp.float32
SIDE = 4
NB = 128
D = 512
HALF = 256
OWN = 4
PARAMS = pltpu.CompilerParams(vmem_limit_bytes=56 * 1024 * 1024)


def dot(a, b):
    return jnp.dot(a, b, preferred_element_type=F32)


def dot_t(a, b):
    return lax.dot_general(a, b, (((0,), (0,)), ((), ())), preferred_element_type=F32)


def silu(v):
    return v * jax.nn.sigmoid(v)


def shift(value, axis, step):
    pairs = []
    for y in range(SIDE):
        for z in range(SIDE):
            to = ((y + step) % SIDE, z) if axis == 0 else (y, (z + step) % SIDE)
            pairs.append((y * SIDE + z, to[0] * SIDE + to[1]))
    return lax.ppermute(value, "mesh", pairs)


class Links:
    def __init__(self):
        self.last = {}

    def send(self, value, axis, step):
        link = (axis, step)
        if link in self.last:
            value, _ = lax.optimization_barrier((value, self.last[link]))
        self.last[link] = shift(value, axis, step)
        return self.last[link]


def place(code):
    row = code // 32
    col = code % 32
    owner = col // 2
    return owner // SIDE, owner % SIDE, row * 2 + col % 2


PARTS = ((2, 1), (3, 0))
ORDER = ((2, 0), (3, 0), (2, 1), (1, 0), (3, 1), (1, 1), (0, 0), (0, 1))
BLOCKS = 4
STEPS = 6


def encode_kernel(dest_ref, x_ref, embed_ref, send_ref, edges_ref, *rest):
    outs, (acc, stage, sems) = rest[:16], rest[16:]
    i = pl.program_id(0)

    @pl.when(i == 0)
    def _():
        acc[...] = jnp.zeros_like(acc)

    latent = silu(dot_t(x_ref[...], embed_ref[...])).astype(BF16)
    proj = dot(latent, send_ref[...]).astype(BF16)
    me = lax.axis_index("mesh")
    my_y, my_z = me // SIDE, me % SIDE
    for b in range(BLOCKS):
        block = proj[b * NB : (b + 1) * NB]
        for j in range(3):
            y, z, local = place(dest_ref[j, i * BLOCKS + b])
            slot = (((y - my_y) & 3) * SIDE + ((z - my_z) & 3)) * OWN + local
            acc[slot] += dot_t(edges_ref[b, j], block)

    @pl.when(i == STEPS - 1)
    def _():
        copies = []
        for n, (k, part) in enumerate(ORDER):
            for h in range(2):
                for m, q in enumerate(PARTS[part]):
                    base = (k * SIDE + q if h == 0 else q * SIDE + k) * OWN
                    stage[h, n, m * OWN : (m + 1) * OWN] = acc[
                        base : base + OWN, :, h * HALF : (h + 1) * HALF
                    ].astype(BF16)
                copy = pltpu.make_async_copy(stage.at[h, n], outs[h * 8 + n], sems.at[h * 8 + n])
                copy.start()
                copies.append(copy)
        for copy in copies:
            copy.wait()


def encode(grid_inputs, embed_weight, send_weight, g2m_dest, g2m_edges):
    rows = BLOCKS * NB

    inputs_t = grid_inputs.T
    return pl.pallas_call(
        encode_kernel,
        grid_spec=pltpu.PrefetchScalarGridSpec(
            num_scalar_prefetch=1,
            grid=(STEPS,),
            in_specs=[
                pl.BlockSpec((inputs_t.shape[0], rows), lambda i, *_: (0, i)),
                pl.BlockSpec(embed_weight.shape, lambda i, *_: (0, 0)),
                pl.BlockSpec(send_weight.shape, lambda i, *_: (0, 0)),
                pl.BlockSpec((BLOCKS, 3, NB, NB), lambda i, *_: (i, 0, 0, 0)),
            ],
            out_specs=[pl.BlockSpec(memory_space=pl.ANY)] * 16,
            scratch_shapes=[
                pltpu.VMEM((64, NB, D), F32),
                pltpu.VMEM((2, 8, 8, NB, HALF), BF16),
                pltpu.SemaphoreType.DMA((16,)),
            ],
        ),
        out_shape=[jax.ShapeDtypeStruct((8, NB, HALF), BF16)] * 16,
        compiler_params=PARAMS,
        name="encode",
    )(g2m_dest.T, inputs_t, embed_weight, send_weight, g2m_edges)


def add(*values):
    total = values[0].astype(F32)
    for value in values[1:]:
        total = total + value.astype(F32)
    return total.astype(BF16)


def reduce(pieces):
    both = range(2)
    links = Links()
    piece = [dict(zip(ORDER, pieces[8 * h : 8 * h + 8])) for h in both]

    def far(part, step):
        return [links.send(piece[h][2, part], h, step) for h in both]

    def near(part, step, got):
        k = step % SIDE
        sent = []
        for h in both:
            value = piece[h][k, part]
            sent.append(links.send(value if got is None else add(value, got[h]), h, step))
        return sent

    def settled(part, at, up, down, *more):
        rows = slice(at * OWN, (at + 1) * OWN)
        values = [piece[h][0, part][rows] for h in both]
        return [
            add(values[h], up[h][rows], down[h][rows], *[m[h] for m in more]) for h in both
        ]

    far_0 = far(0, 1)
    down_0 = near(0, -1, None)
    up_0 = near(0, 1, far_0)
    far_1 = far(1, -1)
    sums_2 = settled(0, 0, up_0, down_0)
    from_2 = [links.send(sums_2[h], 1 - h, 1) for h in both]
    down_1 = near(1, -1, far_1)
    up_1 = near(1, 1, None)
    sums_1 = settled(0, 1, up_0, down_0, from_2)
    from_1 = [links.send(sums_1[h], 1 - h, 1) for h in both]
    sums_3 = settled(1, 0, up_1, down_1)
    from_3 = [links.send(sums_3[h], 1 - h, -1) for h in both]
    terms = []
    for h in both:
        terms += [piece[h][0, 1], up_1[h], down_1[h], from_1[h], from_3[h]]
    return terms


def start_kernel(*refs):
    terms, (encode_ref, message_ref, mesh_ref, *sent_refs) = refs[:10], refs[10:]
    total = None
    for h in range(2):
        value = None
        for term in terms[5 * h : 5 * h + 5]:
            term = term[term.shape[0] - OWN :].astype(F32)
            value = term if value is None else value + term
        act = silu(value).astype(BF16).reshape(OWN * NB, HALF)
        part = dot(act, encode_ref[h * HALF : (h + 1) * HALF, :])
        total = part if total is None else total + part
    mesh = total.astype(BF16)
    mesh_ref[...] = mesh
    put_sent(dot(mesh, message_ref[0]).astype(BF16), sent_refs)


def put_sent(sent, refs):
    sent = sent.reshape(2, 2, NB, D)
    all_ref, first_ref, last_ref = refs
    all_ref[...] = sent
    first_ref[...] = sent[:, 0]
    last_ref[...] = sent[:, 1]


def sent_shapes():
    column = jax.ShapeDtypeStruct((2, NB, D), BF16)
    return [
        jax.ShapeDtypeStruct((OWN * NB, D), BF16),
        jax.ShapeDtypeStruct((2, 2, NB, D), BF16),
        column,
        column,
    ]


def mesh_start(terms, encode_weight, message_weight):
    return pl.pallas_call(
        start_kernel,
        out_shape=sent_shapes(),
        compiler_params=PARAMS,
        name="mesh_start",
    )(*terms, encode_weight, message_weight)


def step_kernel(layer, codes_ref, count_ref, mesh_ref, own_ref, left_ref, right_ref, above_ref, below_ref,
                couplings_ref, node_ref, next_ref, *rest):
    outs, (pad, normed) = rest[:-2], rest[-2:]
    pad[0:4] = above_ref[...]
    pad[12:16] = below_ref[...]
    for r in range(2):
        pad[4 * (r + 1)] = left_ref[r]
        pad[4 * (r + 1) + 1 : 4 * (r + 1) + 3] = own_ref[r]
        pad[4 * (r + 1) + 3] = right_ref[r]
    for r in range(2):
        for c in range(2):
            near, weights = [], []
            for a in range(4):
                code = codes_ref[r * 2 + c, a]
                near.append(pad[(r + code // 3) * 4 + c + code % 3])
                live = (a < count_ref[r, c]).astype(BF16)
                weights.append(couplings_ref[r, c, a] * live)
            agg = dot_t(jnp.concatenate(weights, 0), jnp.concatenate(near, 0))
            act = silu(agg)
            scale = lax.rsqrt(jnp.mean(act * act, axis=-1, keepdims=True) + epsilon)
            at = (r * 2 + c) * NB
            normed[at : at + NB, :] = (act * scale).astype(BF16)
    mesh = (mesh_ref[...].astype(F32) + dot(normed[...], node_ref[layer])).astype(BF16)
    if layer == 0:
        outs[0][...] = mesh
        put_sent(dot(mesh, next_ref[1]).astype(BF16), outs[1:])
    else:
        proj = dot(mesh, next_ref[...]).astype(BF16).reshape(OWN, NB, D)
        outs[0][...] = proj[:, :, :HALF]
        outs[1][...] = proj[:, :, HALF:]


def mesh_step(layer, codes, count, mesh, sent, halo, couplings, node_weight, next_weight):
    if layer == 0:
        out_shape = sent_shapes()
    else:
        out_shape = [jax.ShapeDtypeStruct((OWN, NB, HALF), BF16)] * 2
    smem = pl.BlockSpec(memory_space=pltpu.SMEM)
    vmem = pl.BlockSpec(memory_space=pltpu.VMEM)
    return pl.pallas_call(
        functools.partial(step_kernel, layer),
        in_specs=[smem, smem] + [vmem] * 9,
        out_shape=out_shape,
        scratch_shapes=[pltpu.VMEM((16, NB, D), BF16), pltpu.VMEM((OWN * NB, D), BF16)],
        compiler_params=PARAMS,
        name="mesh_step",
    )(codes, count, mesh, sent[0], *halo, couplings, node_weight, next_weight)


def halo_of(grid, first, last):
    size, length = lax.axis_size("mesh"), lax.axis_size("grid")
    ahead = lambda n: [(i, i + 1) for i in range(n - 1)]
    back = lambda n: [(i + 1, i) for i in range(n - 1)]
    left = lax.ppermute(last, "mesh", ahead(size))
    right = lax.ppermute(first, "mesh", back(size))
    top = jnp.concatenate([left[:1], grid[0], right[:1]], 0)
    bottom = jnp.concatenate([left[1:], grid[1], right[1:]], 0)
    above = lax.ppermute(bottom, "grid", ahead(length))
    below = lax.ppermute(top, "grid", back(length))
    return left, right, above, below


def gather(owns):
    both = range(2)
    links = Links()
    near_1 = [links.send(owns[h], 1 - h, 1) for h in both]
    near_3 = [links.send(owns[h], 1 - h, -1) for h in both]
    part_0 = [jnp.concatenate([owns[h], near_1[h]], 0) for h in both]
    near_2 = [links.send(near_1[h], 1 - h, 1) for h in both]
    down_0 = [links.send(part_0[h], h, -1) for h in both]
    up_0 = [links.send(part_0[h], h, 1) for h in both]
    part_1 = [jnp.concatenate([near_2[h], near_3[h]], 0) for h in both]
    down_1 = [links.send(part_1[h], h, -1) for h in both]
    up_1 = [links.send(part_1[h], h, 1) for h in both]
    far_0 = [links.send(up_0[h], h, 1) for h in both]
    far_1 = [links.send(down_1[h], h, -1) for h in both]
    held = []
    for h in both:
        held += [part_0[h], part_1[h], up_0[h], up_1[h], far_0[h], far_1[h], down_0[h], down_1[h]]
    return held


def decode_kernel(src_ref, x_ref, edges_ref, output_ref, *rest):
    pieces, (out_ref, held, sems) = rest[:16], rest[16:]
    i = pl.program_id(0)

    @pl.when(i == 0)
    def _():
        copies = []
        for n in range(16):
            copy = pltpu.make_async_copy(
                pieces[n], held.at[n // 8, pl.ds(n % 8 * 8, 8)], sems.at[n]
            )
            copy.start()
            copies.append(copy)
        for copy in copies:
            copy.wait()

    me = lax.axis_index("mesh")
    my_y, my_z = me // SIDE, me % SIDE
    for b in range(BLOCKS):
        first, second = [], []
        for j in range(3):
            y, z, local = place(src_ref[j, i * BLOCKS + b])
            ky, kz = (my_y - y) & 3, (my_z - z) & 3
            first.append(held[0, (ky * SIDE + kz) * OWN + local])
            second.append(held[1, (kz * SIDE + ky) * OWN + local])
        edges = edges_ref[b].reshape(3 * NB, NB)
        total = None
        for h, parts in enumerate((first, second)):
            hidden = silu(dot_t(edges, jnp.concatenate(parts, 0))).astype(BF16)
            term = lax.dot_general(
                output_ref[:, h * HALF : (h + 1) * HALF],
                hidden,
                (((1,), (1,)), ((), ())),
                preferred_element_type=F32,
            )
            total = term if total is None else total + term
        columns = pl.ds(b * NB, NB)
        out_ref[:, columns] = (x_ref[:, columns].astype(F32) + total).astype(BF16)


def decode(grid_inputs, m2g_src, m2g_edges, output_weight, pieces):
    rows = BLOCKS * NB
    inputs_t, output_t = grid_inputs.T, output_weight.T
    width = inputs_t.shape[0]
    result = pl.pallas_call(
        decode_kernel,
        grid_spec=pltpu.PrefetchScalarGridSpec(
            num_scalar_prefetch=1,
            grid=(STEPS,),
            in_specs=[
                pl.BlockSpec((width, rows), lambda i, *_: (0, i)),
                pl.BlockSpec((BLOCKS, 3, NB, NB), lambda i, *_: (i, 0, 0, 0)),
                pl.BlockSpec(output_t.shape, lambda i, *_: (0, 0)),
            ]
            + [pl.BlockSpec(memory_space=pl.ANY)] * 16,
            out_specs=pl.BlockSpec((width, rows), lambda i, *_: (0, i)),
            scratch_shapes=[
                pltpu.VMEM((2, 64, NB, HALF), BF16),
                pltpu.SemaphoreType.DMA((16,)),
            ],
        ),
        out_shape=jax.ShapeDtypeStruct(inputs_t.shape, BF16),
        compiler_params=PARAMS,
        name="decode",
    )(m2g_src.T, inputs_t, m2g_edges, output_t, *pieces)
    return result.T


def per_device(
    grid_inputs,
    embed_weight,
    send_weight,
    g2m_dest,
    g2m_edges,
    encode_weight,
    adj_codes,
    adj_count,
    couplings,
    message_weight,
    node_weight,
    decode_weight,
    m2g_src,
    m2g_edges,
    output_weight,
):
    pieces = encode(grid_inputs, embed_weight, send_weight, g2m_dest, g2m_edges)
    mesh, *sent = mesh_start(reduce(pieces), encode_weight, message_weight)
    codes = adj_codes.reshape(OWN, -1)
    mesh, *sent = mesh_step(
        0, codes, adj_count, mesh, sent, halo_of(*sent), couplings, node_weight, message_weight
    )
    owns = mesh_step(
        1, codes, adj_count, mesh, sent, halo_of(*sent), couplings, node_weight, decode_weight
    )
    return decode(grid_inputs, m2g_src, m2g_edges, output_weight, gather(owns))


def solution(mesh):
    placed = (
        P(("grid", "mesh"), None),
        P(),
        P(),
        P(("grid", "mesh"), None),
        P(("grid", "mesh"), None, None, None),
        P(),
        P("grid", "mesh", None),
        P("grid", "mesh"),
        P("grid", "mesh", None, None, None),
        P(),
        P(),
        P(),
        P(("grid", "mesh"), None),
        P(("grid", "mesh"), None, None, None),
        P(),
    )
    return jax.shard_map(
        per_device, mesh=mesh, in_specs=placed, out_specs=P(("grid", "mesh"), None), check_vma=False
    )
```

time: 406 us -> 226 us (0.56)
  waiting for transfers between devices: 255 us -> 96.2 us
  matrix products: 64.2 us -> 0 us
  starting transfers between devices: 19.3 us -> 75.5 us
  Pallas kernels: 0 us -> 41.2 us
  local copies, waits for them, and re-layouts: 45.8 us -> 7.49 us
  between operations: 13.8 us -> 0.72 us
    psum x1 -> x0, waiting for transfers between devices: 144 us -> none  [per_device(): lax.psum(term_part.reshape(patch_total * block_size, feat_width).astype(j...]
    all_gather x1 -> x0, waiting for transfers between devices: 74.2 us -> none  [per_device(): shard_piece = lax.all_gather(mesh_patches, 'mesh', axis=1, tiled=True)]
    dot_general x13 -> x0, matrix products: 64.2 us -> none  [the longest x1 16.1 us: per_device(): jnp.einsum('qk,knd->qnd', select, messages, precision=lax.Precision.HIGHEST)]
    ppermute x8 -> x44, waiting for transfers between devices: 36.1 us -> 96.2 us  [the longest x36 68.6 us: shift(): return lax.ppermute(value, 'mesh', pairs)]
    ppermute x8 -> x44, starting transfers between devices: 19.3 us -> 75.5 us  [the longest x36 57.3 us: shift(): return lax.ppermute(value, 'mesh', pairs)]
    pallas_call x0 -> x5, Pallas kernels: none -> 41.2 us  [the longest x1 14.4 us: decode(): pl.pallas_call(decode_kernel, grid_spec=pltpu.PrefetchScalarGridSpec(num_...]
    reshape x3 -> x0, local copies, waits for them, and re-layouts: 19 us -> none  [the longest x1 18.8 us: per_device(): messages = messages.reshape(-1, block_size, feat_width)]
    gather x3 -> x0, local copies, waits for them, and re-layouts: 13.5 us -> none  [the longest x1 9.49 us: per_device(): taken = band_proj[m2g_src]]
  transfers between devices with their start and end apart: 10 -> 44, of which waited for: 10 -> 32; matrix products, arithmetic and copies ran while one was open for 0% -> 3% of each run, Pallas kernels for 0% -> 0%
where the time goes in v1:
time: 226 us; the launch traced here: 225 us
  waiting for transfers between devices  96.2 us (43%)
  starting transfers between devices  75.5 us (33%)
  Pallas kernels  41.2 us (18%)
  local copies, waits for them, and re-layouts  7.49 us (3%)
  other arithmetic  3.68 us (2%)
    ppermute x36, waiting for transfers between devices, shift(): return lax.ppermute(value, 'mesh', pairs)  68.6 us
    ppermute x36, starting transfers between devices, shift(): return lax.ppermute(value, 'mesh', pairs)  57.3 us
    pallas_call x1, Pallas kernels, decode(): pl.pallas_call(decode_kernel, grid_spec=pltpu.PrefetchScalarGridSpec(num_...  14.4 us
    pallas_call x1, Pallas kernels, encode(): pl.pallas_call(encode_kernel, grid_spec=pltpu.PrefetchScalarGridSpec(num_...  13.1 us
    ppermute x2, waiting for transfers between devices, halo_of(): above = lax.ppermute(bottom, 'grid', ahead(length))  9.7 us
    pallas_call x2, Pallas kernels, mesh_step(): pl.pallas_call(functools.partial(step_kernel, layer), in_specs=[smem, sme...  9.13 us
    ppermute x2, waiting for transfers between devices, halo_of(): right = lax.ppermute(first, 'mesh', back(size))  8.58 us
    ppermute x2, starting transfers between devices, halo_of(): below = lax.ppermute(top, 'grid', back(length))  6.75 us
  transfers between devices with their start and end apart: 44, of which 32 were waited for; matrix products, arithmetic and copies ran while one was open for 3% of the time, Pallas kernels for 0%

profile of v1, /device:TPU:2, one launch (start us, length us, event | category | flops | bytes accessed | tf_op | source)
XLA Modules:
  0.0 224.8 jit_solution(18359454694285671091)
XLA Ops:
  0.0 13.1 %encode.1 = (bf16[8,128,256]{2,1,0:T(8,128)(2,1)}, bf16[8,128,256]{2,1,0:T(8,128)(2,1)}, bf16[8,128,256]{2,1,0:T(8,128)(2,1)}, bf16[8,128,256]{2,1,0:T(8,128)(2,...) custom-call(s32[3,24]{1,0:T(4,128)} %bitcast.19, ...), custom_call_target="tpu_custom_call" | custom-call | tf_op jit(solution)/shard_map/encode/pallas_call | solution.py:107
  20.6 8.8 %collective-permute-done = bf16[8,128,256]{2,1,0:T(8,128)(2,1)S(1)} collective-permute-done((bf16[8,128,256]{2,1,0:T(8,128)(2,1)}, bf16[8,128,256]{2,1,0:T(8,128)(2,1)S(1)}, u32[]{:S(2)}, u32[]{:S(2)}) %collective-permute-start) | collective-permute-done | bytes 524320 | tf_op jit(solution)/shard_map/ppermute | solution.py:39
  33.7 3.2 %collective-permute-start.13 = (bf16[8,128,256]{2,1,0:T(8,128)(2,1)S(1)}, bf16[8,128,256]{2,1,0:T(8,128)(2,1)S(1)}, u32[]{:S(2)}, u32[]{:S(2)}) collective-permute-start(bf16[8,128,256]{2,1,0:T(8,128)(2,1)S(1)} %copy-done.41), channel_id=1, source_target_pairs={{0,3},{1,0},{2,1},{3,2},{4,7},{5,4},{6,5},{7,6},{8,11},{9,8},{10,9... | collective-permute-start | bytes 1572872 | tf_op jit(solution)/shard_map/ppermute | solution.py:39
  38.6 6.5 %collective-permute-done.1 = bf16[8,128,256]{2,1,0:T(8,128)(2,1)S(1)} collective-permute-done((bf16[8,128,256]{2,1,0:T(8,128)(2,1)S(1)}, bf16[8,128,256]{2,1,0:T(8,128)(2,1)S(1)}, u32[]{:S(2)}, u32[]{:S(2)}) %collective-permute-start.1) | collective-permute-done | bytes 524320 | tf_op jit(solution)/shard_map/ppermute | solution.py:39
  48.0 2.9 %collective-permute-start.14 = (bf16[8,128,256]{2,1,0:T(8,128)(2,1)S(1)}, bf16[8,128,256]{2,1,0:T(8,128)(2,1)S(1)}, u32[]{:S(2)}, u32[]{:S(2)}) collective-permute-start(bf16[8,128,256]{2,1,0:T(8,128)(2,1)S(1)} %add_convert_fusion), channel_id=1, source_target_pairs={{0,3},{1,0},{2,1},{3,2},{4,7},{5,4},{6,5},{7,6},{8,11},{9,8},{10,9... | collective-permute-start | bytes 1572872 | tf_op jit(solution)/shard_map/ppermute | solution.py:39
  50.9 3.5 %collective-permute-done.5 = bf16[4,128,256]{2,1,0:T(8,128)(2,1)S(1)} collective-permute-done((bf16[4,128,256]{2,1,0:T(8,128)(2,1)S(1)}, bf16[4,128,256]{2,1,0:T(8,128)(2,1)S(1)}, u32[]{:S(2)}, u32[]{:S(2)}) %collective-permute-start.5) | collective-permute-done | bytes 262176 | tf_op jit(solution)/shard_map/ppermute | solution.py:39
  55.2 3.2 %collective-permute-start.9 = (bf16[8,128,256]{2,1,0:T(8,128)(2,1)S(1)}, bf16[8,128,256]{2,1,0:T(8,128)(2,1)S(1)}, u32[]{:S(2)}, u32[]{:S(2)}) collective-permute-start(bf16[8,128,256]{2,1,0:T(8,128)(2,1)S(1)} %add_convert_fusion.1), channel_id=1, source_target_pairs={{0,12},{1,13},{2,14},{3,15},{4,0},{5,1},{6,2},{7,3},{8,4},{9,5},{1... | collective-permute-start | bytes 1572872 | tf_op jit(solution)/shard_map/ppermute | solution.py:39
  58.7 8.2 %collective-permute-done.6.refs_1_ = bf16[8,128,256]{2,1,0:T(8,128)(2,1)S(1)} collective-permute-done((bf16[8,128,256]{2,1,0:T(8,128)(2,1)S(1)}, bf16[8,128,256]{2,1,0:T(8,128)(2,1)S(1)}, u32[]{:S(2)}, u32[]{:S(2)}) %collective-permute-start.6) | collective-permute-done | bytes 524320 | tf_op jit(solution)/shard_map/ppermute | solution.py:39
  67.4 3.1 %collective-permute-start.15 = (bf16[4,128,256]{2,1,0:T(8,128)(2,1)S(1)}, bf16[4,128,256]{2,1,0:T(8,128)(2,1)S(1)}, u32[]{:S(2)}, u32[]{:S(2)}) collective-permute-start(bf16[4,128,256]{2,1,0:T(8,128)(2,1)S(1)} %add_convert_fusion.6), channel_id=1, source_target_pairs={{0,3},{1,0},{2,1},{3,2},{4,7},{5,4},{6,5},{7,6},{8,11},{9,8},{10,9... | collective-permute-start | bytes 786440 | tf_op jit(solution)/shard_map/ppermute | solution.py:39
  70.6 3.2 %collective-permute-start.17 = (bf16[4,128,256]{2,1,0:T(8,128)(2,1)S(1)}, bf16[4,128,256]{2,1,0:T(8,128)(2,1)S(1)}, u32[]{:S(2)}, u32[]{:S(2)}) collective-permute-start(bf16[4,128,256]{2,1,0:T(8,128)(2,1)S(1)} %add_convert_fusion.4), channel_id=1, source_target_pairs={{0,12},{1,13},{2,14},{3,15},{4,0},{5,1},{6,2},{7,3},{8,4},{9,5},{1... | collective-permute-start | bytes 786440 | tf_op jit(solution)/shard_map/ppermute | solution.py:39
  74.6 3.0 %collective-permute-done.17.refs_9_ = bf16[4,128,256]{2,1,0:T(8,128)(2,1)S(1)} collective-permute-done((bf16[4,128,256]{2,1,0:T(8,128)(2,1)S(1)}, bf16[4,128,256]{2,1,0:T(8,128)(2,1)S(1)}, u32[]{:S(2)}, u32[]{:S(2)}) %collective-permute-start.17) | collective-permute-done | bytes 262176 | tf_op jit(solution)/shard_map/ppermute | solution.py:39
  78.4 4.6 %mesh_start.1 = (bf16[512,512]{1,0:T(8,128)(2,1)}, bf16[2,2,128,512]{3,2,1,0:T(8,128)(2,1)}, bf16[2,128,512]{2,1,0:T(8,128)(2,1)}, bf16[2,128,512]{2,1,0:T(8,128)(2,1)}) custom-call(bf16[8,128,256]{2,1,0:T(8,128)(2,1)} %get-tuple-element.59.refs_0_, bf16[8,128,256]{2,1,0:T(8,128)(2,1)} %copy-done.7, bf16[8,128,256]{2,1,0:T(8,128)(2,1)} %copy-done.9, ...), custom_call_target="tpu_custom_call" | custom-call | tf_op jit(solution)/shard_map/mesh_start/pallas_call | solution.py:214
  88.4 4.3 %collective-permute-done.19.right_ref = bf16[2,128,512]{2,1,0:T(8,128)(2,1)S(1)} collective-permute-done((bf16[2,128,512]{2,1,0:T(8,128)(2,1)}, bf16[2,128,512]{2,1,0:T(8,128)(2,1)S(1)}, u32[]{:S(2)}, u32[]{:S(2)}) %collective-permute-start.19) | collective-permute-done | bytes 262176 | tf_op jit(solution)/shard_map/ppermute | solution.py:276
  94.8 3.6 %collective-permute-start.21 = (bf16[4,128,512]{2,1,0:T(8,128)(2,1)S(1)}, bf16[4,128,512]{2,1,0:T(8,128)(2,1)S(1)}, u32[]{:S(2)}, u32[]{:S(2)}) collective-permute-start(bf16[4,128,512]{2,1,0:T(8,128)(2,1)S(1)} %pad_maximum_fusion.1), channel_id=1, source_target_pairs={{16,0},{32,16},{48,32},{64,48},{80,64},{96,80},{112,96},{17,1},{33... | collective-permute-start | bytes 1572872 | tf_op jit(solution)/shard_map/ppermute | solution.py:280
  98.4 4.8 %collective-permute-done.20.above_ref = bf16[4,128,512]{2,1,0:T(8,128)(2,1)S(1)} collective-permute-done((bf16[4,128,512]{2,1,0:T(8,128)(2,1)S(1)}, bf16[4,128,512]{2,1,0:T(8,128)(2,1)S(1)}, u32[]{:S(2)}, u32[]{:S(2)}) %collective-permute-start.20) | collective-permute-done | bytes 524320 | tf_op jit(solution)/shard_map/ppermute | solution.py:279
  105.9 4.7 %mesh_step.2 = (bf16[512,512]{1,0:T(8,128)(2,1)}, bf16[2,2,128,512]{3,2,1,0:T(8,128)(2,1)}, bf16[2,128,512]{2,1,0:T(8,128)(2,1)}, bf16[2,128,512]{2,1,0:T(8,128)(2,1)}) custom-call(s32[4,4]{1,0:T(4,128)} %bitcast.17, s32[2,2]{1,0:T(2,128)} %count_ref.3, bf16[512,512]{1,0:T(8,128)(2,1)} %get-tuple-element.89.mesh_ref, ...), custom_call_target="tpu_custom_call" | custom-call | tf_op jit(solution)/shard_map/mesh_step/pallas_call | solution.py:261
  110.7 3.1 %collective-permute-start.22 = (bf16[2,128,512]{2,1,0:T(8,128)(2,1)}, bf16[2,128,512]{2,1,0:T(8,128)(2,1)S(1)}, u32[]{:S(2)}, u32[]{:S(2)}) collective-permute-start(bf16[2,128,512]{2,1,0:T(8,128)(2,1)} %get-tuple-element.95), channel_id=1, source_target_pairs={{0,1},{1,2},{2,3},{3,4},{4,5},{5,6},{6,7},{7,8},{8,9},{9,10},{10,1... | collective-permute-start | bytes 786440 | tf_op jit(solution)/shard_map/ppermute | solution.py:275
  116.2 3.9 %collective-permute-done.22.left_ref = bf16[2,128,512]{2,1,0:T(8,128)(2,1)S(1)} collective-permute-done((bf16[2,128,512]{2,1,0:T(8,128)(2,1)}, bf16[2,128,512]{2,1,0:T(8,128)(2,1)S(1)}, u32[]{:S(2)}, u32[]{:S(2)}) %collective-permute-start.22) | collective-permute-done | bytes 262176 | tf_op jit(solution)/shard_map/ppermute | solution.py:275
  120.1 4.3 %collective-permute-done.23.right_ref = bf16[2,128,512]{2,1,0:T(8,128)(2,1)S(1)} collective-permute-done((bf16[2,128,512]{2,1,0:T(8,128)(2,1)}, bf16[2,128,512]{2,1,0:T(8,128)(2,1)S(1)}, u32[]{:S(2)}, u32[]{:S(2)}) %collective-permute-start.23) | collective-permute-done | bytes 262176 | tf_op jit(solution)/shard_map/ppermute | solution.py:276
  127.0 3.1 %collective-permute-start.25 = (bf16[4,128,512]{2,1,0:T(8,128)(2,1)S(1)}, bf16[4,128,512]{2,1,0:T(8,128)(2,1)S(1)}, u32[]{:S(2)}, u32[]{:S(2)}) collective-permute-start(bf16[4,128,512]{2,1,0:T(8,128)(2,1)S(1)} %pad_maximum_fusion.3), channel_id=1, source_target_pairs={{16,0},{32,16},{48,32},{64,48},{80,64},{96,80},{112,96},{17,1},{33... | collective-permute-start | bytes 1572872 | tf_op jit(solution)/shard_map/ppermute | solution.py:280
  130.1 4.8 %collective-permute-done.24.above_ref = bf16[4,128,512]{2,1,0:T(8,128)(2,1)S(1)} collective-permute-done((bf16[4,128,512]{2,1,0:T(8,128)(2,1)S(1)}, bf16[4,128,512]{2,1,0:T(8,128)(2,1)S(1)}, u32[]{:S(2)}, u32[]{:S(2)}) %collective-permute-start.24) | collective-permute-done | bytes 524320 | tf_op jit(solution)/shard_map/ppermute | solution.py:279
  137.6 4.4 %mesh_step.3 = (bf16[4,128,256]{2,1,0:T(8,128)(2,1)}, bf16[4,128,256]{2,1,0:T(8,128)(2,1)}) custom-call(s32[4,4]{1,0:T(4,128)} %bitcast.18, s32[2,2]{1,0:T(2,128)} %count_ref.3, bf16[512,512]{1,0:T(8,128)(2,1)} %get-tuple-element.93.mesh_ref, bf16[2,2,128,512]{3,2,1,0:T(8,128)(2,1)} %get-tuple-element.94.own_ref, bf16[2,128,512]{2,1,0:T(8,128)(2,1)} %copy-done.10, ...), custom_call_target="tpu_custom_call" | custom-call | tf_op jit(solution)/shard_map/mesh_step/pallas_call | solution.py:261
  142.0 4.1 %collective-permute-start.26 = (bf16[4,128,256]{2,1,0:T(8,128)(2,1)}, bf16[4,128,256]{2,1,0:T(8,128)(2,1)S(1)}, u32[]{:S(2)}, u32[]{:S(2)}) collective-permute-start(bf16[4,128,256]{2,1,0:T(8,128)(2,1)} %get-tuple-element.97), channel_id=1, source_target_pairs={{0,1},{1,2},{2,3},{3,0},{4,5},{5,6},{6,7},{7,4},{8,9},{9,10},{10,1... | collective-permute-start | bytes 786440 | tf_op jit(solution)/shard_map/ppermute | solution.py:39
  147.5 2.8 %collective-permute-start.28 = (bf16[4,128,256]{2,1,0:T(8,128)(2,1)}, bf16[4,128,256]{2,1,0:T(8,128)(2,1)S(1)}, u32[]{:S(2)}, u32[]{:S(2)}) collective-permute-start(bf16[4,128,256]{2,1,0:T(8,128)(2,1)} %get-tuple-element.97), channel_id=1, source_target_pairs={{0,3},{1,0},{2,1},{3,2},{4,7},{5,4},{6,5},{7,6},{8,11},{9,8},{10,9... | collective-permute-start | bytes 786440 | tf_op jit(solution)/shard_map/ppermute | solution.py:39
  166.6 6.5 %collective-permute-done.41.rest_14_ = bf16[8,128,256]{2,1,0:T(8,128)(2,1)S(1)} collective-permute-done((bf16[8,128,256]{2,1,0:T(8,128)(2,1)S(1)}, bf16[8,128,256]{2,1,0:T(8,128)(2,1)S(1)}, u32[]{:S(2)}, u32[]{:S(2)}) %collective-permute-start.41) | collective-permute-done | bytes 524320 | tf_op jit(solution)/shard_map/ppermute | solution.py:39
  173.1 3.4 %collective-permute-start.42 = (bf16[8,128,256]{2,1,0:T(8,128)(2,1)S(1)}, bf16[8,128,256]{2,1,0:T(8,128)(2,1)S(1)}, u32[]{:S(2)}, u32[]{:S(2)}) collective-permute-start(bf16[8,128,256]{2,1,0:T(8,128)(2,1)S(1)} %constant_dynamic-update-slice_fusion.6.rest_9_), channel_id=1, source_target_pairs={{0,3},{1,0},{2,1},{3,2},{4,7},{5,4},{6,5},{7,6},{8,11},{9,8},{10,9... | collective-permute-start | bytes 1572872 | tf_op jit(solution)/shard_map/ppermute | solution.py:39
  181.7 6.1 %collective-permute-done.42.rest_15_ = bf16[8,128,256]{2,1,0:T(8,128)(2,1)S(1)} collective-permute-done((bf16[8,128,256]{2,1,0:T(8,128)(2,1)S(1)}, bf16[8,128,256]{2,1,0:T(8,128)(2,1)S(1)}, u32[]{:S(2)}, u32[]{:S(2)}) %collective-permute-start.42) | collective-permute-done | bytes 524320 | tf_op jit(solution)/shard_map/ppermute | solution.py:39
  187.7 3.7 %collective-permute-start.43 = (bf16[8,128,256]{2,1,0:T(8,128)(2,1)S(1)}, bf16[8,128,256]{2,1,0:T(8,128)(2,1)S(1)}, u32[]{:S(2)}, u32[]{:S(2)}) collective-permute-start(bf16[8,128,256]{2,1,0:T(8,128)(2,1)S(1)} %collective-permute-done.42.rest_15_), channel_id=1, source_target_pairs={{0,3},{1,0},{2,1},{3,2},{4,7},{5,4},{6,5},{7,6},{8,11},{9,8},{10,9... | collective-permute-start | bytes 1572872 | tf_op jit(solution)/shard_map/ppermute | solution.py:39
  196.0 5.9 %collective-permute-done.43.rest_13_ = bf16[8,128,256]{2,1,0:T(8,128)(2,1)S(1)} collective-permute-done((bf16[8,128,256]{2,1,0:T(8,128)(2,1)S(1)}, bf16[8,128,256]{2,1,0:T(8,128)(2,1)S(1)}, u32[]{:S(2)}, u32[]{:S(2)}) %collective-permute-start.43) | collective-permute-done | bytes 524320 | tf_op jit(solution)/shard_map/ppermute | solution.py:39
  201.9 3.1 %collective-permute-done.37.rest_5_ = bf16[8,128,256]{2,1,0:T(8,128)(2,1)S(1)} collective-permute-done((bf16[8,128,256]{2,1,0:T(8,128)(2,1)S(1)}, bf16[8,128,256]{2,1,0:T(8,128)(2,1)S(1)}, u32[]{:S(2)}, u32[]{:S(2)}) %collective-permute-start.37) | collective-permute-done | bytes 524320 | tf_op jit(solution)/shard_map/ppermute | solution.py:39
  204.9 3.7 %collective-permute-done.40.rest_12_ = bf16[8,128,256]{2,1,0:T(8,128)(2,1)S(1)} collective-permute-done((bf16[8,128,256]{2,1,0:T(8,128)(2,1)S(1)}, bf16[8,128,256]{2,1,0:T(8,128)(2,1)S(1)}, u32[]{:S(2)}, u32[]{:S(2)}) %collective-permute-start.40) | collective-permute-done | bytes 524320 | tf_op jit(solution)/shard_map/ppermute | solution.py:39
  210.2 14.4 %decode.1 = bf16[227,3072]{1,0:T(8,128)(2,1)} custom-call(s32[3,24]{1,0:T(4,128)} %bitcast.20, bf16[227,3072]{1,0:T(8,128)(2,1)} %bitcast.15, bf16[24,3,128,128]{3,2,1,0:T(8,128)(2,1)} %edges_ref.3, bf16[227,512]{1,0:T(8,128)(2,1)} %bitcast.16, bf16[8,128,256]{2,1,0:T(8,128)(2,1)} %copy-done, bf16[8,128,256]{2,1,0:T(8,128)(2,1)} %copy-done.1, ...), custom_call_target="tpu_custom_call" | custom-call | tf_op jit(solution)/shard_map/decode/pallas_call | solution.py:348
  (173 shorter events, 66.2 us)
Async XLA Ops:
  13.2 16.2 %collective-permute-start = (bf16[8,128,256]{2,1,0:T(8,128)(2,1)}, bf16[8,128,256]{2,1,0:T(8,128)(2,1)S(1)}, u32[]{:S(2)}, u32[]{:S(2)}) collective-permute-start(bf16[8,128,256]{2,1,0:T(8,128)(2,1)} %get-tuple-element.63), channel_id=1, source_target_pairs={{0,1},{1,2},{2,3},{3,0},{4,5},{5,6},{6,7},{7,4},{8,9},{9,10},{10,1... | collective-permute-start | bytes 1572872 | tf_op jit(solution)/shard_map/ppermute | solution.py:39
  15.2 15.6 %collective-permute-start.3 = (bf16[8,128,256]{2,1,0:T(8,128)(2,1)}, bf16[8,128,256]{2,1,0:T(8,128)(2,1)S(1)}, u32[]{:S(2)}, u32[]{:S(2)}) collective-permute-start(bf16[8,128,256]{2,1,0:T(8,128)(2,1)} %get-tuple-element.67), channel_id=1, source_target_pairs={{0,4},{1,5},{2,6},{3,7},{4,8},{5,9},{6,10},{7,11},{8,12},{9,13},{1... | collective-permute-start | bytes 1572872 | tf_op jit(solution)/shard_map/ppermute | solution.py:39
  16.7 17.0 %collective-permute-start.2 = (bf16[8,128,256]{2,1,0:T(8,128)(2,1)}, bf16[8,128,256]{2,1,0:T(8,128)(2,1)S(1)}, u32[]{:S(2)}, u32[]{:S(2)}) collective-permute-start(bf16[8,128,256]{2,1,0:T(8,128)(2,1)} %get-tuple-element.65), channel_id=1, source_target_pairs={{0,3},{1,0},{2,1},{3,2},{4,7},{5,4},{6,5},{7,6},{8,11},{9,8},{10,9... | collective-permute-start | bytes 1572872 | tf_op jit(solution)/shard_map/ppermute | solution.py:39
  18.9 18.0 %collective-permute-start.7 = (bf16[8,128,256]{2,1,0:T(8,128)(2,1)}, bf16[8,128,256]{2,1,0:T(8,128)(2,1)S(1)}, u32[]{:S(2)}, u32[]{:S(2)}) collective-permute-start(bf16[8,128,256]{2,1,0:T(8,128)(2,1)} %get-tuple-element.73), channel_id=1, source_target_pairs={{0,12},{1,13},{2,14},{3,15},{4,0},{5,1},{6,2},{7,3},{8,4},{9,5},{1... | collective-permute-start | bytes 1572872 | tf_op jit(solution)/shard_map/ppermute | solution.py:39
  30.6 14.4 %collective-permute-start.1 = (bf16[8,128,256]{2,1,0:T(8,128)(2,1)S(1)}, bf16[8,128,256]{2,1,0:T(8,128)(2,1)S(1)}, u32[]{:S(2)}, u32[]{:S(2)}) collective-permute-start(bf16[8,128,256]{2,1,0:T(8,128)(2,1)S(1)} %add_convert_fusion.3), channel_id=1, source_target_pairs={{0,1},{1,2},{2,3},{3,0},{4,5},{5,6},{6,7},{7,4},{8,9},{9,10},{10,1... | collective-permute-start | bytes 1572872 | tf_op jit(solution)/shard_map/ppermute | solution.py:39
  32.0 14.5 %collective-permute-start.4 = (bf16[8,128,256]{2,1,0:T(8,128)(2,1)S(1)}, bf16[8,128,256]{2,1,0:T(8,128)(2,1)S(1)}, u32[]{:S(2)}, u32[]{:S(2)}) collective-permute-start(bf16[8,128,256]{2,1,0:T(8,128)(2,1)S(1)} %add_convert_fusion.2), channel_id=1, source_target_pairs={{0,4},{1,5},{2,6},{3,7},{4,8},{5,9},{6,10},{7,11},{8,12},{9,13},{1... | collective-permute-start | bytes 1572872 | tf_op jit(solution)/shard_map/ppermute | solution.py:39
  33.7 14.2 %collective-permute-start.13 = (bf16[8,128,256]{2,1,0:T(8,128)(2,1)S(1)}, bf16[8,128,256]{2,1,0:T(8,128)(2,1)S(1)}, u32[]{:S(2)}, u32[]{:S(2)}) collective-permute-start(bf16[8,128,256]{2,1,0:T(8,128)(2,1)S(1)} %copy-done.41), channel_id=1, source_target_pairs={{0,3},{1,0},{2,1},{3,2},{4,7},{5,4},{6,5},{7,6},{8,11},{9,8},{10,9... | collective-permute-start | bytes 1572872 | tf_op jit(solution)/shard_map/ppermute | solution.py:39
  36.9 18.2 %collective-permute-start.8 = (bf16[8,128,256]{2,1,0:T(8,128)(2,1)S(1)}, bf16[8,128,256]{2,1,0:T(8,128)(2,1)S(1)}, u32[]{:S(2)}, u32[]{:S(2)}) collective-permute-start(bf16[8,128,256]{2,1,0:T(8,128)(2,1)S(1)} %copy-done.40), channel_id=1, source_target_pairs={{0,12},{1,13},{2,14},{3,15},{4,0},{5,1},{6,2},{7,3},{8,4},{9,5},{1... | collective-permute-start | bytes 1572872 | tf_op jit(solution)/shard_map/ppermute | solution.py:39
  48.0 19.2 %collective-permute-start.14 = (bf16[8,128,256]{2,1,0:T(8,128)(2,1)S(1)}, bf16[8,128,256]{2,1,0:T(8,128)(2,1)S(1)}, u32[]{:S(2)}, u32[]{:S(2)}) collective-permute-start(bf16[8,128,256]{2,1,0:T(8,128)(2,1)S(1)} %add_convert_fusion), channel_id=1, source_target_pairs={{0,3},{1,0},{2,1},{3,2},{4,7},{5,4},{6,5},{7,6},{8,11},{9,8},{10,9... | collective-permute-start | bytes 1572872 | tf_op jit(solution)/shard_map/ppermute | solution.py:39
  54.4 12.5 %collective-permute-start.6 = (bf16[8,128,256]{2,1,0:T(8,128)(2,1)S(1)}, bf16[8,128,256]{2,1,0:T(8,128)(2,1)S(1)}, u32[]{:S(2)}, u32[]{:S(2)}) collective-permute-start(bf16[8,128,256]{2,1,0:T(8,128)(2,1)S(1)} %copy-done.39), channel_id=1, source_target_pairs={{0,4},{1,5},{2,6},{3,7},{4,8},{5,9},{6,10},{7,11},{8,12},{9,13},{1... | collective-permute-start | bytes 1572872 | tf_op jit(solution)/shard_map/ppermute | solution.py:39
  54.6 12.4 %collective-permute-start.11 = (bf16[8,128,256]{2,1,0:T(8,128)(2,1)S(1)}, bf16[8,128,256]{2,1,0:T(8,128)(2,1)S(1)}, u32[]{:S(2)}, u32[]{:S(2)}) collective-permute-start(bf16[8,128,256]{2,1,0:T(8,128)(2,1)S(1)} %copy-done.38), channel_id=1, source_target_pairs={{0,1},{1,2},{2,3},{3,0},{4,5},{5,6},{6,7},{7,4},{8,9},{9,10},{10,1... | collective-permute-start | bytes 1572872 | tf_op jit(solution)/shard_map/ppermute | solution.py:39
  55.2 12.1 %collective-permute-start.9 = (bf16[8,128,256]{2,1,0:T(8,128)(2,1)S(1)}, bf16[8,128,256]{2,1,0:T(8,128)(2,1)S(1)}, u32[]{:S(2)}, u32[]{:S(2)}) collective-permute-start(bf16[8,128,256]{2,1,0:T(8,128)(2,1)S(1)} %add_convert_fusion.1), channel_id=1, source_target_pairs={{0,12},{1,13},{2,14},{3,15},{4,0},{5,1},{6,2},{7,3},{8,4},{9,5},{1... | collective-permute-start | bytes 1572872 | tf_op jit(solution)/shard_map/ppermute | solution.py:39
  92.8 10.5 %collective-permute-start.20 = (bf16[4,128,512]{2,1,0:T(8,128)(2,1)S(1)}, bf16[4,128,512]{2,1,0:T(8,128)(2,1)S(1)}, u32[]{:S(2)}, u32[]{:S(2)}) collective-permute-start(bf16[4,128,512]{2,1,0:T(8,128)(2,1)S(1)} %pad_maximum_fusion), channel_id=1, source_target_pairs={{0,16},{16,32},{32,48},{48,64},{64,80},{80,96},{96,112},{1,17},{17... | collective-permute-start | bytes 1572872 | tf_op jit(solution)/shard_map/ppermute | solution.py:279
  94.8 10.3 %collective-permute-start.21 = (bf16[4,128,512]{2,1,0:T(8,128)(2,1)S(1)}, bf16[4,128,512]{2,1,0:T(8,128)(2,1)S(1)}, u32[]{:S(2)}, u32[]{:S(2)}) collective-permute-start(bf16[4,128,512]{2,1,0:T(8,128)(2,1)S(1)} %pad_maximum_fusion.1), channel_id=1, source_target_pairs={{16,0},{32,16},{48,32},{64,48},{80,64},{96,80},{112,96},{17,1},{33... | collective-permute-start | bytes 1572872 | tf_op jit(solution)/shard_map/ppermute | solution.py:280
  113.8 10.6 %collective-permute-start.23 = (bf16[2,128,512]{2,1,0:T(8,128)(2,1)}, bf16[2,128,512]{2,1,0:T(8,128)(2,1)S(1)}, u32[]{:S(2)}, u32[]{:S(2)}) collective-permute-start(bf16[2,128,512]{2,1,0:T(8,128)(2,1)} %get-tuple-element.96), channel_id=1, source_target_pairs={{1,0},{2,1},{3,2},{4,3},{5,4},{6,5},{7,6},{8,7},{9,8},{10,9},{11,1... | collective-permute-start | bytes 786440 | tf_op jit(solution)/shard_map/ppermute | solution.py:276
  124.5 10.5 %collective-permute-start.24 = (bf16[4,128,512]{2,1,0:T(8,128)(2,1)S(1)}, bf16[4,128,512]{2,1,0:T(8,128)(2,1)S(1)}, u32[]{:S(2)}, u32[]{:S(2)}) collective-permute-start(bf16[4,128,512]{2,1,0:T(8,128)(2,1)S(1)} %pad_maximum_fusion.2), channel_id=1, source_target_pairs={{0,16},{16,32},{32,48},{48,64},{64,80},{80,96},{96,112},{1,17},{17... | collective-permute-start | bytes 1572872 | tf_op jit(solution)/shard_map/ppermute | solution.py:279
  142.0 12.8 %collective-permute-start.26 = (bf16[4,128,256]{2,1,0:T(8,128)(2,1)}, bf16[4,128,256]{2,1,0:T(8,128)(2,1)S(1)}, u32[]{:S(2)}, u32[]{:S(2)}) collective-permute-start(bf16[4,128,256]{2,1,0:T(8,128)(2,1)} %get-tuple-element.97), channel_id=1, source_target_pairs={{0,1},{1,2},{2,3},{3,0},{4,5},{5,6},{6,7},{7,4},{8,9},{9,10},{10,1... | collective-permute-start | bytes 786440 | tf_op jit(solution)/shard_map/ppermute | solution.py:39
  147.5 10.7 %collective-permute-start.28 = (bf16[4,128,256]{2,1,0:T(8,128)(2,1)}, bf16[4,128,256]{2,1,0:T(8,128)(2,1)S(1)}, u32[]{:S(2)}, u32[]{:S(2)}) collective-permute-start(bf16[4,128,256]{2,1,0:T(8,128)(2,1)} %get-tuple-element.97), channel_id=1, source_target_pairs={{0,3},{1,0},{2,1},{3,2},{4,7},{5,4},{6,5},{7,6},{8,11},{9,8},{10,9... | collective-permute-start | bytes 786440 | tf_op jit(solution)/shard_map/ppermute | solution.py:39
  150.2 10.4 %collective-permute-start.34 = (bf16[4,128,256]{2,1,0:T(8,128)(2,1)}, bf16[4,128,256]{2,1,0:T(8,128)(2,1)S(1)}, u32[]{:S(2)}, u32[]{:S(2)}) collective-permute-start(bf16[4,128,256]{2,1,0:T(8,128)(2,1)} %get-tuple-element.99), channel_id=1, source_target_pairs={{0,12},{1,13},{2,14},{3,15},{4,0},{5,1},{6,2},{7,3},{8,4},{9,5},{1... | collective-permute-start | bytes 786440 | tf_op jit(solution)/shard_map/ppermute | solution.py:39
  155.8 10.4 %collective-permute-start.30 = (bf16[4,128,256]{2,1,0:T(8,128)(2,1)S(1)}, bf16[4,128,256]{2,1,0:T(8,128)(2,1)S(1)}, u32[]{:S(2)}, u32[]{:S(2)}) collective-permute-start(bf16[4,128,256]{2,1,0:T(8,128)(2,1)S(1)} %collective-permute-done.29), channel_id=1, source_target_pairs={{0,4},{1,5},{2,6},{3,7},{4,8},{5,9},{6,10},{7,11},{8,12},{9,13},{1... | collective-permute-start | bytes 786440 | tf_op jit(solution)/shard_map/ppermute | solution.py:39
  158.1 15.0 %collective-permute-start.41 = (bf16[8,128,256]{2,1,0:T(8,128)(2,1)S(1)}, bf16[8,128,256]{2,1,0:T(8,128)(2,1)S(1)}, u32[]{:S(2)}, u32[]{:S(2)}) collective-permute-start(bf16[8,128,256]{2,1,0:T(8,128)(2,1)S(1)} %constant_dynamic-update-slice_fusion.4.rest_8_), channel_id=1, source_target_pairs={{0,3},{1,0},{2,1},{3,2},{4,7},{5,4},{6,5},{7,6},{8,11},{9,8},{10,9... | collective-permute-start | bytes 1572872 | tf_op jit(solution)/shard_map/ppermute | solution.py:39
  160.6 15.8 %collective-permute-start.35 = (bf16[8,128,256]{2,1,0:T(8,128)(2,1)S(1)}, bf16[8,128,256]{2,1,0:T(8,128)(2,1)S(1)}, u32[]{:S(2)}, u32[]{:S(2)}) collective-permute-start(bf16[8,128,256]{2,1,0:T(8,128)(2,1)S(1)} %constant_dynamic-update-slice_fusion.rest_0_), channel_id=1, source_target_pairs={{0,12},{1,13},{2,14},{3,15},{4,0},{5,1},{6,2},{7,3},{8,4},{9,5},{1... | collective-permute-start | bytes 1572872 | tf_op jit(solution)/shard_map/ppermute | solution.py:39
  164.9 15.4 %collective-permute-start.38 = (bf16[8,128,256]{2,1,0:T(8,128)(2,1)S(1)}, bf16[8,128,256]{2,1,0:T(8,128)(2,1)S(1)}, u32[]{:S(2)}, u32[]{:S(2)}) collective-permute-start(bf16[8,128,256]{2,1,0:T(8,128)(2,1)S(1)} %constant_dynamic-update-slice_fusion.4.rest_8_), channel_id=1, source_target_pairs={{0,1},{1,2},{2,3},{3,0},{4,5},{5,6},{6,7},{7,4},{8,9},{9,10},{10,1... | collective-permute-start | bytes 1572872 | tf_op jit(solution)/shard_map/ppermute | solution.py:39
  166.2 15.1 %collective-permute-start.31 = (bf16[8,128,256]{2,1,0:T(8,128)(2,1)S(1)}, bf16[8,128,256]{2,1,0:T(8,128)(2,1)S(1)}, u32[]{:S(2)}, u32[]{:S(2)}) collective-permute-start(bf16[8,128,256]{2,1,0:T(8,128)(2,1)S(1)} %constant_dynamic-update-slice_fusion.rest_0_), channel_id=1, source_target_pairs={{0,4},{1,5},{2,6},{3,7},{4,8},{5,9},{6,10},{7,11},{8,12},{9,13},{1... | collective-permute-start | bytes 1572872 | tf_op jit(solution)/shard_map/ppermute | solution.py:39
  173.1 14.7 %collective-permute-start.42 = (bf16[8,128,256]{2,1,0:T(8,128)(2,1)S(1)}, bf16[8,128,256]{2,1,0:T(8,128)(2,1)S(1)}, u32[]{:S(2)}, u32[]{:S(2)}) collective-permute-start(bf16[8,128,256]{2,1,0:T(8,128)(2,1)S(1)} %constant_dynamic-update-slice_fusion.6.rest_9_), channel_id=1, source_target_pairs={{0,3},{1,0},{2,1},{3,2},{4,7},{5,4},{6,5},{7,6},{8,11},{9,8},{10,9... | collective-permute-start | bytes 1572872 | tf_op jit(solution)/shard_map/ppermute | solution.py:39
  176.5 15.0 %collective-permute-start.36 = (bf16[8,128,256]{2,1,0:T(8,128)(2,1)S(1)}, bf16[8,128,256]{2,1,0:T(8,128)(2,1)S(1)}, u32[]{:S(2)}, u32[]{:S(2)}) collective-permute-start(bf16[8,128,256]{2,1,0:T(8,128)(2,1)S(1)} %constant_dynamic-update-slice_fusion.2.rest_1_), channel_id=1, source_target_pairs={{0,12},{1,13},{2,14},{3,15},{4,0},{5,1},{6,2},{7,3},{8,4},{9,5},{1... | collective-permute-start | bytes 1572872 | tf_op jit(solution)/shard_map/ppermute | solution.py:39
  180.3 14.6 %collective-permute-start.39 = (bf16[8,128,256]{2,1,0:T(8,128)(2,1)S(1)}, bf16[8,128,256]{2,1,0:T(8,128)(2,1)S(1)}, u32[]{:S(2)}, u32[]{:S(2)}) collective-permute-start(bf16[8,128,256]{2,1,0:T(8,128)(2,1)S(1)} %constant_dynamic-update-slice_fusion.6.rest_9_), channel_id=1, source_target_pairs={{0,1},{1,2},{2,3},{3,0},{4,5},{5,6},{6,7},{7,4},{8,9},{9,10},{10,1... | collective-permute-start | bytes 1572872 | tf_op jit(solution)/shard_map/ppermute | solution.py:39
  181.3 14.5 %collective-permute-start.32 = (bf16[8,128,256]{2,1,0:T(8,128)(2,1)S(1)}, bf16[8,128,256]{2,1,0:T(8,128)(2,1)S(1)}, u32[]{:S(2)}, u32[]{:S(2)}) collective-permute-start(bf16[8,128,256]{2,1,0:T(8,128)(2,1)S(1)} %constant_dynamic-update-slice_fusion.2.rest_1_), channel_id=1, source_target_pairs={{0,4},{1,5},{2,6},{3,7},{4,8},{5,9},{6,10},{7,11},{8,12},{9,13},{1... | collective-permute-start | bytes 1572872 | tf_op jit(solution)/shard_map/ppermute | solution.py:39
  187.7 14.1 %collective-permute-start.43 = (bf16[8,128,256]{2,1,0:T(8,128)(2,1)S(1)}, bf16[8,128,256]{2,1,0:T(8,128)(2,1)S(1)}, u32[]{:S(2)}, u32[]{:S(2)}) collective-permute-start(bf16[8,128,256]{2,1,0:T(8,128)(2,1)S(1)} %collective-permute-done.42.rest_15_), channel_id=1, source_target_pairs={{0,3},{1,0},{2,1},{3,2},{4,7},{5,4},{6,5},{7,6},{8,11},{9,8},{10,9... | collective-permute-start | bytes 1572872 | tf_op jit(solution)/shard_map/ppermute | solution.py:39
  191.4 13.5 %collective-permute-start.37 = (bf16[8,128,256]{2,1,0:T(8,128)(2,1)S(1)}, bf16[8,128,256]{2,1,0:T(8,128)(2,1)S(1)}, u32[]{:S(2)}, u32[]{:S(2)}) collective-permute-start(bf16[8,128,256]{2,1,0:T(8,128)(2,1)S(1)} %collective-permute-done.36.rest_7_), channel_id=1, source_target_pairs={{0,12},{1,13},{2,14},{3,15},{4,0},{5,1},{6,2},{7,3},{8,4},{9,5},{1... | collective-permute-start | bytes 1572872 | tf_op jit(solution)/shard_map/ppermute | solution.py:39
  194.9 13.7 %collective-permute-start.40 = (bf16[8,128,256]{2,1,0:T(8,128)(2,1)S(1)}, bf16[8,128,256]{2,1,0:T(8,128)(2,1)S(1)}, u32[]{:S(2)}, u32[]{:S(2)}) collective-permute-start(bf16[8,128,256]{2,1,0:T(8,128)(2,1)S(1)} %collective-permute-done.38.rest_10_), channel_id=1, source_target_pairs={{0,1},{1,2},{2,3},{3,0},{4,5},{5,6},{6,7},{7,4},{8,9},{9,10},{10,1... | collective-permute-start | bytes 1572872 | tf_op jit(solution)/shard_map/ppermute | solution.py:39
  195.8 13.5 %collective-permute-start.33 = (bf16[8,128,256]{2,1,0:T(8,128)(2,1)S(1)}, bf16[8,128,256]{2,1,0:T(8,128)(2,1)S(1)}, u32[]{:S(2)}, u32[]{:S(2)}) collective-permute-start(bf16[8,128,256]{2,1,0:T(8,128)(2,1)S(1)} %collective-permute-done.31.rest_2_), channel_id=1, source_target_pairs={{0,4},{1,5},{2,6},{3,7},{4,8},{5,9},{6,10},{7,11},{8,12},{9,13},{1... | collective-permute-start | bytes 1572872 | tf_op jit(solution)/shard_map/ppermute | solution.py:39
  (54 other events, 849.8 us)

commit v2 on v1

--- a/solution.py
+++ b/solution.py
@@ -15,7 +15,10 @@
 D = 512
 HALF = 256
 OWN = 4
-PARAMS = pltpu.CompilerParams(vmem_limit_bytes=56 * 1024 * 1024)
+
+
+def params(mib):
+    return pltpu.CompilerParams(vmem_limit_bytes=mib * 1024 * 1024)
 
 
 def dot(a, b):
@@ -27,7 +30,8 @@
 
 
 def silu(v):
-    return v * jax.nn.sigmoid(v)
+    half = 0.5 * v
+    return half + half * jnp.tanh(half)
 
 
 def shift(value, axis, step):
@@ -58,74 +62,82 @@
     return owner // SIDE, owner % SIDE, row * 2 + col % 2
 
 
-PARTS = ((2, 1), (3, 0))
-ORDER = ((2, 0), (3, 0), (2, 1), (1, 0), (3, 1), (1, 1), (0, 0), (0, 1))
-BLOCKS = 4
-STEPS = 6
-
-
-def encode_kernel(dest_ref, x_ref, embed_ref, send_ref, edges_ref, *rest):
-    outs, (acc, stage, sems) = rest[:16], rest[16:]
-    i = pl.program_id(0)
-
-    @pl.when(i == 0)
-    def _():
-        acc[...] = jnp.zeros_like(acc)
-
-    latent = silu(dot_t(x_ref[...], embed_ref[...])).astype(BF16)
-    proj = dot(latent, send_ref[...]).astype(BF16)
+CHUNKS = 3
+CHUNK_BLOCKS = 8
+CHUNK = CHUNK_BLOCKS * NB
+
+
+def encode_kernel(dest_ref, x_hbm, embed_hbm, send_hbm, edges_hbm, out_0, out_1, x, embed, send, edges, sems):
+    copies = [
+        pltpu.make_async_copy(embed_hbm, embed, sems.at[0]),
+        pltpu.make_async_copy(x_hbm.at[:, pl.ds(0, CHUNK)], x.at[0], sems.at[1]),
+        pltpu.make_async_copy(send_hbm, send, sems.at[2]),
+        pltpu.make_async_copy(edges_hbm.at[pl.ds(0, CHUNK_BLOCKS)], edges.at[0], sems.at[3]),
+    ]
+    for c in range(1, CHUNKS):
+        copies += [
+            pltpu.make_async_copy(x_hbm.at[:, pl.ds(c * CHUNK, CHUNK)], x.at[c], sems.at[2 * c + 2]),
+            pltpu.make_async_copy(
+                edges_hbm.at[pl.ds(c * CHUNK_BLOCKS, CHUNK_BLOCKS)], edges.at[c], sems.at[2 * c + 3]
+            ),
+        ]
+    for copy in copies:
+        copy.start()
+    out_0[...] = jnp.zeros_like(out_0)
+    out_1[...] = jnp.zeros_like(out_1)
     me = lax.axis_index("mesh")
     my_y, my_z = me // SIDE, me % SIDE
-    for b in range(BLOCKS):
-        block = proj[b * NB : (b + 1) * NB]
-        for j in range(3):
-            y, z, local = place(dest_ref[j, i * BLOCKS + b])
-            slot = (((y - my_y) & 3) * SIDE + ((z - my_z) & 3)) * OWN + local
-            acc[slot] += dot_t(edges_ref[b, j], block)
-
-    @pl.when(i == STEPS - 1)
-    def _():
-        copies = []
-        for n, (k, part) in enumerate(ORDER):
-            for h in range(2):
-                for m, q in enumerate(PARTS[part]):
-                    base = (k * SIDE + q if h == 0 else q * SIDE + k) * OWN
-                    stage[h, n, m * OWN : (m + 1) * OWN] = acc[
-                        base : base + OWN, :, h * HALF : (h + 1) * HALF
-                    ].astype(BF16)
-                copy = pltpu.make_async_copy(stage.at[h, n], outs[h * 8 + n], sems.at[h * 8 + n])
-                copy.start()
-                copies.append(copy)
-        for copy in copies:
-            copy.wait()
+    for c in range(CHUNKS):
+        if c == 0:
+            copies[0].wait()
+            copies[1].wait()
+        else:
+            copies[2 * c + 2].wait()
+        latent = silu(dot_t(x[c], embed[...])).astype(BF16)
+        if c == 0:
+            copies[2].wait()
+        proj = dot(latent, send[...]).astype(BF16)
+        copies[2 * c + 3].wait()
+        for b in range(CHUNK_BLOCKS):
+            weights = jnp.concatenate([edges[c, b, j] for j in range(3)], 1)
+            message = dot_t(weights, proj[b * NB : (b + 1) * NB])
+            for j in range(3):
+                y, z, local = place(dest_ref[j, c * CHUNK_BLOCKS + b])
+                dy, dz = (y - my_y) & 3, (z - my_z) & 3
+                part = message[j * NB : (j + 1) * NB]
+                at_0 = (dy * SIDE + ((2 - dz) & 3)) * OWN + local
+                at_1 = (dz * SIDE + ((2 - dy) & 3)) * OWN + local
+                out_0[at_0] = (out_0[at_0].astype(F32) + part[:, :HALF]).astype(BF16)
+                out_1[at_1] = (out_1[at_1].astype(F32) + part[:, HALF:]).astype(BF16)
+
+
+def in_hbm(value):
+    return pltpu.with_memory_space_constraint(value, pltpu.HBM)
 
 
 def encode(grid_inputs, embed_weight, send_weight, g2m_dest, g2m_edges):
-    rows = BLOCKS * NB
-
     inputs_t = grid_inputs.T
-    return pl.pallas_call(
+    width = inputs_t.shape[0]
+    halves = pl.pallas_call(
         encode_kernel,
-        grid_spec=pltpu.PrefetchScalarGridSpec(
-            num_scalar_prefetch=1,
-            grid=(STEPS,),
-            in_specs=[
-                pl.BlockSpec((inputs_t.shape[0], rows), lambda i, *_: (0, i)),
-                pl.BlockSpec(embed_weight.shape, lambda i, *_: (0, 0)),
-                pl.BlockSpec(send_weight.shape, lambda i, *_: (0, 0)),
-                pl.BlockSpec((BLOCKS, 3, NB, NB), lambda i, *_: (i, 0, 0, 0)),
-            ],
-            out_specs=[pl.BlockSpec(memory_space=pl.ANY)] * 16,
-            scratch_shapes=[
-                pltpu.VMEM((64, NB, D), F32),
-                pltpu.VMEM((2, 8, 8, NB, HALF), BF16),
-                pltpu.SemaphoreType.DMA((16,)),
-            ],
-        ),
-        out_shape=[jax.ShapeDtypeStruct((8, NB, HALF), BF16)] * 16,
-        compiler_params=PARAMS,
+        in_specs=[pl.BlockSpec(memory_space=pltpu.SMEM)] + [pl.BlockSpec(memory_space=pltpu.HBM)] * 4,
+        out_specs=[pl.BlockSpec(memory_space=pltpu.VMEM)] * 2,
+        out_shape=[pltpu.VMEM((64, NB, HALF), BF16)] * 2,
+        scratch_shapes=[
+            pltpu.VMEM((CHUNKS, width, CHUNK), BF16),
+            pltpu.VMEM(embed_weight.shape, BF16),
+            pltpu.VMEM(send_weight.shape, BF16),
+            pltpu.VMEM((CHUNKS, CHUNK_BLOCKS, 3, NB, NB), BF16),
+            pltpu.SemaphoreType.DMA((2 * CHUNKS + 2,)),
+        ],
+        compiler_params=params(28),
         name="encode",
-    )(g2m_dest.T, inputs_t, embed_weight, send_weight, g2m_edges)
+    )(*map(in_hbm, (g2m_dest.T, inputs_t, embed_weight, send_weight, g2m_edges)))
+    cuts = [(k, part) for k in range(4) for part in range(2)]
+    return [
+        dict(zip(cuts, lax.optimization_barrier([half[16 * k + 8 * part :][:8] for k, part in cuts])))
+        for half in halves
+    ]
 
 
 def add(*values):
@@ -135,10 +147,9 @@
     return total.astype(BF16)
 
 
-def reduce(pieces):
+def reduce(piece):
     both = range(2)
     links = Links()
-    piece = [dict(zip(ORDER, pieces[8 * h : 8 * h + 8])) for h in both]
 
     def far(part, step):
         return [links.send(piece[h][2, part], h, step) for h in both]
@@ -168,7 +179,7 @@
     up_1 = near(1, 1, None)
     sums_1 = settled(0, 1, up_0, down_0, from_2)
     from_1 = [links.send(sums_1[h], 1 - h, 1) for h in both]
-    sums_3 = settled(1, 0, up_1, down_1)
+    sums_3 = settled(1, 1, up_1, down_1)
     from_3 = [links.send(sums_3[h], 1 - h, -1) for h in both]
     terms = []
     for h in both:
@@ -182,7 +193,7 @@
     for h in range(2):
         value = None
         for term in terms[5 * h : 5 * h + 5]:
-            term = term[term.shape[0] - OWN :].astype(F32)
+            term = term[:OWN].astype(F32)
             value = term if value is None else value + term
         act = silu(value).astype(BF16).reshape(OWN * NB, HALF)
         part = dot(act, encode_ref[h * HALF : (h + 1) * HALF, :])
@@ -194,40 +205,37 @@
 
 def put_sent(sent, refs):
     sent = sent.reshape(2, 2, NB, D)
-    all_ref, first_ref, last_ref = refs
-    all_ref[...] = sent
-    first_ref[...] = sent[:, 0]
-    last_ref[...] = sent[:, 1]
+    for n in range(2):
+        refs[n][...] = sent[n]
+        refs[2 + n][...] = sent[:, n]
 
 
 def sent_shapes():
-    column = jax.ShapeDtypeStruct((2, NB, D), BF16)
-    return [
-        jax.ShapeDtypeStruct((OWN * NB, D), BF16),
-        jax.ShapeDtypeStruct((2, 2, NB, D), BF16),
-        column,
-        column,
-    ]
+    return [jax.ShapeDtypeStruct((OWN * NB, D), BF16)] + [
+        jax.ShapeDtypeStruct((2, NB, D), BF16)
+    ] * 4
 
 
 def mesh_start(terms, encode_weight, message_weight):
     return pl.pallas_call(
         start_kernel,
         out_shape=sent_shapes(),
-        compiler_params=PARAMS,
+        compiler_params=params(12),
         name="mesh_start",
     )(*terms, encode_weight, message_weight)
 
 
-def step_kernel(layer, codes_ref, count_ref, mesh_ref, own_ref, left_ref, right_ref, above_ref, below_ref,
-                couplings_ref, node_ref, next_ref, *rest):
+def step_kernel(layer, codes_ref, count_ref, mesh_ref, *rest):
+    band, (couplings_ref, node_ref, next_ref), rest = rest[:8], rest[8:11], rest[11:]
     outs, (pad, normed) = rest[:-2], rest[-2:]
-    pad[0:4] = above_ref[...]
-    pad[12:16] = below_ref[...]
+    left, right, above, rows_0, rows_1, below, corners_above, corners_below = band
+    for row, middle in enumerate((above, rows_0, rows_1, below)):
+        pad[4 * row + 1 : 4 * row + 3] = middle[...]
     for r in range(2):
-        pad[4 * (r + 1)] = left_ref[r]
-        pad[4 * (r + 1) + 1 : 4 * (r + 1) + 3] = own_ref[r]
-        pad[4 * (r + 1) + 3] = right_ref[r]
+        pad[4 * r + 4] = left[r]
+        pad[4 * r + 7] = right[r]
+        pad[3 * r] = corners_above[r]
+        pad[12 + 3 * r] = corners_below[r]
     for r in range(2):
         for c in range(2):
             near, weights = [], []
@@ -251,7 +259,7 @@
         outs[1][...] = proj[:, :, HALF:]
 
 
-def mesh_step(layer, codes, count, mesh, sent, halo, couplings, node_weight, next_weight):
+def mesh_step(layer, codes, count, mesh, band, couplings, node_weight, next_weight):
     if layer == 0:
         out_shape = sent_shapes()
     else:
@@ -260,25 +268,30 @@
     vmem = pl.BlockSpec(memory_space=pltpu.VMEM)
     return pl.pallas_call(
         functools.partial(step_kernel, layer),
-        in_specs=[smem, smem] + [vmem] * 9,
+        in_specs=[smem, smem] + [vmem] * 12,
         out_shape=out_shape,
         scratch_shapes=[pltpu.VMEM((16, NB, D), BF16), pltpu.VMEM((OWN * NB, D), BF16)],
-        compiler_params=PARAMS,
+        compiler_params=params(16),
         name="mesh_step",
-    )(codes, count, mesh, sent[0], *halo, couplings, node_weight, next_weight)
-
-
-def halo_of(grid, first, last):
+    )(codes, count, mesh, *band, couplings, node_weight, next_weight)
+
+
+def band_of(row_0, row_1, first, last):
     size, length = lax.axis_size("mesh"), lax.axis_size("grid")
     ahead = lambda n: [(i, i + 1) for i in range(n - 1)]
     back = lambda n: [(i + 1, i) for i in range(n - 1)]
     left = lax.ppermute(last, "mesh", ahead(size))
     right = lax.ppermute(first, "mesh", back(size))
-    top = jnp.concatenate([left[:1], grid[0], right[:1]], 0)
-    bottom = jnp.concatenate([left[1:], grid[1], right[1:]], 0)
-    above = lax.ppermute(bottom, "grid", ahead(length))
-    below = lax.ppermute(top, "grid", back(length))
-    return left, right, above, below
+    above = lax.ppermute(row_1, "grid", ahead(length))
+    below = lax.ppermute(row_0, "grid", back(length))
+    corners = [jnp.concatenate([left[r : r + 1], right[r : r + 1]], 0) for r in range(2)]
+    corners_above = lax.ppermute(corners[1], "grid", ahead(length))
+    corners_below = lax.ppermute(corners[0], "grid", back(length))
+    return left, right, above, row_0, row_1, below, corners_above, corners_below
+
+
+BLOCKS = 8
+STEPS = 3
 
 
 def gather(owns):
@@ -302,7 +315,7 @@
 
 
 def decode_kernel(src_ref, x_ref, edges_ref, output_ref, *rest):
-    pieces, (out_ref, held, sems) = rest[:16], rest[16:]
+    pieces, (out_ref, held, hidden, sems) = rest[:16], rest[16:]
     i = pl.program_id(0)
 
     @pl.when(i == 0)
@@ -327,18 +340,13 @@
             first.append(held[0, (ky * SIDE + kz) * OWN + local])
             second.append(held[1, (kz * SIDE + ky) * OWN + local])
         edges = edges_ref[b].reshape(3 * NB, NB)
-        total = None
         for h, parts in enumerate((first, second)):
-            hidden = silu(dot_t(edges, jnp.concatenate(parts, 0))).astype(BF16)
-            term = lax.dot_general(
-                output_ref[:, h * HALF : (h + 1) * HALF],
-                hidden,
-                (((1,), (1,)), ((), ())),
-                preferred_element_type=F32,
-            )
-            total = term if total is None else total + term
-        columns = pl.ds(b * NB, NB)
-        out_ref[:, columns] = (x_ref[:, columns].astype(F32) + total).astype(BF16)
+            decoded = dot_t(edges, jnp.concatenate(parts, 0))
+            hidden[b * NB : (b + 1) * NB, h * HALF : (h + 1) * HALF] = silu(decoded).astype(BF16)
+    total = lax.dot_general(
+        output_ref[...], hidden[...], (((1,), (1,)), ((), ())), preferred_element_type=F32
+    )
+    out_ref[...] = (x_ref[...].astype(F32) + total).astype(BF16)
 
 
 def decode(grid_inputs, m2g_src, m2g_edges, output_weight, pieces):
@@ -359,11 +367,12 @@
             out_specs=pl.BlockSpec((width, rows), lambda i, *_: (0, i)),
             scratch_shapes=[
                 pltpu.VMEM((2, 64, NB, HALF), BF16),
+                pltpu.VMEM((rows, D), BF16),
                 pltpu.SemaphoreType.DMA((16,)),
             ],
         ),
         out_shape=jax.ShapeDtypeStruct(inputs_t.shape, BF16),
-        compiler_params=PARAMS,
+        compiler_params=params(20),
         name="decode",
     )(m2g_src.T, inputs_t, m2g_edges, output_t, *pieces)
     return result.T
@@ -390,10 +399,10 @@
     mesh, *sent = mesh_start(reduce(pieces), encode_weight, message_weight)
     codes = adj_codes.reshape(OWN, -1)
     mesh, *sent = mesh_step(
-        0, codes, adj_count, mesh, sent, halo_of(*sent), couplings, node_weight, message_weight
+        0, codes, adj_count, mesh, band_of(*sent), couplings, node_weight, message_weight
     )
     owns = mesh_step(
-        1, codes, adj_count, mesh, sent, halo_of(*sent), couplings, node_weight, decode_weight
+        1, codes, adj_count, mesh, band_of(*sent), couplings, node_weight, decode_weight
     )
     return decode(grid_inputs, m2g_src, m2g_edges, output_weight, gather(owns))
 

time: 226 us -> 195 us (0.86)
  Pallas kernels: 41.2 us -> 20.2 us
  waiting for transfers between devices: 96.2 us -> 79.6 us
  starting transfers between devices: 75.5 us -> 90.8 us
  local copies, waits for them, and re-layouts: 7.49 us -> 1.59 us
  other arithmetic: 3.68 us -> 1.29 us
    ppermute x8 -> x12, waiting for transfers between devices: 27.6 us -> 12.5 us  [the longest x2 4.76 us: band_of(): right = lax.ppermute(first, 'mesh', back(size))]
    ppermute x8 -> x12, starting transfers between devices: 18.2 us -> 31.9 us  [the longest x2 6.94 us: band_of(): left = lax.ppermute(last, 'mesh', ahead(size))]
    pallas_call x1, Pallas kernels: 14.4 us -> 6.29 us  [decode(): pl.pallas_call(decode_kernel, grid_spec=pltpu.PrefetchScalarGridSpec(num_...]
    pallas_call x2, Pallas kernels: 17.7 us -> 10 us  [the longest x1 9.12 us: encode(): pl.pallas_call(encode_kernel, in_specs=[pl.BlockSpec(memory_space=pltpu.S...]
    pallas_call x2, Pallas kernels: 9.13 us -> 3.85 us  [mesh_step(): pl.pallas_call(functools.partial(step_kernel, layer), in_specs=[smem, sme...]
    unnamed x88 -> x26, local copies, waits for them, and re-layouts: 5.21 us -> 0.13 us
  transfers between devices with their start and end apart: 44 -> 48, of which waited for: 32 -> 28; matrix products, arithmetic and copies ran while one was open for 3% -> 1% of each run, Pallas kernels for 0% -> 0%
where the time goes in v2:
time: 195 us; the launch traced here: 194 us
  starting transfers between devices  90.8 us (47%)
  waiting for transfers between devices  79.6 us (41%)
  Pallas kernels  20.2 us (10%)
    ppermute x36, waiting for transfers between devices, shift(): return lax.ppermute(value, 'mesh', pairs)  67.1 us
    ppermute x36, starting transfers between devices, shift(): return lax.ppermute(value, 'mesh', pairs)  58.9 us
    pallas_call x1, Pallas kernels, encode(): pl.pallas_call(encode_kernel, in_specs=[pl.BlockSpec(memory_space=pltpu.S...  9.12 us
    ppermute x2, starting transfers between devices, band_of(): left = lax.ppermute(last, 'mesh', ahead(size))  6.94 us
    ppermute x2, starting transfers between devices, band_of(): corners_below = lax.ppermute(corners[0], 'grid', back(length))  6.73 us
    pallas_call x1, Pallas kernels, decode(): pl.pallas_call(decode_kernel, grid_spec=pltpu.PrefetchScalarGridSpec(num_...  6.29 us
    ppermute x2, starting transfers between devices, band_of(): below = lax.ppermute(row_0, 'grid', back(length))  5.82 us
    ppermute x2, starting transfers between devices, band_of(): above = lax.ppermute(row_1, 'grid', ahead(length))  5.3 us
  transfers between devices with their start and end apart: 48, of which 28 were waited for; matrix products, arithmetic and copies ran while one was open for 1% of the time, Pallas kernels for 0%

profile of v2, /device:TPU:2, one launch (start us, length us, event | category | flops | bytes accessed | tf_op | source)
XLA Modules:
  0.0 194.1 jit_solution(11594829515544511409)
XLA Ops:
  0.0 9.1 %encode.1 = (bf16[64,128,256]{2,1,0:T(8,128)(2,1)S(1)}, bf16[64,128,256]{2,1,0:T(8,128)(2,1)S(1)}) custom-call(s32[3,24]{1,0:T(4,128)} %bitcast.12, bf16[227,3072]{1,0:T(8,128)(2,1)} %bitcast.6, bf16[227,512]{1,0:T(8,128)(2,1)} %embed_hbm.1, bf16[512,512]{1,0:T(8,128)(2,1)} %send_hbm.1, bf16[24,3,128,128]{3,2,1,0:T(8,128)(2,1)} %edges_hbm.1), custom_call_target="tpu_custom_call" | custom-call | tf_op jit(solution)/shard_map/encode/pallas_call | solution.py:121
  17.8 7.7 %collective-permute-done.3 = bf16[8,128,256]{2,1,0:T(8,128)(2,1)S(1)} collective-permute-done((bf16[8,128,256]{2,1,0:T(8,128)(2,1)S(1)}, bf16[8,128,256]{2,1,0:T(8,128)(2,1)S(1)}, u32[]{:S(2)}, u32[]{:S(2)}) %collective-permute-start.3) | collective-permute-done | bytes 524320 | tf_op jit(solution)/shard_map/ppermute | solution.py:43
  28.1 2.9 %collective-permute-start.8 = (bf16[8,128,256]{2,1,0:T(8,128)(2,1)S(1)}, bf16[8,128,256]{2,1,0:T(8,128)(2,1)S(1)}, u32[]{:S(2)}, u32[]{:S(2)}) collective-permute-start(bf16[8,128,256]{2,1,0:T(8,128)(2,1)S(1)} %get-tuple-element.80), channel_id=1, source_target_pairs={{0,12},{1,13},{2,14},{3,15},{4,0},{5,1},{6,2},{7,3},{8,4},{9,5},{1... | collective-permute-start | bytes 1572872 | tf_op jit(solution)/shard_map/ppermute | solution.py:43
  33.2 6.5 %collective-permute-done.4 = bf16[8,128,256]{2,1,0:T(8,128)(2,1)S(1)} collective-permute-done((bf16[8,128,256]{2,1,0:T(8,128)(2,1)S(1)}, bf16[8,128,256]{2,1,0:T(8,128)(2,1)S(1)}, u32[]{:S(2)}, u32[]{:S(2)}) %collective-permute-start.4) | collective-permute-done | bytes 524320 | tf_op jit(solution)/shard_map/ppermute | solution.py:43
  45.6 3.9 %collective-permute-done.10 = bf16[4,128,256]{2,1,0:T(8,128)(2,1)S(1)} collective-permute-done((bf16[4,128,256]{2,1,0:T(8,128)(2,1)S(1)}, bf16[4,128,256]{2,1,0:T(8,128)(2,1)S(1)}, u32[]{:S(2)}, u32[]{:S(2)}) %collective-permute-start.10) | collective-permute-done | bytes 262176 | tf_op jit(solution)/shard_map/ppermute | solution.py:43
  51.3 3.3 %collective-permute-start.14 = (bf16[8,128,256]{2,1,0:T(8,128)(2,1)S(1)}, bf16[8,128,256]{2,1,0:T(8,128)(2,1)S(1)}, u32[]{:S(2)}, u32[]{:S(2)}) collective-permute-start(bf16[8,128,256]{2,1,0:T(8,128)(2,1)S(1)} %add_convert_fusion), channel_id=1, source_target_pairs={{0,3},{1,0},{2,1},{3,2},{4,7},{5,4},{6,5},{7,6},{8,11},{9,8},{10,9... | collective-permute-start | bytes 1572872 | tf_op jit(solution)/shard_map/ppermute | solution.py:43
  54.8 6.8 %collective-permute-done.11.refs_6_ = bf16[8,128,256]{2,1,0:T(8,128)(2,1)S(1)} collective-permute-done((bf16[8,128,256]{2,1,0:T(8,128)(2,1)S(1)}, bf16[8,128,256]{2,1,0:T(8,128)(2,1)S(1)}, u32[]{:S(2)}, u32[]{:S(2)}) %collective-permute-start.11) | collective-permute-done | bytes 524320 | tf_op jit(solution)/shard_map/ppermute | solution.py:43
  65.6 3.0 %collective-permute-start.15 = (bf16[4,128,256]{2,1,0:T(8,128)(2,1)S(1)}, bf16[4,128,256]{2,1,0:T(8,128)(2,1)S(1)}, u32[]{:S(2)}, u32[]{:S(2)}) collective-permute-start(bf16[4,128,256]{2,1,0:T(8,128)(2,1)S(1)} %add_convert_fusion.6), channel_id=1, source_target_pairs={{0,3},{1,0},{2,1},{3,2},{4,7},{5,4},{6,5},{7,6},{8,11},{9,8},{10,9... | collective-permute-start | bytes 786440 | tf_op jit(solution)/shard_map/ppermute | solution.py:43
  69.9 2.5 %collective-permute-done.15.refs_4_ = bf16[4,128,256]{2,1,0:T(8,128)(2,1)S(1)} collective-permute-done((bf16[4,128,256]{2,1,0:T(8,128)(2,1)S(1)}, bf16[4,128,256]{2,1,0:T(8,128)(2,1)S(1)}, u32[]{:S(2)}, u32[]{:S(2)}) %collective-permute-start.15) | collective-permute-done | bytes 262176 | tf_op jit(solution)/shard_map/ppermute | solution.py:43
  73.4 3.0 %collective-permute-start.18 = (bf16[2,128,512]{2,1,0:T(8,128)(2,1)S(1)}, bf16[2,128,512]{2,1,0:T(8,128)(2,1)S(1)}, u32[]{:S(2)}, u32[]{:S(2)}) collective-permute-start(bf16[2,128,512]{2,1,0:T(8,128)(2,1)S(1)} %get-tuple-element.96), channel_id=1, source_target_pairs={{0,1},{1,2},{2,3},{3,4},{4,5},{5,6},{6,7},{7,8},{8,9},{9,10},{10,1... | collective-permute-start | bytes 786440 | tf_op jit(solution)/shard_map/ppermute | solution.py:283
  79.6 3.6 %collective-permute-start.21 = (bf16[2,128,512]{2,1,0:T(8,128)(2,1)S(1)}, bf16[2,128,512]{2,1,0:T(8,128)(2,1)S(1)}, u32[]{:S(2)}, u32[]{:S(2)}) collective-permute-start(bf16[2,128,512]{2,1,0:T(8,128)(2,1)S(1)} %get-tuple-element.99.rest_3_), channel_id=1, source_target_pairs={{16,0},{32,16},{48,32},{64,48},{80,64},{96,80},{112,96},{17,1},{33... | collective-permute-start | bytes 786440 | tf_op jit(solution)/shard_map/ppermute | solution.py:286
  86.8 3.6 %collective-permute-start.23 = (bf16[2,128,512]{2,1,0:T(8,128)(2,1)S(1)}, bf16[2,128,512]{2,1,0:T(8,128)(2,1)S(1)}, u32[]{:S(2)}, u32[]{:S(2)}) collective-permute-start(bf16[2,128,512]{2,1,0:T(8,128)(2,1)S(1)} %pad_maximum_fusion.1), channel_id=1, source_target_pairs={{16,0},{32,16},{48,32},{64,48},{80,64},{96,80},{112,96},{17,1},{33... | collective-permute-start | bytes 786440 | tf_op jit(solution)/shard_map/ppermute | solution.py:289
  96.3 3.9 %collective-permute-start.24 = (bf16[2,128,512]{2,1,0:T(8,128)(2,1)S(1)}, bf16[2,128,512]{2,1,0:T(8,128)(2,1)S(1)}, u32[]{:S(2)}, u32[]{:S(2)}) collective-permute-start(bf16[2,128,512]{2,1,0:T(8,128)(2,1)S(1)} %get-tuple-element.101), channel_id=1, source_target_pairs={{0,1},{1,2},{2,3},{3,4},{4,5},{5,6},{6,7},{7,8},{8,9},{9,10},{10,1... | collective-permute-start | bytes 786440 | tf_op jit(solution)/shard_map/ppermute | solution.py:283
  101.5 3.4 %collective-permute-start.26 = (bf16[2,128,512]{2,1,0:T(8,128)(2,1)S(1)}, bf16[2,128,512]{2,1,0:T(8,128)(2,1)S(1)}, u32[]{:S(2)}, u32[]{:S(2)}) collective-permute-start(bf16[2,128,512]{2,1,0:T(8,128)(2,1)S(1)} %get-tuple-element.103.rest_4_), channel_id=1, source_target_pairs={{0,16},{16,32},{32,48},{48,64},{64,80},{80,96},{96,112},{1,17},{17... | collective-permute-start | bytes 786440 | tf_op jit(solution)/shard_map/ppermute | solution.py:285
  107.2 3.4 %collective-permute-done.25.rest_1_ = bf16[2,128,512]{2,1,0:T(8,128)(2,1)S(1)} collective-permute-done((bf16[2,128,512]{2,1,0:T(8,128)(2,1)S(1)}, bf16[2,128,512]{2,1,0:T(8,128)(2,1)S(1)}, u32[]{:S(2)}, u32[]{:S(2)}) %collective-permute-start.25) | collective-permute-done | bytes 262176 | tf_op jit(solution)/shard_map/ppermute | solution.py:284
  113.1 3.1 %collective-permute-start.29 = (bf16[2,128,512]{2,1,0:T(8,128)(2,1)S(1)}, bf16[2,128,512]{2,1,0:T(8,128)(2,1)S(1)}, u32[]{:S(2)}, u32[]{:S(2)}) collective-permute-start(bf16[2,128,512]{2,1,0:T(8,128)(2,1)S(1)} %pad_maximum_fusion.3), channel_id=1, source_target_pairs={{16,0},{32,16},{48,32},{64,48},{80,64},{96,80},{112,96},{17,1},{33... | collective-permute-start | bytes 786440 | tf_op jit(solution)/shard_map/ppermute | solution.py:289
  125.5 3.6 %collective-permute-start.32 = (bf16[4,128,256]{2,1,0:T(8,128)(2,1)S(1)}, bf16[4,128,256]{2,1,0:T(8,128)(2,1)S(1)}, u32[]{:S(2)}, u32[]{:S(2)}) collective-permute-start(bf16[4,128,256]{2,1,0:T(8,128)(2,1)S(1)} %get-tuple-element.105), channel_id=1, source_target_pairs={{0,3},{1,0},{2,1},{3,2},{4,7},{5,4},{6,5},{7,6},{8,11},{9,8},{10,9... | collective-permute-start | bytes 786440 | tf_op jit(solution)/shard_map/ppermute | solution.py:43
  129.1 2.8 %collective-permute-start.38 = (bf16[4,128,256]{2,1,0:T(8,128)(2,1)S(1)}, bf16[4,128,256]{2,1,0:T(8,128)(2,1)S(1)}, u32[]{:S(2)}, u32[]{:S(2)}) collective-permute-start(bf16[4,128,256]{2,1,0:T(8,128)(2,1)S(1)} %get-tuple-element.107), channel_id=1, source_target_pairs={{0,12},{1,13},{2,14},{3,15},{4,0},{5,1},{6,2},{7,3},{8,4},{9,5},{1... | collective-permute-start | bytes 786440 | tf_op jit(solution)/shard_map/ppermute | solution.py:43
  131.9 2.5 %collective-permute-done.30 = bf16[4,128,256]{2,1,0:T(8,128)(2,1)S(1)} collective-permute-done((bf16[4,128,256]{2,1,0:T(8,128)(2,1)S(1)}, bf16[4,128,256]{2,1,0:T(8,128)(2,1)S(1)}, u32[]{:S(2)}, u32[]{:S(2)}) %collective-permute-start.30) | collective-permute-done | bytes 262176 | tf_op jit(solution)/shard_map/ppermute | solution.py:43
  135.1 3.7 %collective-permute-start.45 = (bf16[8,128,256]{2,1,0:T(8,128)(2,1)S(1)}, bf16[8,128,256]{2,1,0:T(8,128)(2,1)S(1)}, u32[]{:S(2)}, u32[]{:S(2)}) collective-permute-start(bf16[8,128,256]{2,1,0:T(8,128)(2,1)S(1)} %constant_dynamic-update-slice_fusion.4.rest_8_), channel_id=1, source_target_pairs={{0,3},{1,0},{2,1},{3,2},{4,7},{5,4},{6,5},{7,6},{8,11},{9,8},{10,9... | collective-permute-start | bytes 1572872 | tf_op jit(solution)/shard_map/ppermute | solution.py:43
  138.8 3.2 %collective-permute-start.39 = (bf16[8,128,256]{2,1,0:T(8,128)(2,1)S(1)}, bf16[8,128,256]{2,1,0:T(8,128)(2,1)S(1)}, u32[]{:S(2)}, u32[]{:S(2)}) collective-permute-start(bf16[8,128,256]{2,1,0:T(8,128)(2,1)S(1)} %constant_dynamic-update-slice_fusion.rest_0_), channel_id=1, source_target_pairs={{0,12},{1,13},{2,14},{3,15},{4,0},{5,1},{6,2},{7,3},{8,4},{9,5},{1... | collective-permute-start | bytes 1572872 | tf_op jit(solution)/shard_map/ppermute | solution.py:43
  141.9 2.7 %collective-permute-done.31 = bf16[4,128,256]{2,1,0:T(8,128)(2,1)S(1)} collective-permute-done((bf16[4,128,256]{2,1,0:T(8,128)(2,1)S(1)}, bf16[4,128,256]{2,1,0:T(8,128)(2,1)S(1)}, u32[]{:S(2)}, u32[]{:S(2)}) %collective-permute-start.31) | collective-permute-done | bytes 262176 | tf_op jit(solution)/shard_map/ppermute | solution.py:43
  145.1 5.6 %collective-permute-done.45.rest_14_ = bf16[8,128,256]{2,1,0:T(8,128)(2,1)S(1)} collective-permute-done((bf16[8,128,256]{2,1,0:T(8,128)(2,1)S(1)}, bf16[8,128,256]{2,1,0:T(8,128)(2,1)S(1)}, u32[]{:S(2)}, u32[]{:S(2)}) %collective-permute-start.45) | collective-permute-done | bytes 524320 | tf_op jit(solution)/shard_map/ppermute | solution.py:43
  150.6 3.7 %collective-permute-start.46 = (bf16[8,128,256]{2,1,0:T(8,128)(2,1)S(1)}, bf16[8,128,256]{2,1,0:T(8,128)(2,1)S(1)}, u32[]{:S(2)}, u32[]{:S(2)}) collective-permute-start(bf16[8,128,256]{2,1,0:T(8,128)(2,1)S(1)} %constant_dynamic-update-slice_fusion.6.rest_9_), channel_id=1, source_target_pairs={{0,3},{1,0},{2,1},{3,2},{4,7},{5,4},{6,5},{7,6},{8,11},{9,8},{10,9... | collective-permute-start | bytes 1572872 | tf_op jit(solution)/shard_map/ppermute | solution.py:43
  154.3 3.1 %collective-permute-start.40 = (bf16[8,128,256]{2,1,0:T(8,128)(2,1)S(1)}, bf16[8,128,256]{2,1,0:T(8,128)(2,1)S(1)}, u32[]{:S(2)}, u32[]{:S(2)}) collective-permute-start(bf16[8,128,256]{2,1,0:T(8,128)(2,1)S(1)} %constant_dynamic-update-slice_fusion.2.rest_1_), channel_id=1, source_target_pairs={{0,12},{1,13},{2,14},{3,15},{4,0},{5,1},{6,2},{7,3},{8,4},{9,5},{1... | collective-permute-start | bytes 1572872 | tf_op jit(solution)/shard_map/ppermute | solution.py:43
  160.1 5.3 %collective-permute-done.46.rest_15_ = bf16[8,128,256]{2,1,0:T(8,128)(2,1)S(1)} collective-permute-done((bf16[8,128,256]{2,1,0:T(8,128)(2,1)S(1)}, bf16[8,128,256]{2,1,0:T(8,128)(2,1)S(1)}, u32[]{:S(2)}, u32[]{:S(2)}) %collective-permute-start.46) | collective-permute-done | bytes 524320 | tf_op jit(solution)/shard_map/ppermute | solution.py:43
  165.5 3.7 %collective-permute-start.47 = (bf16[8,128,256]{2,1,0:T(8,128)(2,1)S(1)}, bf16[8,128,256]{2,1,0:T(8,128)(2,1)S(1)}, u32[]{:S(2)}, u32[]{:S(2)}) collective-permute-start(bf16[8,128,256]{2,1,0:T(8,128)(2,1)S(1)} %collective-permute-done.46.rest_15_), channel_id=1, source_target_pairs={{0,3},{1,0},{2,1},{3,2},{4,7},{5,4},{6,5},{7,6},{8,11},{9,8},{10,9... | collective-permute-start | bytes 1572872 | tf_op jit(solution)/shard_map/ppermute | solution.py:43
  169.2 3.2 %collective-permute-start.41 = (bf16[8,128,256]{2,1,0:T(8,128)(2,1)S(1)}, bf16[8,128,256]{2,1,0:T(8,128)(2,1)S(1)}, u32[]{:S(2)}, u32[]{:S(2)}) collective-permute-start(bf16[8,128,256]{2,1,0:T(8,128)(2,1)S(1)} %collective-permute-done.40.rest_7_), channel_id=1, source_target_pairs={{0,12},{1,13},{2,14},{3,15},{4,0},{5,1},{6,2},{7,3},{8,4},{9,5},{1... | collective-permute-start | bytes 1572872 | tf_op jit(solution)/shard_map/ppermute | solution.py:43
  174.5 4.9 %collective-permute-done.47.rest_13_ = bf16[8,128,256]{2,1,0:T(8,128)(2,1)S(1)} collective-permute-done((bf16[8,128,256]{2,1,0:T(8,128)(2,1)S(1)}, bf16[8,128,256]{2,1,0:T(8,128)(2,1)S(1)}, u32[]{:S(2)}, u32[]{:S(2)}) %collective-permute-start.47) | collective-permute-done | bytes 524320 | tf_op jit(solution)/shard_map/ppermute | solution.py:43
  179.4 3.1 %collective-permute-done.41.rest_5_ = bf16[8,128,256]{2,1,0:T(8,128)(2,1)S(1)} collective-permute-done((bf16[8,128,256]{2,1,0:T(8,128)(2,1)S(1)}, bf16[8,128,256]{2,1,0:T(8,128)(2,1)S(1)}, u32[]{:S(2)}, u32[]{:S(2)}) %collective-permute-start.41) | collective-permute-done | bytes 524320 | tf_op jit(solution)/shard_map/ppermute | solution.py:43
  182.5 5.1 %collective-permute-done.44.rest_12_ = bf16[8,128,256]{2,1,0:T(8,128)(2,1)S(1)} collective-permute-done((bf16[8,128,256]{2,1,0:T(8,128)(2,1)S(1)}, bf16[8,128,256]{2,1,0:T(8,128)(2,1)S(1)}, u32[]{:S(2)}, u32[]{:S(2)}) %collective-permute-start.44) | collective-permute-done | bytes 524320 | tf_op jit(solution)/shard_map/ppermute | solution.py:43
  187.6 6.3 %decode.1 = bf16[227,3072]{1,0:T(8,128)(2,1)} custom-call(s32[3,24]{1,0:T(4,128)S(1)} %bitcast.11, bf16[227,3072]{1,0:T(8,128)(2,1)S(1)} %bitcast.7, bf16[24,3,128,128]{3,2,1,0:T(8,128)(2,1)S(1)} %copy-done.3, bf16[227,512]{1,0:T(8,128)(2,1)S(1)} %bitcast.8, bf16[8,128,256]{2,1,0:T(8,128)(2,1)S(1)} %constant_dynamic-update-slice_fusion.rest_0_, ...), custom_call_target="tpu_custom_call" | custom-call | tf_op jit(solution)/shard_map/decode/pallas_call | solution.py:356
  (118 shorter events, 61.0 us)
Async XLA Ops:
  10.4 15.0 %collective-permute-start.3 = (bf16[8,128,256]{2,1,0:T(8,128)(2,1)S(1)}, bf16[8,128,256]{2,1,0:T(8,128)(2,1)S(1)}, u32[]{:S(2)}, u32[]{:S(2)}) collective-permute-start(bf16[8,128,256]{2,1,0:T(8,128)(2,1)S(1)} %get-tuple-element.73), channel_id=1, source_target_pairs={{0,4},{1,5},{2,6},{3,7},{4,8},{5,9},{6,10},{7,11},{8,12},{9,13},{1... | collective-permute-start | bytes 1572872 | tf_op jit(solution)/shard_map/ppermute | solution.py:43
  12.1 15.7 %collective-permute-start = (bf16[8,128,256]{2,1,0:T(8,128)(2,1)S(1)}, bf16[8,128,256]{2,1,0:T(8,128)(2,1)S(1)}, u32[]{:S(2)}, u32[]{:S(2)}) collective-permute-start(bf16[8,128,256]{2,1,0:T(8,128)(2,1)S(1)} %get-tuple-element.69), channel_id=1, source_target_pairs={{0,1},{1,2},{2,3},{3,0},{4,5},{5,6},{6,7},{7,4},{8,9},{9,10},{10,1... | collective-permute-start | bytes 1572872 | tf_op jit(solution)/shard_map/ppermute | solution.py:43
  14.0 14.1 %collective-permute-start.7 = (bf16[8,128,256]{2,1,0:T(8,128)(2,1)S(1)}, bf16[8,128,256]{2,1,0:T(8,128)(2,1)S(1)}, u32[]{:S(2)}, u32[]{:S(2)}) collective-permute-start(bf16[8,128,256]{2,1,0:T(8,128)(2,1)S(1)} %get-tuple-element.79), channel_id=1, source_target_pairs={{0,12},{1,13},{2,14},{3,15},{4,0},{5,1},{6,2},{7,3},{8,4},{9,5},{1... | collective-permute-start | bytes 1572872 | tf_op jit(solution)/shard_map/ppermute | solution.py:43
  15.7 15.3 %collective-permute-start.2 = (bf16[8,128,256]{2,1,0:T(8,128)(2,1)S(1)}, bf16[8,128,256]{2,1,0:T(8,128)(2,1)S(1)}, u32[]{:S(2)}, u32[]{:S(2)}) collective-permute-start(bf16[8,128,256]{2,1,0:T(8,128)(2,1)S(1)} %get-tuple-element.71), channel_id=1, source_target_pairs={{0,3},{1,0},{2,1},{3,2},{4,7},{5,4},{6,5},{7,6},{8,11},{9,8},{10,9... | collective-permute-start | bytes 1572872 | tf_op jit(solution)/shard_map/ppermute | solution.py:43
  25.6 14.1 %collective-permute-start.4 = (bf16[8,128,256]{2,1,0:T(8,128)(2,1)S(1)}, bf16[8,128,256]{2,1,0:T(8,128)(2,1)S(1)}, u32[]{:S(2)}, u32[]{:S(2)}) collective-permute-start(bf16[8,128,256]{2,1,0:T(8,128)(2,1)S(1)} %add_convert_fusion.2), channel_id=1, source_target_pairs={{0,4},{1,5},{2,6},{3,7},{4,8},{5,9},{6,10},{7,11},{8,12},{9,13},{1... | collective-permute-start | bytes 1572872 | tf_op jit(solution)/shard_map/ppermute | solution.py:43
  27.9 14.1 %collective-permute-start.1 = (bf16[8,128,256]{2,1,0:T(8,128)(2,1)S(1)}, bf16[8,128,256]{2,1,0:T(8,128)(2,1)S(1)}, u32[]{:S(2)}, u32[]{:S(2)}) collective-permute-start(bf16[8,128,256]{2,1,0:T(8,128)(2,1)S(1)} %add_convert_fusion.3), channel_id=1, source_target_pairs={{0,1},{1,2},{2,3},{3,0},{4,5},{5,6},{6,7},{7,4},{8,9},{9,10},{10,1... | collective-permute-start | bytes 1572872 | tf_op jit(solution)/shard_map/ppermute | solution.py:43
  28.1 15.7 %collective-permute-start.8 = (bf16[8,128,256]{2,1,0:T(8,128)(2,1)S(1)}, bf16[8,128,256]{2,1,0:T(8,128)(2,1)S(1)}, u32[]{:S(2)}, u32[]{:S(2)}) collective-permute-start(bf16[8,128,256]{2,1,0:T(8,128)(2,1)S(1)} %get-tuple-element.80), channel_id=1, source_target_pairs={{0,12},{1,13},{2,14},{3,15},{4,0},{5,1},{6,2},{7,3},{8,4},{9,5},{1... | collective-permute-start | bytes 1572872 | tf_op jit(solution)/shard_map/ppermute | solution.py:43
  31.0 20.1 %collective-permute-start.13 = (bf16[8,128,256]{2,1,0:T(8,128)(2,1)S(1)}, bf16[8,128,256]{2,1,0:T(8,128)(2,1)S(1)}, u32[]{:S(2)}, u32[]{:S(2)}) collective-permute-start(bf16[8,128,256]{2,1,0:T(8,128)(2,1)S(1)} %get-tuple-element.89), channel_id=1, source_target_pairs={{0,3},{1,0},{2,1},{3,2},{4,7},{5,4},{6,5},{7,6},{8,11},{9,8},{10,9... | collective-permute-start | bytes 1572872 | tf_op jit(solution)/shard_map/ppermute | solution.py:43
  43.9 19.4 %collective-permute-start.9 = (bf16[8,128,256]{2,1,0:T(8,128)(2,1)S(1)}, bf16[8,128,256]{2,1,0:T(8,128)(2,1)S(1)}, u32[]{:S(2)}, u32[]{:S(2)}) collective-permute-start(bf16[8,128,256]{2,1,0:T(8,128)(2,1)S(1)} %add_convert_fusion.1), channel_id=1, source_target_pairs={{0,12},{1,13},{2,14},{3,15},{4,0},{5,1},{6,2},{7,3},{8,4},{9,5},{1... | collective-permute-start | bytes 1572872 | tf_op jit(solution)/shard_map/ppermute | solution.py:43
  49.6 12.1 %collective-permute-start.11 = (bf16[8,128,256]{2,1,0:T(8,128)(2,1)S(1)}, bf16[8,128,256]{2,1,0:T(8,128)(2,1)S(1)}, u32[]{:S(2)}, u32[]{:S(2)}) collective-permute-start(bf16[8,128,256]{2,1,0:T(8,128)(2,1)S(1)} %get-tuple-element.85), channel_id=1, source_target_pairs={{0,1},{1,2},{2,3},{3,0},{4,5},{5,6},{6,7},{7,4},{8,9},{9,10},{10,1... | collective-permute-start | bytes 1572872 | tf_op jit(solution)/shard_map/ppermute | solution.py:43
  49.8 12.2 %collective-permute-start.6 = (bf16[8,128,256]{2,1,0:T(8,128)(2,1)S(1)}, bf16[8,128,256]{2,1,0:T(8,128)(2,1)S(1)}, u32[]{:S(2)}, u32[]{:S(2)}) collective-permute-start(bf16[8,128,256]{2,1,0:T(8,128)(2,1)S(1)} %get-tuple-element.76), channel_id=1, source_target_pairs={{0,4},{1,5},{2,6},{3,7},{4,8},{5,9},{6,10},{7,11},{8,12},{9,13},{1... | collective-permute-start | bytes 1572872 | tf_op jit(solution)/shard_map/ppermute | solution.py:43
  51.3 12.1 %collective-permute-start.14 = (bf16[8,128,256]{2,1,0:T(8,128)(2,1)S(1)}, bf16[8,128,256]{2,1,0:T(8,128)(2,1)S(1)}, u32[]{:S(2)}, u32[]{:S(2)}) collective-permute-start(bf16[8,128,256]{2,1,0:T(8,128)(2,1)S(1)} %add_convert_fusion), channel_id=1, source_target_pairs={{0,3},{1,0},{2,1},{3,2},{4,7},{5,4},{6,5},{7,6},{8,11},{9,8},{10,9... | collective-permute-start | bytes 1572872 | tf_op jit(solution)/shard_map/ppermute | solution.py:43
  77.7 12.8 %collective-permute-start.20 = (bf16[2,128,512]{2,1,0:T(8,128)(2,1)S(1)}, bf16[2,128,512]{2,1,0:T(8,128)(2,1)S(1)}, u32[]{:S(2)}, u32[]{:S(2)}) collective-permute-start(bf16[2,128,512]{2,1,0:T(8,128)(2,1)S(1)} %get-tuple-element.98.rest_4_), channel_id=1, source_target_pairs={{0,16},{16,32},{32,48},{48,64},{64,80},{80,96},{96,112},{1,17},{17... | collective-permute-start | bytes 786440 | tf_op jit(solution)/shard_map/ppermute | solution.py:285
  79.6 10.9 %collective-permute-start.21 = (bf16[2,128,512]{2,1,0:T(8,128)(2,1)S(1)}, bf16[2,128,512]{2,1,0:T(8,128)(2,1)S(1)}, u32[]{:S(2)}, u32[]{:S(2)}) collective-permute-start(bf16[2,128,512]{2,1,0:T(8,128)(2,1)S(1)} %get-tuple-element.99.rest_3_), channel_id=1, source_target_pairs={{16,0},{32,16},{48,32},{64,48},{80,64},{96,80},{112,96},{17,1},{33... | collective-permute-start | bytes 786440 | tf_op jit(solution)/shard_map/ppermute | solution.py:286
  96.3 10.8 %collective-permute-start.24 = (bf16[2,128,512]{2,1,0:T(8,128)(2,1)S(1)}, bf16[2,128,512]{2,1,0:T(8,128)(2,1)S(1)}, u32[]{:S(2)}, u32[]{:S(2)}) collective-permute-start(bf16[2,128,512]{2,1,0:T(8,128)(2,1)S(1)} %get-tuple-element.101), channel_id=1, source_target_pairs={{0,1},{1,2},{2,3},{3,4},{4,5},{5,6},{6,7},{7,8},{8,9},{9,10},{10,1... | collective-permute-start | bytes 786440 | tf_op jit(solution)/shard_map/ppermute | solution.py:283
  100.2 10.3 %collective-permute-start.25 = (bf16[2,128,512]{2,1,0:T(8,128)(2,1)S(1)}, bf16[2,128,512]{2,1,0:T(8,128)(2,1)S(1)}, u32[]{:S(2)}, u32[]{:S(2)}) collective-permute-start(bf16[2,128,512]{2,1,0:T(8,128)(2,1)S(1)} %get-tuple-element.102), channel_id=1, source_target_pairs={{1,0},{2,1},{3,2},{4,3},{5,4},{6,5},{7,6},{8,7},{9,8},{10,9},{11,1... | collective-permute-start | bytes 786440 | tf_op jit(solution)/shard_map/ppermute | solution.py:284
  101.5 14.7 %collective-permute-start.26 = (bf16[2,128,512]{2,1,0:T(8,128)(2,1)S(1)}, bf16[2,128,512]{2,1,0:T(8,128)(2,1)S(1)}, u32[]{:S(2)}, u32[]{:S(2)}) collective-permute-start(bf16[2,128,512]{2,1,0:T(8,128)(2,1)S(1)} %get-tuple-element.103.rest_4_), channel_id=1, source_target_pairs={{0,16},{16,32},{32,48},{48,64},{64,80},{80,96},{96,112},{1,17},{17... | collective-permute-start | bytes 786440 | tf_op jit(solution)/shard_map/ppermute | solution.py:285
  104.9 11.3 %collective-permute-start.27 = (bf16[2,128,512]{2,1,0:T(8,128)(2,1)S(1)}, bf16[2,128,512]{2,1,0:T(8,128)(2,1)S(1)}, u32[]{:S(2)}, u32[]{:S(2)}) collective-permute-start(bf16[2,128,512]{2,1,0:T(8,128)(2,1)S(1)} %get-tuple-element.104.rest_3_), channel_id=1, source_target_pairs={{16,0},{32,16},{48,32},{64,48},{80,64},{96,80},{112,96},{17,1},{33... | collective-permute-start | bytes 786440 | tf_op jit(solution)/shard_map/ppermute | solution.py:286
  122.1 12.4 %collective-permute-start.30 = (bf16[4,128,256]{2,1,0:T(8,128)(2,1)S(1)}, bf16[4,128,256]{2,1,0:T(8,128)(2,1)S(1)}, u32[]{:S(2)}, u32[]{:S(2)}) collective-permute-start(bf16[4,128,256]{2,1,0:T(8,128)(2,1)S(1)} %get-tuple-element.105), channel_id=1, source_target_pairs={{0,1},{1,2},{2,3},{3,0},{4,5},{5,6},{6,7},{7,4},{8,9},{9,10},{10,1... | collective-permute-start | bytes 786440 | tf_op jit(solution)/shard_map/ppermute | solution.py:43
  134.4 10.3 %collective-permute-start.34 = (bf16[4,128,256]{2,1,0:T(8,128)(2,1)S(1)}, bf16[4,128,256]{2,1,0:T(8,128)(2,1)S(1)}, u32[]{:S(2)}, u32[]{:S(2)}) collective-permute-start(bf16[4,128,256]{2,1,0:T(8,128)(2,1)S(1)} %collective-permute-done.33), channel_id=1, source_target_pairs={{0,4},{1,5},{2,6},{3,7},{4,8},{5,9},{6,10},{7,11},{8,12},{9,13},{1... | collective-permute-start | bytes 786440 | tf_op jit(solution)/shard_map/ppermute | solution.py:43
  135.1 15.6 %collective-permute-start.45 = (bf16[8,128,256]{2,1,0:T(8,128)(2,1)S(1)}, bf16[8,128,256]{2,1,0:T(8,128)(2,1)S(1)}, u32[]{:S(2)}, u32[]{:S(2)}) collective-permute-start(bf16[8,128,256]{2,1,0:T(8,128)(2,1)S(1)} %constant_dynamic-update-slice_fusion.4.rest_8_), channel_id=1, source_target_pairs={{0,3},{1,0},{2,1},{3,2},{4,7},{5,4},{6,5},{7,6},{8,11},{9,8},{10,9... | collective-permute-start | bytes 1572872 | tf_op jit(solution)/shard_map/ppermute | solution.py:43
  138.8 15.6 %collective-permute-start.39 = (bf16[8,128,256]{2,1,0:T(8,128)(2,1)S(1)}, bf16[8,128,256]{2,1,0:T(8,128)(2,1)S(1)}, u32[]{:S(2)}, u32[]{:S(2)}) collective-permute-start(bf16[8,128,256]{2,1,0:T(8,128)(2,1)S(1)} %constant_dynamic-update-slice_fusion.rest_0_), channel_id=1, source_target_pairs={{0,12},{1,13},{2,14},{3,15},{4,0},{5,1},{6,2},{7,3},{8,4},{9,5},{1... | collective-permute-start | bytes 1572872 | tf_op jit(solution)/shard_map/ppermute | solution.py:43
  144.7 15.2 %collective-permute-start.42 = (bf16[8,128,256]{2,1,0:T(8,128)(2,1)S(1)}, bf16[8,128,256]{2,1,0:T(8,128)(2,1)S(1)}, u32[]{:S(2)}, u32[]{:S(2)}) collective-permute-start(bf16[8,128,256]{2,1,0:T(8,128)(2,1)S(1)} %constant_dynamic-update-slice_fusion.4.rest_8_), channel_id=1, source_target_pairs={{0,1},{1,2},{2,3},{3,0},{4,5},{5,6},{6,7},{7,4},{8,9},{9,10},{10,1... | collective-permute-start | bytes 1572872 | tf_op jit(solution)/shard_map/ppermute | solution.py:43
  144.7 15.2 %collective-permute-start.35 = (bf16[8,128,256]{2,1,0:T(8,128)(2,1)S(1)}, bf16[8,128,256]{2,1,0:T(8,128)(2,1)S(1)}, u32[]{:S(2)}, u32[]{:S(2)}) collective-permute-start(bf16[8,128,256]{2,1,0:T(8,128)(2,1)S(1)} %constant_dynamic-update-slice_fusion.rest_0_), channel_id=1, source_target_pairs={{0,4},{1,5},{2,6},{3,7},{4,8},{5,9},{6,10},{7,11},{8,12},{9,13},{1... | collective-permute-start | bytes 1572872 | tf_op jit(solution)/shard_map/ppermute | solution.py:43
  150.6 14.8 %collective-permute-start.46 = (bf16[8,128,256]{2,1,0:T(8,128)(2,1)S(1)}, bf16[8,128,256]{2,1,0:T(8,128)(2,1)S(1)}, u32[]{:S(2)}, u32[]{:S(2)}) collective-permute-start(bf16[8,128,256]{2,1,0:T(8,128)(2,1)S(1)} %constant_dynamic-update-slice_fusion.6.rest_9_), channel_id=1, source_target_pairs={{0,3},{1,0},{2,1},{3,2},{4,7},{5,4},{6,5},{7,6},{8,11},{9,8},{10,9... | collective-permute-start | bytes 1572872 | tf_op jit(solution)/shard_map/ppermute | solution.py:43
  154.3 14.8 %collective-permute-start.40 = (bf16[8,128,256]{2,1,0:T(8,128)(2,1)S(1)}, bf16[8,128,256]{2,1,0:T(8,128)(2,1)S(1)}, u32[]{:S(2)}, u32[]{:S(2)}) collective-permute-start(bf16[8,128,256]{2,1,0:T(8,128)(2,1)S(1)} %constant_dynamic-update-slice_fusion.2.rest_1_), channel_id=1, source_target_pairs={{0,12},{1,13},{2,14},{3,15},{4,0},{5,1},{6,2},{7,3},{8,4},{9,5},{1... | collective-permute-start | bytes 1572872 | tf_op jit(solution)/shard_map/ppermute | solution.py:43
  159.9 14.3 %collective-permute-start.43 = (bf16[8,128,256]{2,1,0:T(8,128)(2,1)S(1)}, bf16[8,128,256]{2,1,0:T(8,128)(2,1)S(1)}, u32[]{:S(2)}, u32[]{:S(2)}) collective-permute-start(bf16[8,128,256]{2,1,0:T(8,128)(2,1)S(1)} %constant_dynamic-update-slice_fusion.6.rest_9_), channel_id=1, source_target_pairs={{0,1},{1,2},{2,3},{3,0},{4,5},{5,6},{6,7},{7,4},{8,9},{9,10},{10,1... | collective-permute-start | bytes 1572872 | tf_op jit(solution)/shard_map/ppermute | solution.py:43
  159.9 14.3 %collective-permute-start.36 = (bf16[8,128,256]{2,1,0:T(8,128)(2,1)S(1)}, bf16[8,128,256]{2,1,0:T(8,128)(2,1)S(1)}, u32[]{:S(2)}, u32[]{:S(2)}) collective-permute-start(bf16[8,128,256]{2,1,0:T(8,128)(2,1)S(1)} %constant_dynamic-update-slice_fusion.2.rest_1_), channel_id=1, source_target_pairs={{0,4},{1,5},{2,6},{3,7},{4,8},{5,9},{6,10},{7,11},{8,12},{9,13},{1... | collective-permute-start | bytes 1572872 | tf_op jit(solution)/shard_map/ppermute | solution.py:43
  165.5 13.9 %collective-permute-start.47 = (bf16[8,128,256]{2,1,0:T(8,128)(2,1)S(1)}, bf16[8,128,256]{2,1,0:T(8,128)(2,1)S(1)}, u32[]{:S(2)}, u32[]{:S(2)}) collective-permute-start(bf16[8,128,256]{2,1,0:T(8,128)(2,1)S(1)} %collective-permute-done.46.rest_15_), channel_id=1, source_target_pairs={{0,3},{1,0},{2,1},{3,2},{4,7},{5,4},{6,5},{7,6},{8,11},{9,8},{10,9... | collective-permute-start | bytes 1572872 | tf_op jit(solution)/shard_map/ppermute | solution.py:43
  169.2 13.3 %collective-permute-start.41 = (bf16[8,128,256]{2,1,0:T(8,128)(2,1)S(1)}, bf16[8,128,256]{2,1,0:T(8,128)(2,1)S(1)}, u32[]{:S(2)}, u32[]{:S(2)}) collective-permute-start(bf16[8,128,256]{2,1,0:T(8,128)(2,1)S(1)} %collective-permute-done.40.rest_7_), channel_id=1, source_target_pairs={{0,12},{1,13},{2,14},{3,15},{4,0},{5,1},{6,2},{7,3},{8,4},{9,5},{1... | collective-permute-start | bytes 1572872 | tf_op jit(solution)/shard_map/ppermute | solution.py:43
  174.2 13.4 %collective-permute-start.44 = (bf16[8,128,256]{2,1,0:T(8,128)(2,1)S(1)}, bf16[8,128,256]{2,1,0:T(8,128)(2,1)S(1)}, u32[]{:S(2)}, u32[]{:S(2)}) collective-permute-start(bf16[8,128,256]{2,1,0:T(8,128)(2,1)S(1)} %collective-permute-done.42.rest_10_), channel_id=1, source_target_pairs={{0,1},{1,2},{2,3},{3,0},{4,5},{5,6},{6,7},{7,4},{8,9},{9,10},{10,1... | collective-permute-start | bytes 1572872 | tf_op jit(solution)/shard_map/ppermute | solution.py:43
  174.2 13.4 %collective-permute-start.37 = (bf16[8,128,256]{2,1,0:T(8,128)(2,1)S(1)}, bf16[8,128,256]{2,1,0:T(8,128)(2,1)S(1)}, u32[]{:S(2)}, u32[]{:S(2)}) collective-permute-start(bf16[8,128,256]{2,1,0:T(8,128)(2,1)S(1)} %collective-permute-done.35.rest_2_), channel_id=1, source_target_pairs={{0,4},{1,5},{2,6},{3,7},{4,8},{5,9},{6,10},{7,11},{8,12},{9,13},{1... | collective-permute-start | bytes 1572872 | tf_op jit(solution)/shard_map/ppermute | solution.py:43
  (27 other events, 621.5 us)

commit v3 on v2

--- a/solution.py
+++ b/solution.py
@@ -68,39 +68,47 @@
 
 
 def encode_kernel(dest_ref, x_hbm, embed_hbm, send_hbm, edges_hbm, out_0, out_1, x, embed, send, edges, sems):
-    copies = [
-        pltpu.make_async_copy(embed_hbm, embed, sems.at[0]),
-        pltpu.make_async_copy(x_hbm.at[:, pl.ds(0, CHUNK)], x.at[0], sems.at[1]),
-        pltpu.make_async_copy(send_hbm, send, sems.at[2]),
-        pltpu.make_async_copy(edges_hbm.at[pl.ds(0, CHUNK_BLOCKS)], edges.at[0], sems.at[3]),
-    ]
-    for c in range(1, CHUNKS):
-        copies += [
-            pltpu.make_async_copy(x_hbm.at[:, pl.ds(c * CHUNK, CHUNK)], x.at[c], sems.at[2 * c + 2]),
+    def inputs(c):
+        return (
+            pltpu.make_async_copy(
+                x_hbm.at[:, pl.ds(pl.multiple_of(c * CHUNK, CHUNK), CHUNK)], x.at[c], sems.at[2 * c + 2]
+            ),
             pltpu.make_async_copy(
                 edges_hbm.at[pl.ds(c * CHUNK_BLOCKS, CHUNK_BLOCKS)], edges.at[c], sems.at[2 * c + 3]
             ),
-        ]
-    for copy in copies:
+        )
+
+    weights = (
+        pltpu.make_async_copy(embed_hbm, embed, sems.at[0]),
+        pltpu.make_async_copy(send_hbm, send, sems.at[1]),
+    )
+    for copy in weights + inputs(0):
         copy.start()
-    out_0[...] = jnp.zeros_like(out_0)
-    out_1[...] = jnp.zeros_like(out_1)
+
+    @pl.loop(1, CHUNKS)
+    def _(c):
+        for copy in inputs(c):
+            copy.start()
+
+    @pl.loop(0, 64)
+    def _(n):
+        out_0[n] = jnp.zeros((NB, HALF), BF16)
+        out_1[n] = jnp.zeros((NB, HALF), BF16)
+
     me = lax.axis_index("mesh")
     my_y, my_z = me // SIDE, me % SIDE
-    for c in range(CHUNKS):
-        if c == 0:
-            copies[0].wait()
-            copies[1].wait()
-        else:
-            copies[2 * c + 2].wait()
+    for copy in weights:
+        copy.wait()
+
+    @pl.loop(0, CHUNKS)
+    def _(c):
+        for copy in inputs(c):
+            copy.wait()
         latent = silu(dot_t(x[c], embed[...])).astype(BF16)
-        if c == 0:
-            copies[2].wait()
         proj = dot(latent, send[...]).astype(BF16)
-        copies[2 * c + 3].wait()
         for b in range(CHUNK_BLOCKS):
-            weights = jnp.concatenate([edges[c, b, j] for j in range(3)], 1)
-            message = dot_t(weights, proj[b * NB : (b + 1) * NB])
+            both = jnp.concatenate([edges[c, b, j] for j in range(3)], 1)
+            message = dot_t(both, proj[b * NB : (b + 1) * NB])
             for j in range(3):
                 y, z, local = place(dest_ref[j, c * CHUNK_BLOCKS + b])
                 dy, dz = (y - my_y) & 3, (z - my_z) & 3
@@ -203,17 +211,25 @@
     put_sent(dot(mesh, message_ref[0]).astype(BF16), sent_refs)
 
 
+def parity(axis):
+    return lax.rem(lax.axis_index(axis), 2)
+
+
 def put_sent(sent, refs):
     sent = sent.reshape(2, 2, NB, D)
-    for n in range(2):
-        refs[n][...] = sent[n]
-        refs[2 + n][...] = sent[:, n]
+    refs[0][...] = sent
+    for at, axis in ((1, "grid"), (3, "mesh")):
+        first, last = (sent[n] if axis == "grid" else sent[:, n] for n in range(2))
+        even = parity(axis) == 0
+        refs[at][...] = jnp.where(even, last, first)
+        refs[at + 1][...] = jnp.where(even, first, last)
 
 
 def sent_shapes():
-    return [jax.ShapeDtypeStruct((OWN * NB, D), BF16)] + [
-        jax.ShapeDtypeStruct((2, NB, D), BF16)
-    ] * 4
+    return [
+        jax.ShapeDtypeStruct((OWN * NB, D), BF16),
+        jax.ShapeDtypeStruct((2, 2, NB, D), BF16),
+    ] + [jax.ShapeDtypeStruct((2, NB, D), BF16)] * 4
 
 
 def mesh_start(terms, encode_weight, message_weight):
@@ -226,16 +242,19 @@
 
 
 def step_kernel(layer, codes_ref, count_ref, mesh_ref, *rest):
-    band, (couplings_ref, node_ref, next_ref), rest = rest[:8], rest[8:11], rest[11:]
+    band, (couplings_ref, node_ref, next_ref), rest = rest[:7], rest[7:10], rest[10:]
     outs, (pad, normed) = rest[:-2], rest[-2:]
-    left, right, above, rows_0, rows_1, below, corners_above, corners_below = band
-    for row, middle in enumerate((above, rows_0, rows_1, below)):
-        pad[4 * row + 1 : 4 * row + 3] = middle[...]
+    own, col_a, col_b, row_a, row_b, corners_a, corners_b = band
+    col = 3 - 3 * parity("mesh")
+    row = 3 - 3 * parity("grid")
     for r in range(2):
-        pad[4 * r + 4] = left[r]
-        pad[4 * r + 7] = right[r]
-        pad[3 * r] = corners_above[r]
-        pad[12 + 3 * r] = corners_below[r]
+        pad[4 * r + 5 : 4 * r + 7] = own[r]
+        pad[4 * r + 4 + col] = col_a[r]
+        pad[4 * r + 7 - col] = col_b[r]
+    for at, middle, corners in ((row, row_a, corners_a), (3 - row, row_b, corners_b)):
+        pad[pl.ds(4 * at + 1, 2)] = middle[...]
+        pad[4 * at + col] = corners[0]
+        pad[4 * at + 3 - col] = corners[1]
     for r in range(2):
         for c in range(2):
             near, weights = [], []
@@ -268,7 +287,7 @@
     vmem = pl.BlockSpec(memory_space=pltpu.VMEM)
     return pl.pallas_call(
         functools.partial(step_kernel, layer),
-        in_specs=[smem, smem] + [vmem] * 12,
+        in_specs=[smem, smem] + [vmem] * 11,
         out_shape=out_shape,
         scratch_shapes=[pltpu.VMEM((16, NB, D), BF16), pltpu.VMEM((OWN * NB, D), BF16)],
         compiler_params=params(16),
@@ -276,18 +295,21 @@
     )(codes, count, mesh, *band, couplings, node_weight, next_weight)
 
 
-def band_of(row_0, row_1, first, last):
-    size, length = lax.axis_size("mesh"), lax.axis_size("grid")
-    ahead = lambda n: [(i, i + 1) for i in range(n - 1)]
-    back = lambda n: [(i + 1, i) for i in range(n - 1)]
-    left = lax.ppermute(last, "mesh", ahead(size))
-    right = lax.ppermute(first, "mesh", back(size))
-    above = lax.ppermute(row_1, "grid", ahead(length))
-    below = lax.ppermute(row_0, "grid", back(length))
-    corners = [jnp.concatenate([left[r : r + 1], right[r : r + 1]], 0) for r in range(2)]
-    corners_above = lax.ppermute(corners[1], "grid", ahead(length))
-    corners_below = lax.ppermute(corners[0], "grid", back(length))
-    return left, right, above, row_0, row_1, below, corners_above, corners_below
+def trade(value, axis, odd):
+    size = lax.axis_size(axis)
+    pairs = [(i, i + 1) for i in range(odd, size - 1, 2)]
+    return lax.ppermute(value, axis, pairs + [(b, a) for a, b in pairs])
+
+
+def band_of(own, row_a, row_b, col_a, col_b):
+    col_a, col_b = trade(col_a, "mesh", 0), trade(col_b, "mesh", 1)
+    row_a, row_b = trade(row_a, "grid", 0), trade(row_b, "grid", 1)
+    corners = []
+    for odd in range(2):
+        row = 1 - (parity("grid") + odd) % 2
+        ends = [lax.dynamic_slice_in_dim(value, row, 1, 0) for value in (col_a, col_b)]
+        corners.append(trade(jnp.concatenate(ends, 0), "grid", odd))
+    return own, col_a, col_b, row_a, row_b, *corners
 
 
 BLOCKS = 8

time: 195 us -> 191 us (0.979)
  the two profiles are of different devices: /device:TPU:2 before, /device:TPU:0 now
where the time goes in v3:
time: 191 us; the launch traced here: 190 us
  waiting for transfers between devices  81.9 us (43%)
  starting transfers between devices  80.5 us (42%)
  Pallas kernels  20.1 us (11%)
  local copies, waits for them, and re-layouts  5.99 us (3%)
    ppermute x36, waiting for transfers between devices, shift(): return lax.ppermute(value, 'mesh', pairs)  73.6 us
    ppermute x36, starting transfers between devices, shift(): return lax.ppermute(value, 'mesh', pairs)  59.2 us
    ppermute x12, starting transfers between devices, trade(): return lax.ppermute(value, axis, pairs + [(b, a) for a, b in pairs])  21.3 us
    ppermute x12, waiting for transfers between devices, trade(): return lax.ppermute(value, axis, pairs + [(b, a) for a, b in pairs])  8.3 us
    pallas_call x1, Pallas kernels, encode(): pl.pallas_call(encode_kernel, in_specs=[pl.BlockSpec(memory_space=pltpu.S...  8.23 us
    pallas_call x1, Pallas kernels, decode(): pl.pallas_call(decode_kernel, grid_spec=pltpu.PrefetchScalarGridSpec(num_...  6.26 us
    unnamed x36, local copies, waits for them, and re-layouts  4.51 us
    pallas_call x2, Pallas kernels, mesh_step(): pl.pallas_call(functools.partial(step_kernel, layer), in_specs=[smem, sme...  3.88 us
  transfers between devices with their start and end apart: 48, of which 25 were waited for; matrix products, arithmetic and copies ran while one was open for 1% of the time, Pallas kernels for 0%

profile of v3, /device:TPU:0, one launch (start us, length us, event | category | flops | bytes accessed | tf_op | source)
XLA Modules:
  0.0 190.4 jit_solution(6852297268742990711)
XLA Ops:
  0.0 8.2 %encode.1 = (bf16[64,128,256]{2,1,0:T(8,128)(2,1)S(1)}, bf16[64,128,256]{2,1,0:T(8,128)(2,1)S(1)}) custom-call(s32[3,24]{1,0:T(4,128)} %bitcast.12, bf16[227,3072]{1,0:T(8,128)(2,1)} %bitcast.6, bf16[227,512]{1,0:T(8,128)(2,1)} %embed_hbm.1, bf16[512,512]{1,0:T(8,128)(2,1)} %send_hbm.1, bf16[24,3,128,128]{3,2,1,0:T(8,128)(2,1)} %edges_hbm.1), custom_call_target="tpu_custom_call" | custom-call | tf_op jit(solution)/shard_map/encode/pallas_call | solution.py:129
  13.2 2.1 %collective-permute-start.2 = (bf16[8,128,256]{2,1,0:T(8,128)(2,1)S(1)}, bf16[8,128,256]{2,1,0:T(8,128)(2,1)S(1)}, u32[]{:S(2)}, u32[]{:S(2)}) collective-permute-start(bf16[8,128,256]{2,1,0:T(8,128)(2,1)S(1)} %get-tuple-element.73), channel_id=1, source_target_pairs={{0,3},{1,0},{2,1},{3,2},{4,7},{5,4},{6,5},{7,6},{8,11},{9,8},{10,9... | collective-permute-start | bytes 1572872 | tf_op jit(solution)/shard_map/ppermute | solution.py:43
  17.0 7.7 %collective-permute-done.3 = bf16[8,128,256]{2,1,0:T(8,128)(2,1)S(1)} collective-permute-done((bf16[8,128,256]{2,1,0:T(8,128)(2,1)S(1)}, bf16[8,128,256]{2,1,0:T(8,128)(2,1)S(1)}, u32[]{:S(2)}, u32[]{:S(2)}) %collective-permute-start.3) | collective-permute-done | bytes 524320 | tf_op jit(solution)/shard_map/ppermute | solution.py:43
  27.3 3.1 %collective-permute-start.13 = (bf16[8,128,256]{2,1,0:T(8,128)(2,1)S(1)}, bf16[8,128,256]{2,1,0:T(8,128)(2,1)S(1)}, u32[]{:S(2)}, u32[]{:S(2)}) collective-permute-start(bf16[8,128,256]{2,1,0:T(8,128)(2,1)S(1)} %get-tuple-element.91), channel_id=1, source_target_pairs={{0,3},{1,0},{2,1},{3,2},{4,7},{5,4},{6,5},{7,6},{8,11},{9,8},{10,9... | collective-permute-start | bytes 1572872 | tf_op jit(solution)/shard_map/ppermute | solution.py:43
  32.4 6.6 %collective-permute-done.4 = bf16[8,128,256]{2,1,0:T(8,128)(2,1)S(1)} collective-permute-done((bf16[8,128,256]{2,1,0:T(8,128)(2,1)S(1)}, bf16[8,128,256]{2,1,0:T(8,128)(2,1)S(1)}, u32[]{:S(2)}, u32[]{:S(2)}) %collective-permute-start.4) | collective-permute-done | bytes 524320 | tf_op jit(solution)/shard_map/ppermute | solution.py:43
  39.1 2.0 %collective-permute-done.1 = bf16[8,128,256]{2,1,0:T(8,128)(2,1)S(1)} collective-permute-done((bf16[8,128,256]{2,1,0:T(8,128)(2,1)S(1)}, bf16[8,128,256]{2,1,0:T(8,128)(2,1)S(1)}, u32[]{:S(2)}, u32[]{:S(2)}) %collective-permute-start.1) | collective-permute-done | bytes 524320 | tf_op jit(solution)/shard_map/ppermute | solution.py:43
  41.3 3.3 %collective-permute-start.14 = (bf16[8,128,256]{2,1,0:T(8,128)(2,1)S(1)}, bf16[8,128,256]{2,1,0:T(8,128)(2,1)S(1)}, u32[]{:S(2)}, u32[]{:S(2)}) collective-permute-start(bf16[8,128,256]{2,1,0:T(8,128)(2,1)S(1)} %add_convert_fusion), channel_id=1, source_target_pairs={{0,3},{1,0},{2,1},{3,2},{4,7},{5,4},{6,5},{7,6},{8,11},{9,8},{10,9... | collective-permute-start | bytes 1572872 | tf_op jit(solution)/shard_map/ppermute | solution.py:43
  46.3 2.4 %collective-permute-done.10 = bf16[4,128,256]{2,1,0:T(8,128)(2,1)S(1)} collective-permute-done((bf16[4,128,256]{2,1,0:T(8,128)(2,1)S(1)}, bf16[4,128,256]{2,1,0:T(8,128)(2,1)S(1)}, u32[]{:S(2)}, u32[]{:S(2)}) %collective-permute-start.10) | collective-permute-done | bytes 262176 | tf_op jit(solution)/shard_map/ppermute | solution.py:43
  48.9 2.1 %collective-permute-start.9 = (bf16[8,128,256]{2,1,0:T(8,128)(2,1)S(1)}, bf16[8,128,256]{2,1,0:T(8,128)(2,1)S(1)}, u32[]{:S(2)}, u32[]{:S(2)}) collective-permute-start(bf16[8,128,256]{2,1,0:T(8,128)(2,1)S(1)} %add_convert_fusion.1), channel_id=1, source_target_pairs={{0,12},{1,13},{2,14},{3,15},{4,0},{5,1},{6,2},{7,3},{8,4},{9,5},{1... | collective-permute-start | bytes 1572872 | tf_op jit(solution)/shard_map/ppermute | solution.py:43
  53.7 7.0 %collective-permute-done.11.refs_6_ = bf16[8,128,256]{2,1,0:T(8,128)(2,1)S(1)} collective-permute-done((bf16[8,128,256]{2,1,0:T(8,128)(2,1)S(1)}, bf16[8,128,256]{2,1,0:T(8,128)(2,1)S(1)}, u32[]{:S(2)}, u32[]{:S(2)}) %collective-permute-start.11) | collective-permute-done | bytes 524320 | tf_op jit(solution)/shard_map/ppermute | solution.py:43
  60.8 2.2 %collective-permute-start.17 = (bf16[4,128,256]{2,1,0:T(8,128)(2,1)S(1)}, bf16[4,128,256]{2,1,0:T(8,128)(2,1)S(1)}, u32[]{:S(2)}, u32[]{:S(2)}) collective-permute-start(bf16[4,128,256]{2,1,0:T(8,128)(2,1)S(1)} %add_convert_fusion.4), channel_id=1, source_target_pairs={{0,12},{1,13},{2,14},{3,15},{4,0},{5,1},{6,2},{7,3},{8,4},{9,5},{1... | collective-permute-start | bytes 786440 | tf_op jit(solution)/shard_map/ppermute | solution.py:43
  67.7 4.3 %collective-permute-done.16.refs_8_ = bf16[4,128,256]{2,1,0:T(8,128)(2,1)S(1)} collective-permute-done((bf16[4,128,256]{2,1,0:T(8,128)(2,1)S(1)}, bf16[4,128,256]{2,1,0:T(8,128)(2,1)S(1)}, u32[]{:S(2)}, u32[]{:S(2)}) %collective-permute-start.16) | collective-permute-done | bytes 262176 | tf_op jit(solution)/shard_map/ppermute | solution.py:43
  72.1 2.1 %collective-permute-done.12.refs_3_ = bf16[4,128,256]{2,1,0:T(8,128)(2,1)S(1)} collective-permute-done((bf16[4,128,256]{2,1,0:T(8,128)(2,1)S(1)}, bf16[4,128,256]{2,1,0:T(8,128)(2,1)S(1)}, u32[]{:S(2)}, u32[]{:S(2)}) %collective-permute-start.12) | collective-permute-done | bytes 262176 | tf_op jit(solution)/shard_map/ppermute | solution.py:43
  79.9 4.9 %collective-permute-done.18.rest_1_ = bf16[2,128,512]{2,1,0:T(8,128)(2,1)S(1)} collective-permute-done((bf16[2,128,512]{2,1,0:T(8,128)(2,1)}, bf16[2,128,512]{2,1,0:T(8,128)(2,1)S(1)}, u32[]{:S(2)}, u32[]{:S(2)}) %collective-permute-start.18) | collective-permute-done | bytes 262176 | tf_op jit(solution)/shard_map/ppermute | solution.py:301
  85.7 2.9 %collective-permute-start.22 = (bf16[2,128,512]{2,1,0:T(8,128)(2,1)S(1)}, bf16[2,128,512]{2,1,0:T(8,128)(2,1)S(1)}, u32[]{:S(2)}, u32[]{:S(2)}) collective-permute-start(bf16[2,128,512]{2,1,0:T(8,128)(2,1)S(1)} %pad_maximum_fusion), channel_id=1, source_target_pairs={{0,16},{32,48},{64,80},{96,112},{16,0},{48,32},{80,64},{112,96},{1... | collective-permute-start | bytes 786440 | tf_op jit(solution)/shard_map/ppermute | solution.py:301
  93.9 3.9 %collective-permute-start.24 = (bf16[2,128,512]{2,1,0:T(8,128)(2,1)S(1)}, bf16[2,128,512]{2,1,0:T(8,128)(2,1)S(1)}, u32[]{:S(2)}, u32[]{:S(2)}) collective-permute-start(bf16[2,128,512]{2,1,0:T(8,128)(2,1)S(1)} %get-tuple-element.105), channel_id=1, source_target_pairs={{0,1},{2,3},{4,5},{6,7},{8,9},{10,11},{12,13},{14,15},{1,0},{3,2},... | collective-permute-start | bytes 786440 | tf_op jit(solution)/shard_map/ppermute | solution.py:301
  98.5 2.6 %collective-permute-start.26 = (bf16[2,128,512]{2,1,0:T(8,128)(2,1)S(1)}, bf16[2,128,512]{2,1,0:T(8,128)(2,1)S(1)}, u32[]{:S(2)}, u32[]{:S(2)}) collective-permute-start(bf16[2,128,512]{2,1,0:T(8,128)(2,1)S(1)} %get-tuple-element.107), channel_id=1, source_target_pairs={{0,16},{32,48},{64,80},{96,112},{16,0},{48,32},{80,64},{112,96},{1... | collective-permute-start | bytes 786440 | tf_op jit(solution)/shard_map/ppermute | solution.py:301
  103.6 7.4 %collective-permute-start.28 = (bf16[2,128,512]{2,1,0:T(8,128)(2,1)S(1)}, bf16[2,128,512]{2,1,0:T(8,128)(2,1)S(1)}, u32[]{:S(2)}, u32[]{:S(2)}) collective-permute-start(bf16[2,128,512]{2,1,0:T(8,128)(2,1)S(1)} %pad_maximum_fusion.2), channel_id=1, source_target_pairs={{0,16},{32,48},{64,80},{96,112},{16,0},{48,32},{80,64},{112,96},{1... | collective-permute-start | bytes 786440 | tf_op jit(solution)/shard_map/ppermute | solution.py:301
  114.2 7.5 %collective-permute-start.33 = (bf16[4,128,256]{2,1,0:T(8,128)(2,1)S(1)}, bf16[4,128,256]{2,1,0:T(8,128)(2,1)S(1)}, u32[]{:S(2)}, u32[]{:S(2)}) collective-permute-start(bf16[4,128,256]{2,1,0:T(8,128)(2,1)S(1)} %get-tuple-element.111), channel_id=1, source_target_pairs={{0,4},{1,5},{2,6},{3,7},{4,8},{5,9},{6,10},{7,11},{8,12},{9,13},{1... | collective-permute-start | bytes 786440 | tf_op jit(solution)/shard_map/ppermute | solution.py:43
  121.6 3.2 %collective-permute-start.32 = (bf16[4,128,256]{2,1,0:T(8,128)(2,1)S(1)}, bf16[4,128,256]{2,1,0:T(8,128)(2,1)S(1)}, u32[]{:S(2)}, u32[]{:S(2)}) collective-permute-start(bf16[4,128,256]{2,1,0:T(8,128)(2,1)S(1)} %get-tuple-element.109), channel_id=1, source_target_pairs={{0,3},{1,0},{2,1},{3,2},{4,7},{5,4},{6,5},{7,6},{8,11},{9,8},{10,9... | collective-permute-start | bytes 786440 | tf_op jit(solution)/shard_map/ppermute | solution.py:43
  130.5 3.5 %collective-permute-start.45 = (bf16[8,128,256]{2,1,0:T(8,128)(2,1)S(1)}, bf16[8,128,256]{2,1,0:T(8,128)(2,1)S(1)}, u32[]{:S(2)}, u32[]{:S(2)}) collective-permute-start(bf16[8,128,256]{2,1,0:T(8,128)(2,1)S(1)} %constant_dynamic-update-slice_fusion.4.rest_8_), channel_id=1, source_target_pairs={{0,3},{1,0},{2,1},{3,2},{4,7},{5,4},{6,5},{7,6},{8,11},{9,8},{10,9... | collective-permute-start | bytes 1572872 | tf_op jit(solution)/shard_map/ppermute | solution.py:43
  135.8 4.6 %collective-permute-done.31 = bf16[4,128,256]{2,1,0:T(8,128)(2,1)S(1)} collective-permute-done((bf16[4,128,256]{2,1,0:T(8,128)(2,1)S(1)}, bf16[4,128,256]{2,1,0:T(8,128)(2,1)S(1)}, u32[]{:S(2)}, u32[]{:S(2)}) %collective-permute-start.31) | collective-permute-done | bytes 262176 | tf_op jit(solution)/shard_map/ppermute | solution.py:43
  141.6 4.3 %collective-permute-done.45.rest_14_ = bf16[8,128,256]{2,1,0:T(8,128)(2,1)S(1)} collective-permute-done((bf16[8,128,256]{2,1,0:T(8,128)(2,1)S(1)}, bf16[8,128,256]{2,1,0:T(8,128)(2,1)S(1)}, u32[]{:S(2)}, u32[]{:S(2)}) %collective-permute-start.45) | collective-permute-done | bytes 524320 | tf_op jit(solution)/shard_map/ppermute | solution.py:43
  145.9 3.7 %collective-permute-start.46 = (bf16[8,128,256]{2,1,0:T(8,128)(2,1)S(1)}, bf16[8,128,256]{2,1,0:T(8,128)(2,1)S(1)}, u32[]{:S(2)}, u32[]{:S(2)}) collective-permute-start(bf16[8,128,256]{2,1,0:T(8,128)(2,1)S(1)} %constant_dynamic-update-slice_fusion.6.rest_9_), channel_id=1, source_target_pairs={{0,3},{1,0},{2,1},{3,2},{4,7},{5,4},{6,5},{7,6},{8,11},{9,8},{10,9... | collective-permute-start | bytes 1572872 | tf_op jit(solution)/shard_map/ppermute | solution.py:43
  151.4 4.2 %collective-permute-done.42.rest_10_ = bf16[8,128,256]{2,1,0:T(8,128)(2,1)S(1)} collective-permute-done((bf16[8,128,256]{2,1,0:T(8,128)(2,1)S(1)}, bf16[8,128,256]{2,1,0:T(8,128)(2,1)S(1)}, u32[]{:S(2)}, u32[]{:S(2)}) %collective-permute-start.42) | collective-permute-done | bytes 524320 | tf_op jit(solution)/shard_map/ppermute | solution.py:43
  156.8 4.7 %collective-permute-done.46.rest_15_ = bf16[8,128,256]{2,1,0:T(8,128)(2,1)S(1)} collective-permute-done((bf16[8,128,256]{2,1,0:T(8,128)(2,1)S(1)}, bf16[8,128,256]{2,1,0:T(8,128)(2,1)S(1)}, u32[]{:S(2)}, u32[]{:S(2)}) %collective-permute-start.46) | collective-permute-done | bytes 524320 | tf_op jit(solution)/shard_map/ppermute | solution.py:43
  161.4 3.7 %collective-permute-start.47 = (bf16[8,128,256]{2,1,0:T(8,128)(2,1)S(1)}, bf16[8,128,256]{2,1,0:T(8,128)(2,1)S(1)}, u32[]{:S(2)}, u32[]{:S(2)}) collective-permute-start(bf16[8,128,256]{2,1,0:T(8,128)(2,1)S(1)} %collective-permute-done.46.rest_15_), channel_id=1, source_target_pairs={{0,3},{1,0},{2,1},{3,2},{4,7},{5,4},{6,5},{7,6},{8,11},{9,8},{10,9... | collective-permute-start | bytes 1572872 | tf_op jit(solution)/shard_map/ppermute | solution.py:43
  166.9 3.2 %collective-permute-done.43.rest_11_ = bf16[8,128,256]{2,1,0:T(8,128)(2,1)S(1)} collective-permute-done((bf16[8,128,256]{2,1,0:T(8,128)(2,1)S(1)}, bf16[8,128,256]{2,1,0:T(8,128)(2,1)S(1)}, u32[]{:S(2)}, u32[]{:S(2)}) %collective-permute-start.43) | collective-permute-done | bytes 524320 | tf_op jit(solution)/shard_map/ppermute | solution.py:43
  171.2 5.0 %collective-permute-done.47.rest_13_ = bf16[8,128,256]{2,1,0:T(8,128)(2,1)S(1)} collective-permute-done((bf16[8,128,256]{2,1,0:T(8,128)(2,1)S(1)}, bf16[8,128,256]{2,1,0:T(8,128)(2,1)S(1)}, u32[]{:S(2)}, u32[]{:S(2)}) %collective-permute-start.47) | collective-permute-done | bytes 524320 | tf_op jit(solution)/shard_map/ppermute | solution.py:43
  176.2 2.2 %collective-permute-done.41.rest_5_ = bf16[8,128,256]{2,1,0:T(8,128)(2,1)S(1)} collective-permute-done((bf16[8,128,256]{2,1,0:T(8,128)(2,1)S(1)}, bf16[8,128,256]{2,1,0:T(8,128)(2,1)S(1)}, u32[]{:S(2)}, u32[]{:S(2)}) %collective-permute-start.41) | collective-permute-done | bytes 524320 | tf_op jit(solution)/shard_map/ppermute | solution.py:43
  178.4 5.2 %collective-permute-done.44.rest_12_ = bf16[8,128,256]{2,1,0:T(8,128)(2,1)S(1)} collective-permute-done((bf16[8,128,256]{2,1,0:T(8,128)(2,1)S(1)}, bf16[8,128,256]{2,1,0:T(8,128)(2,1)S(1)}, u32[]{:S(2)}, u32[]{:S(2)}) %collective-permute-start.44) | collective-permute-done | bytes 524320 | tf_op jit(solution)/shard_map/ppermute | solution.py:43
  184.0 6.3 %decode.1 = bf16[227,3072]{1,0:T(8,128)(2,1)} custom-call(s32[3,24]{1,0:T(4,128)S(1)} %bitcast.11, bf16[227,3072]{1,0:T(8,128)(2,1)S(1)} %bitcast.7, bf16[24,3,128,128]{3,2,1,0:T(8,128)(2,1)S(1)} %copy-done.3, bf16[227,512]{1,0:T(8,128)(2,1)S(1)} %bitcast.8, bf16[8,128,256]{2,1,0:T(8,128)(2,1)S(1)} %constant_dynamic-update-slice_fusion.rest_0_, ...), custom_call_target="tpu_custom_call" | custom-call | tf_op jit(solution)/shard_map/decode/pallas_call | solution.py:378
  (128 shorter events, 53.6 us)
Async XLA Ops:
  9.6 15.1 %collective-permute-start.3 = (bf16[8,128,256]{2,1,0:T(8,128)(2,1)S(1)}, bf16[8,128,256]{2,1,0:T(8,128)(2,1)S(1)}, u32[]{:S(2)}, u32[]{:S(2)}) collective-permute-start(bf16[8,128,256]{2,1,0:T(8,128)(2,1)S(1)} %get-tuple-element.75), channel_id=1, source_target_pairs={{0,4},{1,5},{2,6},{3,7},{4,8},{5,9},{6,10},{7,11},{8,12},{9,13},{1... | collective-permute-start | bytes 1572872 | tf_op jit(solution)/shard_map/ppermute | solution.py:43
  11.3 15.7 %collective-permute-start = (bf16[8,128,256]{2,1,0:T(8,128)(2,1)S(1)}, bf16[8,128,256]{2,1,0:T(8,128)(2,1)S(1)}, u32[]{:S(2)}, u32[]{:S(2)}) collective-permute-start(bf16[8,128,256]{2,1,0:T(8,128)(2,1)S(1)} %get-tuple-element.71), channel_id=1, source_target_pairs={{0,1},{1,2},{2,3},{3,0},{4,5},{5,6},{6,7},{7,4},{8,9},{9,10},{10,1... | collective-permute-start | bytes 1572872 | tf_op jit(solution)/shard_map/ppermute | solution.py:43
  13.2 14.1 %collective-permute-start.2 = (bf16[8,128,256]{2,1,0:T(8,128)(2,1)S(1)}, bf16[8,128,256]{2,1,0:T(8,128)(2,1)S(1)}, u32[]{:S(2)}, u32[]{:S(2)}) collective-permute-start(bf16[8,128,256]{2,1,0:T(8,128)(2,1)S(1)} %get-tuple-element.73), channel_id=1, source_target_pairs={{0,3},{1,0},{2,1},{3,2},{4,7},{5,4},{6,5},{7,6},{8,11},{9,8},{10,9... | collective-permute-start | bytes 1572872 | tf_op jit(solution)/shard_map/ppermute | solution.py:43
  15.3 15.1 %collective-permute-start.7 = (bf16[8,128,256]{2,1,0:T(8,128)(2,1)S(1)}, bf16[8,128,256]{2,1,0:T(8,128)(2,1)S(1)}, u32[]{:S(2)}, u32[]{:S(2)}) collective-permute-start(bf16[8,128,256]{2,1,0:T(8,128)(2,1)S(1)} %get-tuple-element.81), channel_id=1, source_target_pairs={{0,12},{1,13},{2,14},{3,15},{4,0},{5,1},{6,2},{7,3},{8,4},{9,5},{1... | collective-permute-start | bytes 1572872 | tf_op jit(solution)/shard_map/ppermute | solution.py:43
  24.8 14.2 %collective-permute-start.4 = (bf16[8,128,256]{2,1,0:T(8,128)(2,1)S(1)}, bf16[8,128,256]{2,1,0:T(8,128)(2,1)S(1)}, u32[]{:S(2)}, u32[]{:S(2)}) collective-permute-start(bf16[8,128,256]{2,1,0:T(8,128)(2,1)S(1)} %add_convert_fusion.2), channel_id=1, source_target_pairs={{0,4},{1,5},{2,6},{3,7},{4,8},{5,9},{6,10},{7,11},{8,12},{9,13},{1... | collective-permute-start | bytes 1572872 | tf_op jit(solution)/shard_map/ppermute | solution.py:43
  27.1 14.1 %collective-permute-start.1 = (bf16[8,128,256]{2,1,0:T(8,128)(2,1)S(1)}, bf16[8,128,256]{2,1,0:T(8,128)(2,1)S(1)}, u32[]{:S(2)}, u32[]{:S(2)}) collective-permute-start(bf16[8,128,256]{2,1,0:T(8,128)(2,1)S(1)} %add_convert_fusion.3), channel_id=1, source_target_pairs={{0,1},{1,2},{2,3},{3,0},{4,5},{5,6},{6,7},{7,4},{8,9},{9,10},{10,1... | collective-permute-start | bytes 1572872 | tf_op jit(solution)/shard_map/ppermute | solution.py:43
  27.3 13.9 %collective-permute-start.13 = (bf16[8,128,256]{2,1,0:T(8,128)(2,1)S(1)}, bf16[8,128,256]{2,1,0:T(8,128)(2,1)S(1)}, u32[]{:S(2)}, u32[]{:S(2)}) collective-permute-start(bf16[8,128,256]{2,1,0:T(8,128)(2,1)S(1)} %get-tuple-element.91), channel_id=1, source_target_pairs={{0,3},{1,0},{2,1},{3,2},{4,7},{5,4},{6,5},{7,6},{8,11},{9,8},{10,9... | collective-permute-start | bytes 1572872 | tf_op jit(solution)/shard_map/ppermute | solution.py:43
  30.4 18.3 %collective-permute-start.8 = (bf16[8,128,256]{2,1,0:T(8,128)(2,1)S(1)}, bf16[8,128,256]{2,1,0:T(8,128)(2,1)S(1)}, u32[]{:S(2)}, u32[]{:S(2)}) collective-permute-start(bf16[8,128,256]{2,1,0:T(8,128)(2,1)S(1)} %get-tuple-element.82), channel_id=1, source_target_pairs={{0,12},{1,13},{2,14},{3,15},{4,0},{5,1},{6,2},{7,3},{8,4},{9,5},{1... | collective-permute-start | bytes 1572872 | tf_op jit(solution)/shard_map/ppermute | solution.py:43
  41.3 12.4 %collective-permute-start.14 = (bf16[8,128,256]{2,1,0:T(8,128)(2,1)S(1)}, bf16[8,128,256]{2,1,0:T(8,128)(2,1)S(1)}, u32[]{:S(2)}, u32[]{:S(2)}) collective-permute-start(bf16[8,128,256]{2,1,0:T(8,128)(2,1)S(1)} %add_convert_fusion), channel_id=1, source_target_pairs={{0,3},{1,0},{2,1},{3,2},{4,7},{5,4},{6,5},{7,6},{8,11},{9,8},{10,9... | collective-permute-start | bytes 1572872 | tf_op jit(solution)/shard_map/ppermute | solution.py:43
  48.8 11.9 %collective-permute-start.11 = (bf16[8,128,256]{2,1,0:T(8,128)(2,1)S(1)}, bf16[8,128,256]{2,1,0:T(8,128)(2,1)S(1)}, u32[]{:S(2)}, u32[]{:S(2)}) collective-permute-start(bf16[8,128,256]{2,1,0:T(8,128)(2,1)S(1)} %get-tuple-element.87), channel_id=1, source_target_pairs={{0,1},{1,2},{2,3},{3,0},{4,5},{5,6},{6,7},{7,4},{8,9},{9,10},{10,1... | collective-permute-start | bytes 1572872 | tf_op jit(solution)/shard_map/ppermute | solution.py:43
  48.9 11.9 %collective-permute-start.9 = (bf16[8,128,256]{2,1,0:T(8,128)(2,1)S(1)}, bf16[8,128,256]{2,1,0:T(8,128)(2,1)S(1)}, u32[]{:S(2)}, u32[]{:S(2)}) collective-permute-start(bf16[8,128,256]{2,1,0:T(8,128)(2,1)S(1)} %add_convert_fusion.1), channel_id=1, source_target_pairs={{0,12},{1,13},{2,14},{3,15},{4,0},{5,1},{6,2},{7,3},{8,4},{9,5},{1... | collective-permute-start | bytes 1572872 | tf_op jit(solution)/shard_map/ppermute | solution.py:43
  52.4 12.1 %collective-permute-start.6 = (bf16[8,128,256]{2,1,0:T(8,128)(2,1)S(1)}, bf16[8,128,256]{2,1,0:T(8,128)(2,1)S(1)}, u32[]{:S(2)}, u32[]{:S(2)}) collective-permute-start(bf16[8,128,256]{2,1,0:T(8,128)(2,1)S(1)} %get-tuple-element.78), channel_id=1, source_target_pairs={{0,4},{1,5},{2,6},{3,7},{4,8},{5,9},{6,10},{7,11},{8,12},{9,13},{1... | collective-permute-start | bytes 1572872 | tf_op jit(solution)/shard_map/ppermute | solution.py:43
  78.9 9.8 %collective-permute-start.20 = (bf16[2,128,512]{2,1,0:T(8,128)(2,1)}, bf16[2,128,512]{2,1,0:T(8,128)(2,1)S(1)}, u32[]{:S(2)}, u32[]{:S(2)}) collective-permute-start(bf16[2,128,512]{2,1,0:T(8,128)(2,1)} %copy-done.15), channel_id=1, source_target_pairs={{0,16},{32,48},{64,80},{96,112},{16,0},{48,32},{80,64},{112,96},{1... | collective-permute-start | bytes 786440 | tf_op jit(solution)/shard_map/ppermute | solution.py:301
  79.0 9.7 %collective-permute-start.21 = (bf16[2,128,512]{2,1,0:T(8,128)(2,1)S(1)}, bf16[2,128,512]{2,1,0:T(8,128)(2,1)S(1)}, u32[]{:S(2)}, u32[]{:S(2)}) collective-permute-start(bf16[2,128,512]{2,1,0:T(8,128)(2,1)S(1)} %get-tuple-element.102), channel_id=1, source_target_pairs={{16,32},{48,64},{80,96},{32,16},{64,48},{96,80},{17,33},{49,65},{8... | collective-permute-start | bytes 786440 | tf_op jit(solution)/shard_map/ppermute | solution.py:301
  98.5 12.6 %collective-permute-start.26 = (bf16[2,128,512]{2,1,0:T(8,128)(2,1)S(1)}, bf16[2,128,512]{2,1,0:T(8,128)(2,1)S(1)}, u32[]{:S(2)}, u32[]{:S(2)}) collective-permute-start(bf16[2,128,512]{2,1,0:T(8,128)(2,1)S(1)} %get-tuple-element.107), channel_id=1, source_target_pairs={{0,16},{32,48},{64,80},{96,112},{16,0},{48,32},{80,64},{112,96},{1... | collective-permute-start | bytes 786440 | tf_op jit(solution)/shard_map/ppermute | solution.py:301
  101.1 10.0 %collective-permute-start.27 = (bf16[2,128,512]{2,1,0:T(8,128)(2,1)S(1)}, bf16[2,128,512]{2,1,0:T(8,128)(2,1)S(1)}, u32[]{:S(2)}, u32[]{:S(2)}) collective-permute-start(bf16[2,128,512]{2,1,0:T(8,128)(2,1)S(1)} %get-tuple-element.108), channel_id=1, source_target_pairs={{16,32},{48,64},{80,96},{32,16},{64,48},{96,80},{17,33},{49,65},{8... | collective-permute-start | bytes 786440 | tf_op jit(solution)/shard_map/ppermute | solution.py:301
  114.2 14.1 %collective-permute-start.33 = (bf16[4,128,256]{2,1,0:T(8,128)(2,1)S(1)}, bf16[4,128,256]{2,1,0:T(8,128)(2,1)S(1)}, u32[]{:S(2)}, u32[]{:S(2)}) collective-permute-start(bf16[4,128,256]{2,1,0:T(8,128)(2,1)S(1)} %get-tuple-element.111), channel_id=1, source_target_pairs={{0,4},{1,5},{2,6},{3,7},{4,8},{5,9},{6,10},{7,11},{8,12},{9,13},{1... | collective-permute-start | bytes 786440 | tf_op jit(solution)/shard_map/ppermute | solution.py:43
  124.9 9.1 %collective-permute-start.38 = (bf16[4,128,256]{2,1,0:T(8,128)(2,1)S(1)}, bf16[4,128,256]{2,1,0:T(8,128)(2,1)S(1)}, u32[]{:S(2)}, u32[]{:S(2)}) collective-permute-start(bf16[4,128,256]{2,1,0:T(8,128)(2,1)S(1)} %get-tuple-element.111), channel_id=1, source_target_pairs={{0,12},{1,13},{2,14},{3,15},{4,0},{5,1},{6,2},{7,3},{8,4},{9,5},{1... | collective-permute-start | bytes 786440 | tf_op jit(solution)/shard_map/ppermute | solution.py:43
  128.2 12.2 %collective-permute-start.34 = (bf16[4,128,256]{2,1,0:T(8,128)(2,1)S(1)}, bf16[4,128,256]{2,1,0:T(8,128)(2,1)S(1)}, u32[]{:S(2)}, u32[]{:S(2)}) collective-permute-start(bf16[4,128,256]{2,1,0:T(8,128)(2,1)S(1)} %collective-permute-done.33), channel_id=1, source_target_pairs={{0,4},{1,5},{2,6},{3,7},{4,8},{5,9},{6,10},{7,11},{8,12},{9,13},{1... | collective-permute-start | bytes 786440 | tf_op jit(solution)/shard_map/ppermute | solution.py:43
  130.4 10.0 %collective-permute-start.31 = (bf16[4,128,256]{2,1,0:T(8,128)(2,1)S(1)}, bf16[4,128,256]{2,1,0:T(8,128)(2,1)S(1)}, u32[]{:S(2)}, u32[]{:S(2)}) collective-permute-start(bf16[4,128,256]{2,1,0:T(8,128)(2,1)S(1)} %collective-permute-done.30), channel_id=1, source_target_pairs={{0,1},{1,2},{2,3},{3,0},{4,5},{5,6},{6,7},{7,4},{8,9},{9,10},{10,1... | collective-permute-start | bytes 786440 | tf_op jit(solution)/shard_map/ppermute | solution.py:43
  130.5 15.4 %collective-permute-start.45 = (bf16[8,128,256]{2,1,0:T(8,128)(2,1)S(1)}, bf16[8,128,256]{2,1,0:T(8,128)(2,1)S(1)}, u32[]{:S(2)}, u32[]{:S(2)}) collective-permute-start(bf16[8,128,256]{2,1,0:T(8,128)(2,1)S(1)} %constant_dynamic-update-slice_fusion.4.rest_8_), channel_id=1, source_target_pairs={{0,3},{1,0},{2,1},{3,2},{4,7},{5,4},{6,5},{7,6},{8,11},{9,8},{10,9... | collective-permute-start | bytes 1572872 | tf_op jit(solution)/shard_map/ppermute | solution.py:43
  134.0 15.6 %collective-permute-start.39 = (bf16[8,128,256]{2,1,0:T(8,128)(2,1)S(1)}, bf16[8,128,256]{2,1,0:T(8,128)(2,1)S(1)}, u32[]{:S(2)}, u32[]{:S(2)}) collective-permute-start(bf16[8,128,256]{2,1,0:T(8,128)(2,1)S(1)} %constant_dynamic-update-slice_fusion.rest_0_), channel_id=1, source_target_pairs={{0,12},{1,13},{2,14},{3,15},{4,0},{5,1},{6,2},{7,3},{8,4},{9,5},{1... | collective-permute-start | bytes 1572872 | tf_op jit(solution)/shard_map/ppermute | solution.py:43
  140.4 15.2 %collective-permute-start.42 = (bf16[8,128,256]{2,1,0:T(8,128)(2,1)S(1)}, bf16[8,128,256]{2,1,0:T(8,128)(2,1)S(1)}, u32[]{:S(2)}, u32[]{:S(2)}) collective-permute-start(bf16[8,128,256]{2,1,0:T(8,128)(2,1)S(1)} %constant_dynamic-update-slice_fusion.4.rest_8_), channel_id=1, source_target_pairs={{0,1},{1,2},{2,3},{3,0},{4,5},{5,6},{6,7},{7,4},{8,9},{9,10},{10,1... | collective-permute-start | bytes 1572872 | tf_op jit(solution)/shard_map/ppermute | solution.py:43
  140.4 15.3 %collective-permute-start.35 = (bf16[8,128,256]{2,1,0:T(8,128)(2,1)S(1)}, bf16[8,128,256]{2,1,0:T(8,128)(2,1)S(1)}, u32[]{:S(2)}, u32[]{:S(2)}) collective-permute-start(bf16[8,128,256]{2,1,0:T(8,128)(2,1)S(1)} %constant_dynamic-update-slice_fusion.rest_0_), channel_id=1, source_target_pairs={{0,4},{1,5},{2,6},{3,7},{4,8},{5,9},{6,10},{7,11},{8,12},{9,13},{1... | collective-permute-start | bytes 1572872 | tf_op jit(solution)/shard_map/ppermute | solution.py:43
  145.9 15.5 %collective-permute-start.46 = (bf16[8,128,256]{2,1,0:T(8,128)(2,1)S(1)}, bf16[8,128,256]{2,1,0:T(8,128)(2,1)S(1)}, u32[]{:S(2)}, u32[]{:S(2)}) collective-permute-start(bf16[8,128,256]{2,1,0:T(8,128)(2,1)S(1)} %constant_dynamic-update-slice_fusion.6.rest_9_), channel_id=1, source_target_pairs={{0,3},{1,0},{2,1},{3,2},{4,7},{5,4},{6,5},{7,6},{8,11},{9,8},{10,9... | collective-permute-start | bytes 1572872 | tf_op jit(solution)/shard_map/ppermute | solution.py:43
  149.6 15.5 %collective-permute-start.40 = (bf16[8,128,256]{2,1,0:T(8,128)(2,1)S(1)}, bf16[8,128,256]{2,1,0:T(8,128)(2,1)S(1)}, u32[]{:S(2)}, u32[]{:S(2)}) collective-permute-start(bf16[8,128,256]{2,1,0:T(8,128)(2,1)S(1)} %constant_dynamic-update-slice_fusion.2.rest_1_), channel_id=1, source_target_pairs={{0,12},{1,13},{2,14},{3,15},{4,0},{5,1},{6,2},{7,3},{8,4},{9,5},{1... | collective-permute-start | bytes 1572872 | tf_op jit(solution)/shard_map/ppermute | solution.py:43
  155.7 14.4 %collective-permute-start.43 = (bf16[8,128,256]{2,1,0:T(8,128)(2,1)S(1)}, bf16[8,128,256]{2,1,0:T(8,128)(2,1)S(1)}, u32[]{:S(2)}, u32[]{:S(2)}) collective-permute-start(bf16[8,128,256]{2,1,0:T(8,128)(2,1)S(1)} %constant_dynamic-update-slice_fusion.6.rest_9_), channel_id=1, source_target_pairs={{0,1},{1,2},{2,3},{3,0},{4,5},{5,6},{6,7},{7,4},{8,9},{9,10},{10,1... | collective-permute-start | bytes 1572872 | tf_op jit(solution)/shard_map/ppermute | solution.py:43
  155.7 14.4 %collective-permute-start.36 = (bf16[8,128,256]{2,1,0:T(8,128)(2,1)S(1)}, bf16[8,128,256]{2,1,0:T(8,128)(2,1)S(1)}, u32[]{:S(2)}, u32[]{:S(2)}) collective-permute-start(bf16[8,128,256]{2,1,0:T(8,128)(2,1)S(1)} %constant_dynamic-update-slice_fusion.2.rest_1_), channel_id=1, source_target_pairs={{0,4},{1,5},{2,6},{3,7},{4,8},{5,9},{6,10},{7,11},{8,12},{9,13},{1... | collective-permute-start | bytes 1572872 | tf_op jit(solution)/shard_map/ppermute | solution.py:43
  161.4 14.7 %collective-permute-start.47 = (bf16[8,128,256]{2,1,0:T(8,128)(2,1)S(1)}, bf16[8,128,256]{2,1,0:T(8,128)(2,1)S(1)}, u32[]{:S(2)}, u32[]{:S(2)}) collective-permute-start(bf16[8,128,256]{2,1,0:T(8,128)(2,1)S(1)} %collective-permute-done.46.rest_15_), channel_id=1, source_target_pairs={{0,3},{1,0},{2,1},{3,2},{4,7},{5,4},{6,5},{7,6},{8,11},{9,8},{10,9... | collective-permute-start | bytes 1572872 | tf_op jit(solution)/shard_map/ppermute | solution.py:43
  165.1 13.3 %collective-permute-start.41 = (bf16[8,128,256]{2,1,0:T(8,128)(2,1)S(1)}, bf16[8,128,256]{2,1,0:T(8,128)(2,1)S(1)}, u32[]{:S(2)}, u32[]{:S(2)}) collective-permute-start(bf16[8,128,256]{2,1,0:T(8,128)(2,1)S(1)} %collective-permute-done.40.rest_7_), channel_id=1, source_target_pairs={{0,12},{1,13},{2,14},{3,15},{4,0},{5,1},{6,2},{7,3},{8,4},{9,5},{1... | collective-permute-start | bytes 1572872 | tf_op jit(solution)/shard_map/ppermute | solution.py:43
  170.1 13.5 %collective-permute-start.44 = (bf16[8,128,256]{2,1,0:T(8,128)(2,1)S(1)}, bf16[8,128,256]{2,1,0:T(8,128)(2,1)S(1)}, u32[]{:S(2)}, u32[]{:S(2)}) collective-permute-start(bf16[8,128,256]{2,1,0:T(8,128)(2,1)S(1)} %collective-permute-done.42.rest_10_), channel_id=1, source_target_pairs={{0,1},{1,2},{2,3},{3,0},{4,5},{5,6},{6,7},{7,4},{8,9},{9,10},{10,1... | collective-permute-start | bytes 1572872 | tf_op jit(solution)/shard_map/ppermute | solution.py:43
  170.1 13.9 %collective-permute-start.37 = (bf16[8,128,256]{2,1,0:T(8,128)(2,1)S(1)}, bf16[8,128,256]{2,1,0:T(8,128)(2,1)S(1)}, u32[]{:S(2)}, u32[]{:S(2)}) collective-permute-start(bf16[8,128,256]{2,1,0:T(8,128)(2,1)S(1)} %collective-permute-done.35.rest_2_), channel_id=1, source_target_pairs={{0,4},{1,5},{2,6},{3,7},{4,8},{5,9},{6,10},{7,11},{8,12},{9,13},{1... | collective-permute-start | bytes 1572872 | tf_op jit(solution)/shard_map/ppermute | solution.py:43
  (32 other events, 598.8 us)

commit v4 on v3

--- a/solution.py
+++ b/solution.py
@@ -301,14 +301,13 @@
     return lax.ppermute(value, axis, pairs + [(b, a) for a, b in pairs])
 
 
-def band_of(own, row_a, row_b, col_a, col_b):
+def band_of(ends, own, row_a, row_b, col_a, col_b):
     col_a, col_b = trade(col_a, "mesh", 0), trade(col_b, "mesh", 1)
     row_a, row_b = trade(row_a, "grid", 0), trade(row_b, "grid", 1)
     corners = []
     for odd in range(2):
-        row = 1 - (parity("grid") + odd) % 2
-        ends = [lax.dynamic_slice_in_dim(value, row, 1, 0) for value in (col_a, col_b)]
-        corners.append(trade(jnp.concatenate(ends, 0), "grid", odd))
+        parts = [lax.dynamic_slice(col, ends[odd], (1, NB, D)) for col in (col_a, col_b)]
+        corners.append(trade(jnp.concatenate(parts, 0), "grid", odd))
     return own, col_a, col_b, row_a, row_b, *corners
 
 
@@ -417,14 +416,18 @@
     m2g_edges,
     output_weight,
 ):
+    zero = jnp.uint32(0)
+    odd = parity("grid").astype(jnp.uint32)
+    ends = [(1 - odd, zero, zero), (odd, zero, zero)]
+    g2m_dest, ends = lax.optimization_barrier((g2m_dest, ends))
     pieces = encode(grid_inputs, embed_weight, send_weight, g2m_dest, g2m_edges)
     mesh, *sent = mesh_start(reduce(pieces), encode_weight, message_weight)
     codes = adj_codes.reshape(OWN, -1)
     mesh, *sent = mesh_step(
-        0, codes, adj_count, mesh, band_of(*sent), couplings, node_weight, message_weight
+        0, codes, adj_count, mesh, band_of(ends, *sent), couplings, node_weight, message_weight
     )
     owns = mesh_step(
-        1, codes, adj_count, mesh, band_of(*sent), couplings, node_weight, decode_weight
+        1, codes, adj_count, mesh, band_of(ends, *sent), couplings, node_weight, decode_weight
     )
     return decode(grid_inputs, m2g_src, m2g_edges, output_weight, gather(owns))
 

time: 191 us -> 183 us (0.958)
  the two profiles are of different devices: /device:TPU:0 before, /device:TPU:2 now
where the time goes in v4:
time: 183 us
  waiting for transfers between devices  83.3 us (46%)
  starting transfers between devices  76.7 us (42%)
  Pallas kernels  19.4 us (11%)
    ppermute x36, waiting for transfers between devices, shift(): return lax.ppermute(value, 'mesh', pairs)  66 us
    ppermute x36, starting transfers between devices, shift(): return lax.ppermute(value, 'mesh', pairs)  61 us
    ppermute x12, waiting for transfers between devices, trade(): return lax.ppermute(value, axis, pairs + [(b, a) for a, b in pairs])  17.2 us
    ppermute x12, starting transfers between devices, trade(): return lax.ppermute(value, axis, pairs + [(b, a) for a, b in pairs])  15.7 us
    pallas_call x1, Pallas kernels, encode(): pl.pallas_call(encode_kernel, in_specs=[pl.BlockSpec(memory_space=pltpu.S...  8.23 us
    pallas_call x1, Pallas kernels, decode(): pl.pallas_call(decode_kernel, grid_spec=pltpu.PrefetchScalarGridSpec(num_...  6.34 us
    pallas_call x2, Pallas kernels, mesh_step(): pl.pallas_call(functools.partial(step_kernel, layer), in_specs=[smem, sme...  3.9 us
  transfers between devices with their start and end apart: 48, of which 25 were waited for; matrix products, arithmetic and copies ran while one was open for 1% of the time, Pallas kernels for 0%

profile of v4, /device:TPU:2, one launch (start us, length us, event | category | flops | bytes accessed | tf_op | source)
XLA Modules:
  0.0 182.9 jit_solution(2866301036896704224)
XLA Ops:
  0.0 8.2 %encode.1 = (bf16[64,128,256]{2,1,0:T(8,128)(2,1)S(1)}, bf16[64,128,256]{2,1,0:T(8,128)(2,1)S(1)}) custom-call(s32[3,24]{1,0:T(4,128)} %bitcast.12, bf16[227,3072]{1,0:T(8,128)(2,1)} %bitcast.6, bf16[227,512]{1,0:T(8,128)(2,1)} %embed_hbm.1, bf16[512,512]{1,0:T(8,128)(2,1)} %send_hbm.1, bf16[24,3,128,128]{3,2,1,0:T(8,128)(2,1)} %edges_hbm.1), custom_call_target="tpu_custom_call" | custom-call | tf_op jit(solution)/shard_map/encode/pallas_call | solution.py:129
  16.9 7.7 %collective-permute-done.3 = bf16[8,128,256]{2,1,0:T(8,128)(2,1)S(1)} collective-permute-done((bf16[8,128,256]{2,1,0:T(8,128)(2,1)S(1)}, bf16[8,128,256]{2,1,0:T(8,128)(2,1)S(1)}, u32[]{:S(2)}, u32[]{:S(2)}) %collective-permute-start.3) | collective-permute-done | bytes 524320 | tf_op jit(solution)/shard_map/ppermute | solution.py:43
  27.2 2.9 %collective-permute-start.8 = (bf16[8,128,256]{2,1,0:T(8,128)(2,1)S(1)}, bf16[8,128,256]{2,1,0:T(8,128)(2,1)S(1)}, u32[]{:S(2)}, u32[]{:S(2)}) collective-permute-start(bf16[8,128,256]{2,1,0:T(8,128)(2,1)S(1)} %get-tuple-element.86), channel_id=1, source_target_pairs={{0,12},{1,13},{2,14},{3,15},{4,0},{5,1},{6,2},{7,3},{8,4},{9,5},{1... | collective-permute-start | bytes 1572872 | tf_op jit(solution)/shard_map/ppermute | solution.py:43
  32.3 6.5 %collective-permute-done.4 = bf16[8,128,256]{2,1,0:T(8,128)(2,1)S(1)} collective-permute-done((bf16[8,128,256]{2,1,0:T(8,128)(2,1)S(1)}, bf16[8,128,256]{2,1,0:T(8,128)(2,1)S(1)}, u32[]{:S(2)}, u32[]{:S(2)}) %collective-permute-start.4) | collective-permute-done | bytes 524320 | tf_op jit(solution)/shard_map/ppermute | solution.py:43
  44.7 3.9 %collective-permute-done.10 = bf16[4,128,256]{2,1,0:T(8,128)(2,1)S(1)} collective-permute-done((bf16[4,128,256]{2,1,0:T(8,128)(2,1)S(1)}, bf16[4,128,256]{2,1,0:T(8,128)(2,1)S(1)}, u32[]{:S(2)}, u32[]{:S(2)}) %collective-permute-start.10) | collective-permute-done | bytes 262176 | tf_op jit(solution)/shard_map/ppermute | solution.py:43
  50.4 3.3 %collective-permute-start.14 = (bf16[8,128,256]{2,1,0:T(8,128)(2,1)S(1)}, bf16[8,128,256]{2,1,0:T(8,128)(2,1)S(1)}, u32[]{:S(2)}, u32[]{:S(2)}) collective-permute-start(bf16[8,128,256]{2,1,0:T(8,128)(2,1)S(1)} %add_convert_fusion), channel_id=1, source_target_pairs={{0,3},{1,0},{2,1},{3,2},{4,7},{5,4},{6,5},{7,6},{8,11},{9,8},{10,9... | collective-permute-start | bytes 1572872 | tf_op jit(solution)/shard_map/ppermute | solution.py:43
  54.0 6.8 %collective-permute-done.11.refs_6_ = bf16[8,128,256]{2,1,0:T(8,128)(2,1)S(1)} collective-permute-done((bf16[8,128,256]{2,1,0:T(8,128)(2,1)S(1)}, bf16[8,128,256]{2,1,0:T(8,128)(2,1)S(1)}, u32[]{:S(2)}, u32[]{:S(2)}) %collective-permute-start.11) | collective-permute-done | bytes 524320 | tf_op jit(solution)/shard_map/ppermute | solution.py:43
  64.7 3.0 %collective-permute-start.15 = (bf16[4,128,256]{2,1,0:T(8,128)(2,1)S(1)}, bf16[4,128,256]{2,1,0:T(8,128)(2,1)S(1)}, u32[]{:S(2)}, u32[]{:S(2)}) collective-permute-start(bf16[4,128,256]{2,1,0:T(8,128)(2,1)S(1)} %add_convert_fusion.6), channel_id=1, source_target_pairs={{0,3},{1,0},{2,1},{3,2},{4,7},{5,4},{6,5},{7,6},{8,11},{9,8},{10,9... | collective-permute-start | bytes 786440 | tf_op jit(solution)/shard_map/ppermute | solution.py:43
  69.1 3.5 %collective-permute-done.15.refs_4_ = bf16[4,128,256]{2,1,0:T(8,128)(2,1)S(1)} collective-permute-done((bf16[4,128,256]{2,1,0:T(8,128)(2,1)S(1)}, bf16[4,128,256]{2,1,0:T(8,128)(2,1)S(1)}, u32[]{:S(2)}, u32[]{:S(2)}) %collective-permute-start.15) | collective-permute-done | bytes 262176 | tf_op jit(solution)/shard_map/ppermute | solution.py:43
  74.4 2.7 %collective-permute-start.21 = (bf16[2,128,512]{2,1,0:T(8,128)(2,1)S(1)}, bf16[2,128,512]{2,1,0:T(8,128)(2,1)S(1)}, u32[]{:S(2)}, u32[]{:S(2)}) collective-permute-start(bf16[2,128,512]{2,1,0:T(8,128)(2,1)S(1)} %get-tuple-element.106), channel_id=1, source_target_pairs={{16,32},{48,64},{80,96},{32,16},{64,48},{96,80},{17,33},{49,65},{8... | collective-permute-start | bytes 786440 | tf_op jit(solution)/shard_map/ppermute | solution.py:301
  77.2 2.7 %collective-permute-done.18.rest_1_ = bf16[2,128,512]{2,1,0:T(8,128)(2,1)S(1)} collective-permute-done((bf16[2,128,512]{2,1,0:T(8,128)(2,1)S(1)}, bf16[2,128,512]{2,1,0:T(8,128)(2,1)S(1)}, u32[]{:S(2)}, u32[]{:S(2)}) %collective-permute-start.18) | collective-permute-done | bytes 262176 | tf_op jit(solution)/shard_map/ppermute | solution.py:301
  80.2 2.5 %collective-permute-start.23 = (bf16[2,128,512]{2,1,0:T(8,128)(2,1)S(1)}, bf16[2,128,512]{2,1,0:T(8,128)(2,1)S(1)}, u32[]{:S(2)}, u32[]{:S(2)}) collective-permute-start(bf16[2,128,512]{2,1,0:T(8,128)(2,1)S(1)} %pad_maximum_fusion.1), channel_id=1, source_target_pairs={{16,32},{48,64},{80,96},{32,16},{64,48},{96,80},{17,33},{49,65},{8... | collective-permute-start | bytes 786440 | tf_op jit(solution)/shard_map/ppermute | solution.py:301
  82.7 5.1 %collective-permute-done.23.rest_6_ = bf16[2,128,512]{2,1,0:T(8,128)(2,1)S(1)} collective-permute-done((bf16[2,128,512]{2,1,0:T(8,128)(2,1)S(1)}, bf16[2,128,512]{2,1,0:T(8,128)(2,1)S(1)}, u32[]{:S(2)}, u32[]{:S(2)}) %collective-permute-start.23) | collective-permute-done | bytes 262176 | tf_op jit(solution)/shard_map/ppermute | solution.py:301
  89.9 4.1 %collective-permute-start.24 = (bf16[2,128,512]{2,1,0:T(8,128)(2,1)S(1)}, bf16[2,128,512]{2,1,0:T(8,128)(2,1)S(1)}, u32[]{:S(2)}, u32[]{:S(2)}) collective-permute-start(bf16[2,128,512]{2,1,0:T(8,128)(2,1)S(1)} %get-tuple-element.111), channel_id=1, source_target_pairs={{0,1},{2,3},{4,5},{6,7},{8,9},{10,11},{12,13},{14,15},{1,0},{3,2},... | collective-permute-start | bytes 786440 | tf_op jit(solution)/shard_map/ppermute | solution.py:301
  97.2 3.6 %collective-permute-done.24.rest_1_ = bf16[2,128,512]{2,1,0:T(8,128)(2,1)S(1)} collective-permute-done((bf16[2,128,512]{2,1,0:T(8,128)(2,1)S(1)}, bf16[2,128,512]{2,1,0:T(8,128)(2,1)S(1)}, u32[]{:S(2)}, u32[]{:S(2)}) %collective-permute-start.24) | collective-permute-done | bytes 262176 | tf_op jit(solution)/shard_map/ppermute | solution.py:301
  103.1 5.7 %collective-permute-done.29.rest_6_ = bf16[2,128,512]{2,1,0:T(8,128)(2,1)S(1)} collective-permute-done((bf16[2,128,512]{2,1,0:T(8,128)(2,1)S(1)}, bf16[2,128,512]{2,1,0:T(8,128)(2,1)S(1)}, u32[]{:S(2)}, u32[]{:S(2)}) %collective-permute-start.29) | collective-permute-done | bytes 262176 | tf_op jit(solution)/shard_map/ppermute | solution.py:301
  110.8 7.1 %collective-permute-start.30 = (bf16[4,128,256]{2,1,0:T(8,128)(2,1)S(1)}, bf16[4,128,256]{2,1,0:T(8,128)(2,1)S(1)}, u32[]{:S(2)}, u32[]{:S(2)}) collective-permute-start(bf16[4,128,256]{2,1,0:T(8,128)(2,1)S(1)} %get-tuple-element.115), channel_id=1, source_target_pairs={{0,1},{1,2},{2,3},{3,0},{4,5},{5,6},{6,7},{7,4},{8,9},{9,10},{10,1... | collective-permute-start | bytes 786440 | tf_op jit(solution)/shard_map/ppermute | solution.py:43
  118.3 3.2 %collective-permute-start.32 = (bf16[4,128,256]{2,1,0:T(8,128)(2,1)S(1)}, bf16[4,128,256]{2,1,0:T(8,128)(2,1)S(1)}, u32[]{:S(2)}, u32[]{:S(2)}) collective-permute-start(bf16[4,128,256]{2,1,0:T(8,128)(2,1)S(1)} %get-tuple-element.115), channel_id=1, source_target_pairs={{0,3},{1,0},{2,1},{3,2},{4,7},{5,4},{6,5},{7,6},{8,11},{9,8},{10,9... | collective-permute-start | bytes 786440 | tf_op jit(solution)/shard_map/ppermute | solution.py:43
  124.0 3.6 %collective-permute-done.30 = bf16[4,128,256]{2,1,0:T(8,128)(2,1)S(1)} collective-permute-done((bf16[4,128,256]{2,1,0:T(8,128)(2,1)S(1)}, bf16[4,128,256]{2,1,0:T(8,128)(2,1)S(1)}, u32[]{:S(2)}, u32[]{:S(2)}) %collective-permute-start.30) | collective-permute-done | bytes 262176 | tf_op jit(solution)/shard_map/ppermute | solution.py:43
  128.2 3.3 %collective-permute-start.45 = (bf16[8,128,256]{2,1,0:T(8,128)(2,1)S(1)}, bf16[8,128,256]{2,1,0:T(8,128)(2,1)S(1)}, u32[]{:S(2)}, u32[]{:S(2)}) collective-permute-start(bf16[8,128,256]{2,1,0:T(8,128)(2,1)S(1)} %constant_dynamic-update-slice_fusion.4.rest_8_), channel_id=1, source_target_pairs={{0,3},{1,0},{2,1},{3,2},{4,7},{5,4},{6,5},{7,6},{8,11},{9,8},{10,9... | collective-permute-start | bytes 1572872 | tf_op jit(solution)/shard_map/ppermute | solution.py:43
  131.5 2.7 %collective-permute-start.39 = (bf16[8,128,256]{2,1,0:T(8,128)(2,1)S(1)}, bf16[8,128,256]{2,1,0:T(8,128)(2,1)S(1)}, u32[]{:S(2)}, u32[]{:S(2)}) collective-permute-start(bf16[8,128,256]{2,1,0:T(8,128)(2,1)S(1)} %constant_dynamic-update-slice_fusion.rest_0_), channel_id=1, source_target_pairs={{0,12},{1,13},{2,14},{3,15},{4,0},{5,1},{6,2},{7,3},{8,4},{9,5},{1... | collective-permute-start | bytes 1572872 | tf_op jit(solution)/shard_map/ppermute | solution.py:43
  134.3 2.6 %collective-permute-done.31 = bf16[4,128,256]{2,1,0:T(8,128)(2,1)S(1)} collective-permute-done((bf16[4,128,256]{2,1,0:T(8,128)(2,1)S(1)}, bf16[4,128,256]{2,1,0:T(8,128)(2,1)S(1)}, u32[]{:S(2)}, u32[]{:S(2)}) %collective-permute-start.31) | collective-permute-done | bytes 262176 | tf_op jit(solution)/shard_map/ppermute | solution.py:43
  137.4 4.6 %collective-permute-done.45.rest_14_ = bf16[8,128,256]{2,1,0:T(8,128)(2,1)S(1)} collective-permute-done((bf16[8,128,256]{2,1,0:T(8,128)(2,1)S(1)}, bf16[8,128,256]{2,1,0:T(8,128)(2,1)S(1)}, u32[]{:S(2)}, u32[]{:S(2)}) %collective-permute-start.45) | collective-permute-done | bytes 524320 | tf_op jit(solution)/shard_map/ppermute | solution.py:43
  142.0 3.7 %collective-permute-start.46 = (bf16[8,128,256]{2,1,0:T(8,128)(2,1)S(1)}, bf16[8,128,256]{2,1,0:T(8,128)(2,1)S(1)}, u32[]{:S(2)}, u32[]{:S(2)}) collective-permute-start(bf16[8,128,256]{2,1,0:T(8,128)(2,1)S(1)} %constant_dynamic-update-slice_fusion.6.rest_9_), channel_id=1, source_target_pairs={{0,3},{1,0},{2,1},{3,2},{4,7},{5,4},{6,5},{7,6},{8,11},{9,8},{10,9... | collective-permute-start | bytes 1572872 | tf_op jit(solution)/shard_map/ppermute | solution.py:43
  145.7 2.9 %collective-permute-start.40 = (bf16[8,128,256]{2,1,0:T(8,128)(2,1)S(1)}, bf16[8,128,256]{2,1,0:T(8,128)(2,1)S(1)}, u32[]{:S(2)}, u32[]{:S(2)}) collective-permute-start(bf16[8,128,256]{2,1,0:T(8,128)(2,1)S(1)} %constant_dynamic-update-slice_fusion.2.rest_1_), channel_id=1, source_target_pairs={{0,12},{1,13},{2,14},{3,15},{4,0},{5,1},{6,2},{7,3},{8,4},{9,5},{1... | collective-permute-start | bytes 1572872 | tf_op jit(solution)/shard_map/ppermute | solution.py:43
  151.1 4.1 %collective-permute-done.46.rest_15_ = bf16[8,128,256]{2,1,0:T(8,128)(2,1)S(1)} collective-permute-done((bf16[8,128,256]{2,1,0:T(8,128)(2,1)S(1)}, bf16[8,128,256]{2,1,0:T(8,128)(2,1)S(1)}, u32[]{:S(2)}, u32[]{:S(2)}) %collective-permute-start.46) | collective-permute-done | bytes 524320 | tf_op jit(solution)/shard_map/ppermute | solution.py:43
  155.3 3.7 %collective-permute-start.47 = (bf16[8,128,256]{2,1,0:T(8,128)(2,1)S(1)}, bf16[8,128,256]{2,1,0:T(8,128)(2,1)S(1)}, u32[]{:S(2)}, u32[]{:S(2)}) collective-permute-start(bf16[8,128,256]{2,1,0:T(8,128)(2,1)S(1)} %collective-permute-done.46.rest_15_), channel_id=1, source_target_pairs={{0,3},{1,0},{2,1},{3,2},{4,7},{5,4},{6,5},{7,6},{8,11},{9,8},{10,9... | collective-permute-start | bytes 1572872 | tf_op jit(solution)/shard_map/ppermute | solution.py:43
  159.0 3.1 %collective-permute-start.41 = (bf16[8,128,256]{2,1,0:T(8,128)(2,1)S(1)}, bf16[8,128,256]{2,1,0:T(8,128)(2,1)S(1)}, u32[]{:S(2)}, u32[]{:S(2)}) collective-permute-start(bf16[8,128,256]{2,1,0:T(8,128)(2,1)S(1)} %collective-permute-done.40.rest_7_), channel_id=1, source_target_pairs={{0,12},{1,13},{2,14},{3,15},{4,0},{5,1},{6,2},{7,3},{8,4},{9,5},{1... | collective-permute-start | bytes 1572872 | tf_op jit(solution)/shard_map/ppermute | solution.py:43
  164.2 3.5 %collective-permute-done.47.rest_13_ = bf16[8,128,256]{2,1,0:T(8,128)(2,1)S(1)} collective-permute-done((bf16[8,128,256]{2,1,0:T(8,128)(2,1)S(1)}, bf16[8,128,256]{2,1,0:T(8,128)(2,1)S(1)}, u32[]{:S(2)}, u32[]{:S(2)}) %collective-permute-start.47) | collective-permute-done | bytes 524320 | tf_op jit(solution)/shard_map/ppermute | solution.py:43
  167.6 3.0 %collective-permute-done.41.rest_5_ = bf16[8,128,256]{2,1,0:T(8,128)(2,1)S(1)} collective-permute-done((bf16[8,128,256]{2,1,0:T(8,128)(2,1)S(1)}, bf16[8,128,256]{2,1,0:T(8,128)(2,1)S(1)}, u32[]{:S(2)}, u32[]{:S(2)}) %collective-permute-start.41) | collective-permute-done | bytes 524320 | tf_op jit(solution)/shard_map/ppermute | solution.py:43
  170.6 5.8 %collective-permute-done.44.rest_12_ = bf16[8,128,256]{2,1,0:T(8,128)(2,1)S(1)} collective-permute-done((bf16[8,128,256]{2,1,0:T(8,128)(2,1)S(1)}, bf16[8,128,256]{2,1,0:T(8,128)(2,1)S(1)}, u32[]{:S(2)}, u32[]{:S(2)}) %collective-permute-start.44) | collective-permute-done | bytes 524320 | tf_op jit(solution)/shard_map/ppermute | solution.py:43
  176.4 6.3 %decode.1 = bf16[227,3072]{1,0:T(8,128)(2,1)} custom-call(s32[3,24]{1,0:T(4,128)S(1)} %bitcast.11, bf16[227,3072]{1,0:T(8,128)(2,1)S(1)} %bitcast.7, bf16[24,3,128,128]{3,2,1,0:T(8,128)(2,1)S(1)} %copy-done.3, bf16[227,512]{1,0:T(8,128)(2,1)S(1)} %bitcast.8, bf16[8,128,256]{2,1,0:T(8,128)(2,1)S(1)} %constant_dynamic-update-slice_fusion.rest_0_, ...), custom_call_target="tpu_custom_call" | custom-call | tf_op jit(solution)/shard_map/decode/pallas_call | solution.py:377
  (118 shorter events, 46.7 us)
Async XLA Ops:
  9.6 15.0 %collective-permute-start.3 = (bf16[8,128,256]{2,1,0:T(8,128)(2,1)S(1)}, bf16[8,128,256]{2,1,0:T(8,128)(2,1)S(1)}, u32[]{:S(2)}, u32[]{:S(2)}) collective-permute-start(bf16[8,128,256]{2,1,0:T(8,128)(2,1)S(1)} %get-tuple-element.79), channel_id=1, source_target_pairs={{0,4},{1,5},{2,6},{3,7},{4,8},{5,9},{6,10},{7,11},{8,12},{9,13},{1... | collective-permute-start | bytes 1572872 | tf_op jit(solution)/shard_map/ppermute | solution.py:43
  11.2 15.7 %collective-permute-start = (bf16[8,128,256]{2,1,0:T(8,128)(2,1)S(1)}, bf16[8,128,256]{2,1,0:T(8,128)(2,1)S(1)}, u32[]{:S(2)}, u32[]{:S(2)}) collective-permute-start(bf16[8,128,256]{2,1,0:T(8,128)(2,1)S(1)} %get-tuple-element.75), channel_id=1, source_target_pairs={{0,1},{1,2},{2,3},{3,0},{4,5},{5,6},{6,7},{7,4},{8,9},{9,10},{10,1... | collective-permute-start | bytes 1572872 | tf_op jit(solution)/shard_map/ppermute | solution.py:43
  13.1 14.1 %collective-permute-start.7 = (bf16[8,128,256]{2,1,0:T(8,128)(2,1)S(1)}, bf16[8,128,256]{2,1,0:T(8,128)(2,1)S(1)}, u32[]{:S(2)}, u32[]{:S(2)}) collective-permute-start(bf16[8,128,256]{2,1,0:T(8,128)(2,1)S(1)} %get-tuple-element.85), channel_id=1, source_target_pairs={{0,12},{1,13},{2,14},{3,15},{4,0},{5,1},{6,2},{7,3},{8,4},{9,5},{1... | collective-permute-start | bytes 1572872 | tf_op jit(solution)/shard_map/ppermute | solution.py:43
  14.8 15.4 %collective-permute-start.2 = (bf16[8,128,256]{2,1,0:T(8,128)(2,1)S(1)}, bf16[8,128,256]{2,1,0:T(8,128)(2,1)S(1)}, u32[]{:S(2)}, u32[]{:S(2)}) collective-permute-start(bf16[8,128,256]{2,1,0:T(8,128)(2,1)S(1)} %get-tuple-element.77), channel_id=1, source_target_pairs={{0,3},{1,0},{2,1},{3,2},{4,7},{5,4},{6,5},{7,6},{8,11},{9,8},{10,9... | collective-permute-start | bytes 1572872 | tf_op jit(solution)/shard_map/ppermute | solution.py:43
  24.7 14.1 %collective-permute-start.4 = (bf16[8,128,256]{2,1,0:T(8,128)(2,1)S(1)}, bf16[8,128,256]{2,1,0:T(8,128)(2,1)S(1)}, u32[]{:S(2)}, u32[]{:S(2)}) collective-permute-start(bf16[8,128,256]{2,1,0:T(8,128)(2,1)S(1)} %add_convert_fusion.2), channel_id=1, source_target_pairs={{0,4},{1,5},{2,6},{3,7},{4,8},{5,9},{6,10},{7,11},{8,12},{9,13},{1... | collective-permute-start | bytes 1572872 | tf_op jit(solution)/shard_map/ppermute | solution.py:43
  27.0 14.1 %collective-permute-start.1 = (bf16[8,128,256]{2,1,0:T(8,128)(2,1)S(1)}, bf16[8,128,256]{2,1,0:T(8,128)(2,1)S(1)}, u32[]{:S(2)}, u32[]{:S(2)}) collective-permute-start(bf16[8,128,256]{2,1,0:T(8,128)(2,1)S(1)} %add_convert_fusion.3), channel_id=1, source_target_pairs={{0,1},{1,2},{2,3},{3,0},{4,5},{5,6},{6,7},{7,4},{8,9},{9,10},{10,1... | collective-permute-start | bytes 1572872 | tf_op jit(solution)/shard_map/ppermute | solution.py:43
  27.2 15.7 %collective-permute-start.8 = (bf16[8,128,256]{2,1,0:T(8,128)(2,1)S(1)}, bf16[8,128,256]{2,1,0:T(8,128)(2,1)S(1)}, u32[]{:S(2)}, u32[]{:S(2)}) collective-permute-start(bf16[8,128,256]{2,1,0:T(8,128)(2,1)S(1)} %get-tuple-element.86), channel_id=1, source_target_pairs={{0,12},{1,13},{2,14},{3,15},{4,0},{5,1},{6,2},{7,3},{8,4},{9,5},{1... | collective-permute-start | bytes 1572872 | tf_op jit(solution)/shard_map/ppermute | solution.py:43
  30.1 20.1 %collective-permute-start.13 = (bf16[8,128,256]{2,1,0:T(8,128)(2,1)S(1)}, bf16[8,128,256]{2,1,0:T(8,128)(2,1)S(1)}, u32[]{:S(2)}, u32[]{:S(2)}) collective-permute-start(bf16[8,128,256]{2,1,0:T(8,128)(2,1)S(1)} %get-tuple-element.95), channel_id=1, source_target_pairs={{0,3},{1,0},{2,1},{3,2},{4,7},{5,4},{6,5},{7,6},{8,11},{9,8},{10,9... | collective-permute-start | bytes 1572872 | tf_op jit(solution)/shard_map/ppermute | solution.py:43
  43.0 19.4 %collective-permute-start.9 = (bf16[8,128,256]{2,1,0:T(8,128)(2,1)S(1)}, bf16[8,128,256]{2,1,0:T(8,128)(2,1)S(1)}, u32[]{:S(2)}, u32[]{:S(2)}) collective-permute-start(bf16[8,128,256]{2,1,0:T(8,128)(2,1)S(1)} %add_convert_fusion.1), channel_id=1, source_target_pairs={{0,12},{1,13},{2,14},{3,15},{4,0},{5,1},{6,2},{7,3},{8,4},{9,5},{1... | collective-permute-start | bytes 1572872 | tf_op jit(solution)/shard_map/ppermute | solution.py:43
  48.7 12.1 %collective-permute-start.11 = (bf16[8,128,256]{2,1,0:T(8,128)(2,1)S(1)}, bf16[8,128,256]{2,1,0:T(8,128)(2,1)S(1)}, u32[]{:S(2)}, u32[]{:S(2)}) collective-permute-start(bf16[8,128,256]{2,1,0:T(8,128)(2,1)S(1)} %get-tuple-element.91), channel_id=1, source_target_pairs={{0,1},{1,2},{2,3},{3,0},{4,5},{5,6},{6,7},{7,4},{8,9},{9,10},{10,1... | collective-permute-start | bytes 1572872 | tf_op jit(solution)/shard_map/ppermute | solution.py:43
  48.9 12.2 %collective-permute-start.6 = (bf16[8,128,256]{2,1,0:T(8,128)(2,1)S(1)}, bf16[8,128,256]{2,1,0:T(8,128)(2,1)S(1)}, u32[]{:S(2)}, u32[]{:S(2)}) collective-permute-start(bf16[8,128,256]{2,1,0:T(8,128)(2,1)S(1)} %get-tuple-element.82), channel_id=1, source_target_pairs={{0,4},{1,5},{2,6},{3,7},{4,8},{5,9},{6,10},{7,11},{8,12},{9,13},{1... | collective-permute-start | bytes 1572872 | tf_op jit(solution)/shard_map/ppermute | solution.py:43
  50.4 12.1 %collective-permute-start.14 = (bf16[8,128,256]{2,1,0:T(8,128)(2,1)S(1)}, bf16[8,128,256]{2,1,0:T(8,128)(2,1)S(1)}, u32[]{:S(2)}, u32[]{:S(2)}) collective-permute-start(bf16[8,128,256]{2,1,0:T(8,128)(2,1)S(1)} %add_convert_fusion), channel_id=1, source_target_pairs={{0,3},{1,0},{2,1},{3,2},{4,7},{5,4},{6,5},{7,6},{8,11},{9,8},{10,9... | collective-permute-start | bytes 1572872 | tf_op jit(solution)/shard_map/ppermute | solution.py:43
  89.9 11.0 %collective-permute-start.24 = (bf16[2,128,512]{2,1,0:T(8,128)(2,1)S(1)}, bf16[2,128,512]{2,1,0:T(8,128)(2,1)S(1)}, u32[]{:S(2)}, u32[]{:S(2)}) collective-permute-start(bf16[2,128,512]{2,1,0:T(8,128)(2,1)S(1)} %get-tuple-element.111), channel_id=1, source_target_pairs={{0,1},{2,3},{4,5},{6,7},{8,9},{10,11},{12,13},{14,15},{1,0},{3,2},... | collective-permute-start | bytes 786440 | tf_op jit(solution)/shard_map/ppermute | solution.py:301
  94.6 8.4 %collective-permute-start.26 = (bf16[2,128,512]{2,1,0:T(8,128)(2,1)S(1)}, bf16[2,128,512]{2,1,0:T(8,128)(2,1)S(1)}, u32[]{:S(2)}, u32[]{:S(2)}) collective-permute-start(bf16[2,128,512]{2,1,0:T(8,128)(2,1)S(1)} %get-tuple-element.113), channel_id=1, source_target_pairs={{0,16},{32,48},{64,80},{96,112},{16,0},{48,32},{80,64},{112,96},{1... | collective-permute-start | bytes 786440 | tf_op jit(solution)/shard_map/ppermute | solution.py:301
  110.8 16.8 %collective-permute-start.30 = (bf16[4,128,256]{2,1,0:T(8,128)(2,1)S(1)}, bf16[4,128,256]{2,1,0:T(8,128)(2,1)S(1)}, u32[]{:S(2)}, u32[]{:S(2)}) collective-permute-start(bf16[4,128,256]{2,1,0:T(8,128)(2,1)S(1)} %get-tuple-element.115), channel_id=1, source_target_pairs={{0,1},{1,2},{2,3},{3,0},{4,5},{5,6},{6,7},{7,4},{8,9},{9,10},{10,1... | collective-permute-start | bytes 786440 | tf_op jit(solution)/shard_map/ppermute | solution.py:43
  117.9 9.7 %collective-permute-start.33 = (bf16[4,128,256]{2,1,0:T(8,128)(2,1)S(1)}, bf16[4,128,256]{2,1,0:T(8,128)(2,1)S(1)}, u32[]{:S(2)}, u32[]{:S(2)}) collective-permute-start(bf16[4,128,256]{2,1,0:T(8,128)(2,1)S(1)} %get-tuple-element.117), channel_id=1, source_target_pairs={{0,4},{1,5},{2,6},{3,7},{4,8},{5,9},{6,10},{7,11},{8,12},{9,13},{1... | collective-permute-start | bytes 786440 | tf_op jit(solution)/shard_map/ppermute | solution.py:43
  118.3 9.9 %collective-permute-start.32 = (bf16[4,128,256]{2,1,0:T(8,128)(2,1)S(1)}, bf16[4,128,256]{2,1,0:T(8,128)(2,1)S(1)}, u32[]{:S(2)}, u32[]{:S(2)}) collective-permute-start(bf16[4,128,256]{2,1,0:T(8,128)(2,1)S(1)} %get-tuple-element.115), channel_id=1, source_target_pairs={{0,3},{1,0},{2,1},{3,2},{4,7},{5,4},{6,5},{7,6},{8,11},{9,8},{10,9... | collective-permute-start | bytes 786440 | tf_op jit(solution)/shard_map/ppermute | solution.py:43
  121.5 10.1 %collective-permute-start.38 = (bf16[4,128,256]{2,1,0:T(8,128)(2,1)S(1)}, bf16[4,128,256]{2,1,0:T(8,128)(2,1)S(1)}, u32[]{:S(2)}, u32[]{:S(2)}) collective-permute-start(bf16[4,128,256]{2,1,0:T(8,128)(2,1)S(1)} %get-tuple-element.117), channel_id=1, source_target_pairs={{0,12},{1,13},{2,14},{3,15},{4,0},{5,1},{6,2},{7,3},{8,4},{9,5},{1... | collective-permute-start | bytes 786440 | tf_op jit(solution)/shard_map/ppermute | solution.py:43
  127.6 9.3 %collective-permute-start.31 = (bf16[4,128,256]{2,1,0:T(8,128)(2,1)S(1)}, bf16[4,128,256]{2,1,0:T(8,128)(2,1)S(1)}, u32[]{:S(2)}, u32[]{:S(2)}) collective-permute-start(bf16[4,128,256]{2,1,0:T(8,128)(2,1)S(1)} %collective-permute-done.30), channel_id=1, source_target_pairs={{0,1},{1,2},{2,3},{3,0},{4,5},{5,6},{6,7},{7,4},{8,9},{9,10},{10,1... | collective-permute-start | bytes 786440 | tf_op jit(solution)/shard_map/ppermute | solution.py:43
  127.6 9.3 %collective-permute-start.34 = (bf16[4,128,256]{2,1,0:T(8,128)(2,1)S(1)}, bf16[4,128,256]{2,1,0:T(8,128)(2,1)S(1)}, u32[]{:S(2)}, u32[]{:S(2)}) collective-permute-start(bf16[4,128,256]{2,1,0:T(8,128)(2,1)S(1)} %collective-permute-done.33), channel_id=1, source_target_pairs={{0,4},{1,5},{2,6},{3,7},{4,8},{5,9},{6,10},{7,11},{8,12},{9,13},{1... | collective-permute-start | bytes 786440 | tf_op jit(solution)/shard_map/ppermute | solution.py:43
  128.2 13.8 %collective-permute-start.45 = (bf16[8,128,256]{2,1,0:T(8,128)(2,1)S(1)}, bf16[8,128,256]{2,1,0:T(8,128)(2,1)S(1)}, u32[]{:S(2)}, u32[]{:S(2)}) collective-permute-start(bf16[8,128,256]{2,1,0:T(8,128)(2,1)S(1)} %constant_dynamic-update-slice_fusion.4.rest_8_), channel_id=1, source_target_pairs={{0,3},{1,0},{2,1},{3,2},{4,7},{5,4},{6,5},{7,6},{8,11},{9,8},{10,9... | collective-permute-start | bytes 1572872 | tf_op jit(solution)/shard_map/ppermute | solution.py:43
  131.5 14.2 %collective-permute-start.39 = (bf16[8,128,256]{2,1,0:T(8,128)(2,1)S(1)}, bf16[8,128,256]{2,1,0:T(8,128)(2,1)S(1)}, u32[]{:S(2)}, u32[]{:S(2)}) collective-permute-start(bf16[8,128,256]{2,1,0:T(8,128)(2,1)S(1)} %constant_dynamic-update-slice_fusion.rest_0_), channel_id=1, source_target_pairs={{0,12},{1,13},{2,14},{3,15},{4,0},{5,1},{6,2},{7,3},{8,4},{9,5},{1... | collective-permute-start | bytes 1572872 | tf_op jit(solution)/shard_map/ppermute | solution.py:43
  136.9 14.1 %collective-permute-start.42 = (bf16[8,128,256]{2,1,0:T(8,128)(2,1)S(1)}, bf16[8,128,256]{2,1,0:T(8,128)(2,1)S(1)}, u32[]{:S(2)}, u32[]{:S(2)}) collective-permute-start(bf16[8,128,256]{2,1,0:T(8,128)(2,1)S(1)} %constant_dynamic-update-slice_fusion.4.rest_8_), channel_id=1, source_target_pairs={{0,1},{1,2},{2,3},{3,0},{4,5},{5,6},{6,7},{7,4},{8,9},{9,10},{10,1... | collective-permute-start | bytes 1572872 | tf_op jit(solution)/shard_map/ppermute | solution.py:43
  136.9 14.1 %collective-permute-start.35 = (bf16[8,128,256]{2,1,0:T(8,128)(2,1)S(1)}, bf16[8,128,256]{2,1,0:T(8,128)(2,1)S(1)}, u32[]{:S(2)}, u32[]{:S(2)}) collective-permute-start(bf16[8,128,256]{2,1,0:T(8,128)(2,1)S(1)} %constant_dynamic-update-slice_fusion.rest_0_), channel_id=1, source_target_pairs={{0,4},{1,5},{2,6},{3,7},{4,8},{5,9},{6,10},{7,11},{8,12},{9,13},{1... | collective-permute-start | bytes 1572872 | tf_op jit(solution)/shard_map/ppermute | solution.py:43
  142.0 13.3 %collective-permute-start.46 = (bf16[8,128,256]{2,1,0:T(8,128)(2,1)S(1)}, bf16[8,128,256]{2,1,0:T(8,128)(2,1)S(1)}, u32[]{:S(2)}, u32[]{:S(2)}) collective-permute-start(bf16[8,128,256]{2,1,0:T(8,128)(2,1)S(1)} %constant_dynamic-update-slice_fusion.6.rest_9_), channel_id=1, source_target_pairs={{0,3},{1,0},{2,1},{3,2},{4,7},{5,4},{6,5},{7,6},{8,11},{9,8},{10,9... | collective-permute-start | bytes 1572872 | tf_op jit(solution)/shard_map/ppermute | solution.py:43
  145.7 13.3 %collective-permute-start.40 = (bf16[8,128,256]{2,1,0:T(8,128)(2,1)S(1)}, bf16[8,128,256]{2,1,0:T(8,128)(2,1)S(1)}, u32[]{:S(2)}, u32[]{:S(2)}) collective-permute-start(bf16[8,128,256]{2,1,0:T(8,128)(2,1)S(1)} %constant_dynamic-update-slice_fusion.2.rest_1_), channel_id=1, source_target_pairs={{0,12},{1,13},{2,14},{3,15},{4,0},{5,1},{6,2},{7,3},{8,4},{9,5},{1... | collective-permute-start | bytes 1572872 | tf_op jit(solution)/shard_map/ppermute | solution.py:43
  151.0 13.2 %collective-permute-start.43 = (bf16[8,128,256]{2,1,0:T(8,128)(2,1)S(1)}, bf16[8,128,256]{2,1,0:T(8,128)(2,1)S(1)}, u32[]{:S(2)}, u32[]{:S(2)}) collective-permute-start(bf16[8,128,256]{2,1,0:T(8,128)(2,1)S(1)} %constant_dynamic-update-slice_fusion.6.rest_9_), channel_id=1, source_target_pairs={{0,1},{1,2},{2,3},{3,0},{4,5},{5,6},{6,7},{7,4},{8,9},{9,10},{10,1... | collective-permute-start | bytes 1572872 | tf_op jit(solution)/shard_map/ppermute | solution.py:43
  151.0 13.2 %collective-permute-start.36 = (bf16[8,128,256]{2,1,0:T(8,128)(2,1)S(1)}, bf16[8,128,256]{2,1,0:T(8,128)(2,1)S(1)}, u32[]{:S(2)}, u32[]{:S(2)}) collective-permute-start(bf16[8,128,256]{2,1,0:T(8,128)(2,1)S(1)} %constant_dynamic-update-slice_fusion.2.rest_1_), channel_id=1, source_target_pairs={{0,4},{1,5},{2,6},{3,7},{4,8},{5,9},{6,10},{7,11},{8,12},{9,13},{1... | collective-permute-start | bytes 1572872 | tf_op jit(solution)/shard_map/ppermute | solution.py:43
  155.3 12.3 %collective-permute-start.47 = (bf16[8,128,256]{2,1,0:T(8,128)(2,1)S(1)}, bf16[8,128,256]{2,1,0:T(8,128)(2,1)S(1)}, u32[]{:S(2)}, u32[]{:S(2)}) collective-permute-start(bf16[8,128,256]{2,1,0:T(8,128)(2,1)S(1)} %collective-permute-done.46.rest_15_), channel_id=1, source_target_pairs={{0,3},{1,0},{2,1},{3,2},{4,7},{5,4},{6,5},{7,6},{8,11},{9,8},{10,9... | collective-permute-start | bytes 1572872 | tf_op jit(solution)/shard_map/ppermute | solution.py:43
  159.0 11.6 %collective-permute-start.41 = (bf16[8,128,256]{2,1,0:T(8,128)(2,1)S(1)}, bf16[8,128,256]{2,1,0:T(8,128)(2,1)S(1)}, u32[]{:S(2)}, u32[]{:S(2)}) collective-permute-start(bf16[8,128,256]{2,1,0:T(8,128)(2,1)S(1)} %collective-permute-done.40.rest_7_), channel_id=1, source_target_pairs={{0,12},{1,13},{2,14},{3,15},{4,0},{5,1},{6,2},{7,3},{8,4},{9,5},{1... | collective-permute-start | bytes 1572872 | tf_op jit(solution)/shard_map/ppermute | solution.py:43
  164.1 12.2 %collective-permute-start.44 = (bf16[8,128,256]{2,1,0:T(8,128)(2,1)S(1)}, bf16[8,128,256]{2,1,0:T(8,128)(2,1)S(1)}, u32[]{:S(2)}, u32[]{:S(2)}) collective-permute-start(bf16[8,128,256]{2,1,0:T(8,128)(2,1)S(1)} %collective-permute-done.42.rest_10_), channel_id=1, source_target_pairs={{0,1},{1,2},{2,3},{3,0},{4,5},{5,6},{6,7},{7,4},{8,9},{9,10},{10,1... | collective-permute-start | bytes 1572872 | tf_op jit(solution)/shard_map/ppermute | solution.py:43
  164.2 12.2 %collective-permute-start.37 = (bf16[8,128,256]{2,1,0:T(8,128)(2,1)S(1)}, bf16[8,128,256]{2,1,0:T(8,128)(2,1)S(1)}, u32[]{:S(2)}, u32[]{:S(2)}) collective-permute-start(bf16[8,128,256]{2,1,0:T(8,128)(2,1)S(1)} %collective-permute-done.35.rest_2_), channel_id=1, source_target_pairs={{0,4},{1,5},{2,6},{3,7},{4,8},{5,9},{6,10},{7,11},{8,12},{9,13},{1... | collective-permute-start | bytes 1572872 | tf_op jit(solution)/shard_map/ppermute | solution.py:43
  (27 other events, 572.4 us)

commit v5 on v4

--- a/solution.py
+++ b/solution.py
@@ -141,11 +141,14 @@
         compiler_params=params(28),
         name="encode",
     )(*map(in_hbm, (g2m_dest.T, inputs_t, embed_weight, send_weight, g2m_edges)))
-    cuts = [(k, part) for k in range(4) for part in range(2)]
-    return [
-        dict(zip(cuts, lax.optimization_barrier([half[16 * k + 8 * part :][:8] for k, part in cuts])))
-        for half in halves
-    ]
+    early = ((2, 0), (3, 0), (2, 1))
+    late = [(k, part) for k in range(4) for part in range(2) if (k, part) not in early]
+    pieces = [{}, {}]
+    for cuts in (early, late):
+        values = [[half[16 * k + 8 * part :][:8] for k, part in cuts] for half in halves]
+        for piece, cut in zip(pieces, lax.optimization_barrier(values)):
+            piece.update(zip(cuts, cut))
+    return pieces
 
 
 def add(*values):

time: 183 us -> 182 us (level)
  transfers between devices with their start and end apart: 48 -> 48, of which waited for: 25 -> 29; matrix products, arithmetic and copies ran while one was open for 1% -> 1% of each run, Pallas kernels for 0% -> 0%
where the time goes in v5:
time: 182 us; the launch traced here: 181 us
  waiting for transfers between devices  83.3 us (46%)
  starting transfers between devices  75.1 us (41%)
  Pallas kernels  19.4 us (11%)
    ppermute x36, waiting for transfers between devices, shift(): return lax.ppermute(value, 'mesh', pairs)  66 us
    ppermute x36, starting transfers between devices, shift(): return lax.ppermute(value, 'mesh', pairs)  59.6 us
    ppermute x12, waiting for transfers between devices, trade(): return lax.ppermute(value, axis, pairs + [(b, a) for a, b in pairs])  17.4 us
    ppermute x12, starting transfers between devices, trade(): return lax.ppermute(value, axis, pairs + [(b, a) for a, b in pairs])  15.5 us
    pallas_call x1, Pallas kernels, encode(): pl.pallas_call(encode_kernel, in_specs=[pl.BlockSpec(memory_space=pltpu.S...  8.23 us
    pallas_call x1, Pallas kernels, decode(): pl.pallas_call(decode_kernel, grid_spec=pltpu.PrefetchScalarGridSpec(num_...  6.3 us
    pallas_call x2, Pallas kernels, mesh_step(): pl.pallas_call(functools.partial(step_kernel, layer), in_specs=[smem, sme...  3.89 us
  transfers between devices with their start and end apart: 48, of which 29 were waited for; matrix products, arithmetic and copies ran while one was open for 1% of the time, Pallas kernels for 0%

profile of v5, /device:TPU:2, one launch (start us, length us, event | category | flops | bytes accessed | tf_op | source)
XLA Modules:
  0.0 181.3 jit_solution(9532560753296609423)
XLA Ops:
  0.0 8.2 %encode.1 = (bf16[64,128,256]{2,1,0:T(8,128)(2,1)S(1)}, bf16[64,128,256]{2,1,0:T(8,128)(2,1)S(1)}) custom-call(s32[3,24]{1,0:T(4,128)} %bitcast.12, bf16[227,3072]{1,0:T(8,128)(2,1)} %bitcast.6, bf16[227,512]{1,0:T(8,128)(2,1)} %embed_hbm.1, bf16[512,512]{1,0:T(8,128)(2,1)} %send_hbm.1, bf16[24,3,128,128]{3,2,1,0:T(8,128)(2,1)} %edges_hbm.1), custom_call_target="tpu_custom_call" | custom-call | tf_op jit(solution)/shard_map/encode/pallas_call | solution.py:129
  13.1 2.2 %collective-permute-start.2 = (bf16[8,128,256]{2,1,0:T(8,128)(2,1)S(1)}, bf16[8,128,256]{2,1,0:T(8,128)(2,1)S(1)}, u32[]{:S(2)}, u32[]{:S(2)}) collective-permute-start(bf16[8,128,256]{2,1,0:T(8,128)(2,1)S(1)} %get-tuple-element.77), channel_id=1, source_target_pairs={{0,3},{1,0},{2,1},{3,2},{4,7},{5,4},{6,5},{7,6},{8,11},{9,8},{10,9... | collective-permute-start | bytes 1572872 | tf_op jit(solution)/shard_map/ppermute | solution.py:43
  17.0 8.6 %collective-permute-done = bf16[8,128,256]{2,1,0:T(8,128)(2,1)S(1)} collective-permute-done((bf16[8,128,256]{2,1,0:T(8,128)(2,1)S(1)}, bf16[8,128,256]{2,1,0:T(8,128)(2,1)S(1)}, u32[]{:S(2)}, u32[]{:S(2)}) %collective-permute-start) | collective-permute-done | bytes 524320 | tf_op jit(solution)/shard_map/ppermute | solution.py:43
  27.6 3.2 %collective-permute-start.13 = (bf16[8,128,256]{2,1,0:T(8,128)(2,1)S(1)}, bf16[8,128,256]{2,1,0:T(8,128)(2,1)S(1)}, u32[]{:S(2)}, u32[]{:S(2)}) collective-permute-start(bf16[8,128,256]{2,1,0:T(8,128)(2,1)S(1)} %get-tuple-element.95), channel_id=1, source_target_pairs={{0,3},{1,0},{2,1},{3,2},{4,7},{5,4},{6,5},{7,6},{8,11},{9,8},{10,9... | collective-permute-start | bytes 1572872 | tf_op jit(solution)/shard_map/ppermute | solution.py:43
  32.5 7.6 %collective-permute-done.1 = bf16[8,128,256]{2,1,0:T(8,128)(2,1)S(1)} collective-permute-done((bf16[8,128,256]{2,1,0:T(8,128)(2,1)S(1)}, bf16[8,128,256]{2,1,0:T(8,128)(2,1)S(1)}, u32[]{:S(2)}, u32[]{:S(2)}) %collective-permute-start.1) | collective-permute-done | bytes 524320 | tf_op jit(solution)/shard_map/ppermute | solution.py:43
  42.4 3.1 %collective-permute-start.14 = (bf16[8,128,256]{2,1,0:T(8,128)(2,1)S(1)}, bf16[8,128,256]{2,1,0:T(8,128)(2,1)S(1)}, u32[]{:S(2)}, u32[]{:S(2)}) collective-permute-start(bf16[8,128,256]{2,1,0:T(8,128)(2,1)S(1)} %add_convert_fusion), channel_id=1, source_target_pairs={{0,3},{1,0},{2,1},{3,2},{4,7},{5,4},{6,5},{7,6},{8,11},{9,8},{10,9... | collective-permute-start | bytes 1572872 | tf_op jit(solution)/shard_map/ppermute | solution.py:43
  45.5 2.6 %collective-permute-done.5 = bf16[4,128,256]{2,1,0:T(8,128)(2,1)S(1)} collective-permute-done((bf16[4,128,256]{2,1,0:T(8,128)(2,1)S(1)}, bf16[4,128,256]{2,1,0:T(8,128)(2,1)S(1)}, u32[]{:S(2)}, u32[]{:S(2)}) %collective-permute-start.5) | collective-permute-done | bytes 262176 | tf_op jit(solution)/shard_map/ppermute | solution.py:43
  49.8 3.3 %collective-permute-start.9 = (bf16[8,128,256]{2,1,0:T(8,128)(2,1)S(1)}, bf16[8,128,256]{2,1,0:T(8,128)(2,1)S(1)}, u32[]{:S(2)}, u32[]{:S(2)}) collective-permute-start(bf16[8,128,256]{2,1,0:T(8,128)(2,1)S(1)} %add_convert_fusion.1), channel_id=1, source_target_pairs={{0,12},{1,13},{2,14},{3,15},{4,0},{5,1},{6,2},{7,3},{8,4},{9,5},{1... | collective-permute-start | bytes 1572872 | tf_op jit(solution)/shard_map/ppermute | solution.py:43
  53.4 7.2 %collective-permute-done.6.refs_1_ = bf16[8,128,256]{2,1,0:T(8,128)(2,1)S(1)} collective-permute-done((bf16[8,128,256]{2,1,0:T(8,128)(2,1)S(1)}, bf16[8,128,256]{2,1,0:T(8,128)(2,1)S(1)}, u32[]{:S(2)}, u32[]{:S(2)}) %collective-permute-start.6) | collective-permute-done | bytes 524320 | tf_op jit(solution)/shard_map/ppermute | solution.py:43
  62.2 3.3 %collective-permute-start.15 = (bf16[4,128,256]{2,1,0:T(8,128)(2,1)S(1)}, bf16[4,128,256]{2,1,0:T(8,128)(2,1)S(1)}, u32[]{:S(2)}, u32[]{:S(2)}) collective-permute-start(bf16[4,128,256]{2,1,0:T(8,128)(2,1)S(1)} %add_convert_fusion.6), channel_id=1, source_target_pairs={{0,3},{1,0},{2,1},{3,2},{4,7},{5,4},{6,5},{7,6},{8,11},{9,8},{10,9... | collective-permute-start | bytes 786440 | tf_op jit(solution)/shard_map/ppermute | solution.py:43
  69.5 2.4 %collective-permute-done.17.refs_9_ = bf16[4,128,256]{2,1,0:T(8,128)(2,1)S(1)} collective-permute-done((bf16[4,128,256]{2,1,0:T(8,128)(2,1)S(1)}, bf16[4,128,256]{2,1,0:T(8,128)(2,1)S(1)}, u32[]{:S(2)}, u32[]{:S(2)}) %collective-permute-start.17) | collective-permute-done | bytes 262176 | tf_op jit(solution)/shard_map/ppermute | solution.py:43
  73.7 2.7 %collective-permute-start.21 = (bf16[2,128,512]{2,1,0:T(8,128)(2,1)S(1)}, bf16[2,128,512]{2,1,0:T(8,128)(2,1)S(1)}, u32[]{:S(2)}, u32[]{:S(2)}) collective-permute-start(bf16[2,128,512]{2,1,0:T(8,128)(2,1)S(1)} %get-tuple-element.106), channel_id=1, source_target_pairs={{16,32},{48,64},{80,96},{32,16},{64,48},{96,80},{17,33},{49,65},{8... | collective-permute-start | bytes 786440 | tf_op jit(solution)/shard_map/ppermute | solution.py:304
  76.4 2.9 %collective-permute-done.18.rest_1_ = bf16[2,128,512]{2,1,0:T(8,128)(2,1)S(1)} collective-permute-done((bf16[2,128,512]{2,1,0:T(8,128)(2,1)S(1)}, bf16[2,128,512]{2,1,0:T(8,128)(2,1)S(1)}, u32[]{:S(2)}, u32[]{:S(2)}) %collective-permute-start.18) | collective-permute-done | bytes 262176 | tf_op jit(solution)/shard_map/ppermute | solution.py:304
  79.5 2.5 %collective-permute-start.23 = (bf16[2,128,512]{2,1,0:T(8,128)(2,1)S(1)}, bf16[2,128,512]{2,1,0:T(8,128)(2,1)S(1)}, u32[]{:S(2)}, u32[]{:S(2)}) collective-permute-start(bf16[2,128,512]{2,1,0:T(8,128)(2,1)S(1)} %pad_maximum_fusion.1), channel_id=1, source_target_pairs={{16,32},{48,64},{80,96},{32,16},{64,48},{96,80},{17,33},{49,65},{8... | collective-permute-start | bytes 786440 | tf_op jit(solution)/shard_map/ppermute | solution.py:304
  82.1 5.1 %collective-permute-done.23.rest_6_ = bf16[2,128,512]{2,1,0:T(8,128)(2,1)S(1)} collective-permute-done((bf16[2,128,512]{2,1,0:T(8,128)(2,1)S(1)}, bf16[2,128,512]{2,1,0:T(8,128)(2,1)S(1)}, u32[]{:S(2)}, u32[]{:S(2)}) %collective-permute-start.23) | collective-permute-done | bytes 262176 | tf_op jit(solution)/shard_map/ppermute | solution.py:304
  89.2 3.9 %collective-permute-start.24 = (bf16[2,128,512]{2,1,0:T(8,128)(2,1)S(1)}, bf16[2,128,512]{2,1,0:T(8,128)(2,1)S(1)}, u32[]{:S(2)}, u32[]{:S(2)}) collective-permute-start(bf16[2,128,512]{2,1,0:T(8,128)(2,1)S(1)} %get-tuple-element.111), channel_id=1, source_target_pairs={{0,1},{2,3},{4,5},{6,7},{8,9},{10,11},{12,13},{14,15},{1,0},{3,2},... | collective-permute-start | bytes 786440 | tf_op jit(solution)/shard_map/ppermute | solution.py:304
  94.1 2.4 %collective-permute-start.27 = (bf16[2,128,512]{2,1,0:T(8,128)(2,1)S(1)}, bf16[2,128,512]{2,1,0:T(8,128)(2,1)S(1)}, u32[]{:S(2)}, u32[]{:S(2)}) collective-permute-start(bf16[2,128,512]{2,1,0:T(8,128)(2,1)S(1)} %get-tuple-element.114), channel_id=1, source_target_pairs={{16,32},{48,64},{80,96},{32,16},{64,48},{96,80},{17,33},{49,65},{8... | collective-permute-start | bytes 786440 | tf_op jit(solution)/shard_map/ppermute | solution.py:304
  96.5 3.6 %collective-permute-done.24.rest_1_ = bf16[2,128,512]{2,1,0:T(8,128)(2,1)S(1)} collective-permute-done((bf16[2,128,512]{2,1,0:T(8,128)(2,1)S(1)}, bf16[2,128,512]{2,1,0:T(8,128)(2,1)S(1)}, u32[]{:S(2)}, u32[]{:S(2)}) %collective-permute-start.24) | collective-permute-done | bytes 262176 | tf_op jit(solution)/shard_map/ppermute | solution.py:304
  102.3 5.7 %collective-permute-done.29.rest_6_ = bf16[2,128,512]{2,1,0:T(8,128)(2,1)S(1)} collective-permute-done((bf16[2,128,512]{2,1,0:T(8,128)(2,1)S(1)}, bf16[2,128,512]{2,1,0:T(8,128)(2,1)S(1)}, u32[]{:S(2)}, u32[]{:S(2)}) %collective-permute-start.29) | collective-permute-done | bytes 262176 | tf_op jit(solution)/shard_map/ppermute | solution.py:304
  110.0 4.7 %collective-permute-start.30 = (bf16[4,128,256]{2,1,0:T(8,128)(2,1)S(1)}, bf16[4,128,256]{2,1,0:T(8,128)(2,1)S(1)}, u32[]{:S(2)}, u32[]{:S(2)}) collective-permute-start(bf16[4,128,256]{2,1,0:T(8,128)(2,1)S(1)} %get-tuple-element.115), channel_id=1, source_target_pairs={{0,1},{1,2},{2,3},{3,0},{4,5},{5,6},{6,7},{7,4},{8,9},{9,10},{10,1... | collective-permute-start | bytes 786440 | tf_op jit(solution)/shard_map/ppermute | solution.py:43
  114.7 2.6 %collective-permute-start.33 = (bf16[4,128,256]{2,1,0:T(8,128)(2,1)S(1)}, bf16[4,128,256]{2,1,0:T(8,128)(2,1)S(1)}, u32[]{:S(2)}, u32[]{:S(2)}) collective-permute-start(bf16[4,128,256]{2,1,0:T(8,128)(2,1)S(1)} %get-tuple-element.117), channel_id=1, source_target_pairs={{0,4},{1,5},{2,6},{3,7},{4,8},{5,9},{6,10},{7,11},{8,12},{9,13},{1... | collective-permute-start | bytes 786440 | tf_op jit(solution)/shard_map/ppermute | solution.py:43
  117.3 3.2 %collective-permute-start.32 = (bf16[4,128,256]{2,1,0:T(8,128)(2,1)S(1)}, bf16[4,128,256]{2,1,0:T(8,128)(2,1)S(1)}, u32[]{:S(2)}, u32[]{:S(2)}) collective-permute-start(bf16[4,128,256]{2,1,0:T(8,128)(2,1)S(1)} %get-tuple-element.115), channel_id=1, source_target_pairs={{0,3},{1,0},{2,1},{3,2},{4,7},{5,4},{6,5},{7,6},{8,11},{9,8},{10,9... | collective-permute-start | bytes 786440 | tf_op jit(solution)/shard_map/ppermute | solution.py:43
  127.2 3.3 %collective-permute-start.45 = (bf16[8,128,256]{2,1,0:T(8,128)(2,1)S(1)}, bf16[8,128,256]{2,1,0:T(8,128)(2,1)S(1)}, u32[]{:S(2)}, u32[]{:S(2)}) collective-permute-start(bf16[8,128,256]{2,1,0:T(8,128)(2,1)S(1)} %constant_dynamic-update-slice_fusion.4.rest_8_), channel_id=1, source_target_pairs={{0,3},{1,0},{2,1},{3,2},{4,7},{5,4},{6,5},{7,6},{8,11},{9,8},{10,9... | collective-permute-start | bytes 1572872 | tf_op jit(solution)/shard_map/ppermute | solution.py:43
  136.4 4.6 %collective-permute-done.45.rest_14_ = bf16[8,128,256]{2,1,0:T(8,128)(2,1)S(1)} collective-permute-done((bf16[8,128,256]{2,1,0:T(8,128)(2,1)S(1)}, bf16[8,128,256]{2,1,0:T(8,128)(2,1)S(1)}, u32[]{:S(2)}, u32[]{:S(2)}) %collective-permute-start.45) | collective-permute-done | bytes 524320 | tf_op jit(solution)/shard_map/ppermute | solution.py:43
  141.0 3.7 %collective-permute-start.46 = (bf16[8,128,256]{2,1,0:T(8,128)(2,1)S(1)}, bf16[8,128,256]{2,1,0:T(8,128)(2,1)S(1)}, u32[]{:S(2)}, u32[]{:S(2)}) collective-permute-start(bf16[8,128,256]{2,1,0:T(8,128)(2,1)S(1)} %constant_dynamic-update-slice_fusion.6.rest_9_), channel_id=1, source_target_pairs={{0,3},{1,0},{2,1},{3,2},{4,7},{5,4},{6,5},{7,6},{8,11},{9,8},{10,9... | collective-permute-start | bytes 1572872 | tf_op jit(solution)/shard_map/ppermute | solution.py:43
  150.2 4.1 %collective-permute-done.46.rest_15_ = bf16[8,128,256]{2,1,0:T(8,128)(2,1)S(1)} collective-permute-done((bf16[8,128,256]{2,1,0:T(8,128)(2,1)S(1)}, bf16[8,128,256]{2,1,0:T(8,128)(2,1)S(1)}, u32[]{:S(2)}, u32[]{:S(2)}) %collective-permute-start.46) | collective-permute-done | bytes 524320 | tf_op jit(solution)/shard_map/ppermute | solution.py:43
  154.3 3.7 %collective-permute-start.47 = (bf16[8,128,256]{2,1,0:T(8,128)(2,1)S(1)}, bf16[8,128,256]{2,1,0:T(8,128)(2,1)S(1)}, u32[]{:S(2)}, u32[]{:S(2)}) collective-permute-start(bf16[8,128,256]{2,1,0:T(8,128)(2,1)S(1)} %collective-permute-done.46.rest_15_), channel_id=1, source_target_pairs={{0,3},{1,0},{2,1},{3,2},{4,7},{5,4},{6,5},{7,6},{8,11},{9,8},{10,9... | collective-permute-start | bytes 1572872 | tf_op jit(solution)/shard_map/ppermute | solution.py:43
  158.0 2.3 %collective-permute-start.41 = (bf16[8,128,256]{2,1,0:T(8,128)(2,1)S(1)}, bf16[8,128,256]{2,1,0:T(8,128)(2,1)S(1)}, u32[]{:S(2)}, u32[]{:S(2)}) collective-permute-start(bf16[8,128,256]{2,1,0:T(8,128)(2,1)S(1)} %collective-permute-done.40.rest_7_), channel_id=1, source_target_pairs={{0,12},{1,13},{2,14},{3,15},{4,0},{5,1},{6,2},{7,3},{8,4},{9,5},{1... | collective-permute-start | bytes 1572872 | tf_op jit(solution)/shard_map/ppermute | solution.py:43
  163.1 3.5 %collective-permute-done.47.rest_13_ = bf16[8,128,256]{2,1,0:T(8,128)(2,1)S(1)} collective-permute-done((bf16[8,128,256]{2,1,0:T(8,128)(2,1)S(1)}, bf16[8,128,256]{2,1,0:T(8,128)(2,1)S(1)}, u32[]{:S(2)}, u32[]{:S(2)}) %collective-permute-start.47) | collective-permute-done | bytes 524320 | tf_op jit(solution)/shard_map/ppermute | solution.py:43
  166.6 2.2 %collective-permute-done.41.rest_5_ = bf16[8,128,256]{2,1,0:T(8,128)(2,1)S(1)} collective-permute-done((bf16[8,128,256]{2,1,0:T(8,128)(2,1)S(1)}, bf16[8,128,256]{2,1,0:T(8,128)(2,1)S(1)}, u32[]{:S(2)}, u32[]{:S(2)}) %collective-permute-start.41) | collective-permute-done | bytes 524320 | tf_op jit(solution)/shard_map/ppermute | solution.py:43
  168.9 4.4 %collective-permute-done.44.rest_12_ = bf16[8,128,256]{2,1,0:T(8,128)(2,1)S(1)} collective-permute-done((bf16[8,128,256]{2,1,0:T(8,128)(2,1)S(1)}, bf16[8,128,256]{2,1,0:T(8,128)(2,1)S(1)}, u32[]{:S(2)}, u32[]{:S(2)}) %collective-permute-start.44) | collective-permute-done | bytes 524320 | tf_op jit(solution)/shard_map/ppermute | solution.py:43
  174.8 6.3 %decode.1 = bf16[227,3072]{1,0:T(8,128)(2,1)} custom-call(s32[3,24]{1,0:T(4,128)S(1)} %bitcast.11, bf16[227,3072]{1,0:T(8,128)(2,1)S(1)} %bitcast.7, bf16[24,3,128,128]{3,2,1,0:T(8,128)(2,1)S(1)} %copy-done.3, bf16[227,512]{1,0:T(8,128)(2,1)S(1)} %bitcast.8, bf16[8,128,256]{2,1,0:T(8,128)(2,1)S(1)} %constant_dynamic-update-slice_fusion.rest_0_, ...), custom_call_target="tpu_custom_call" | custom-call | tf_op jit(solution)/shard_map/decode/pallas_call | solution.py:380
  (118 shorter events, 51.3 us)
Async XLA Ops:
  9.5 16.0 %collective-permute-start = (bf16[8,128,256]{2,1,0:T(8,128)(2,1)S(1)}, bf16[8,128,256]{2,1,0:T(8,128)(2,1)S(1)}, u32[]{:S(2)}, u32[]{:S(2)}) collective-permute-start(bf16[8,128,256]{2,1,0:T(8,128)(2,1)S(1)} %get-tuple-element.75), channel_id=1, source_target_pairs={{0,1},{1,2},{2,3},{3,0},{4,5},{5,6},{6,7},{7,4},{8,9},{9,10},{10,1... | collective-permute-start | bytes 1572872 | tf_op jit(solution)/shard_map/ppermute | solution.py:43
  11.5 14.7 %collective-permute-start.3 = (bf16[8,128,256]{2,1,0:T(8,128)(2,1)S(1)}, bf16[8,128,256]{2,1,0:T(8,128)(2,1)S(1)}, u32[]{:S(2)}, u32[]{:S(2)}) collective-permute-start(bf16[8,128,256]{2,1,0:T(8,128)(2,1)S(1)} %get-tuple-element.79), channel_id=1, source_target_pairs={{0,4},{1,5},{2,6},{3,7},{4,8},{5,9},{6,10},{7,11},{8,12},{9,13},{1... | collective-permute-start | bytes 1572872 | tf_op jit(solution)/shard_map/ppermute | solution.py:43
  13.1 14.5 %collective-permute-start.2 = (bf16[8,128,256]{2,1,0:T(8,128)(2,1)S(1)}, bf16[8,128,256]{2,1,0:T(8,128)(2,1)S(1)}, u32[]{:S(2)}, u32[]{:S(2)}) collective-permute-start(bf16[8,128,256]{2,1,0:T(8,128)(2,1)S(1)} %get-tuple-element.77), channel_id=1, source_target_pairs={{0,3},{1,0},{2,1},{3,2},{4,7},{5,4},{6,5},{7,6},{8,11},{9,8},{10,9... | collective-permute-start | bytes 1572872 | tf_op jit(solution)/shard_map/ppermute | solution.py:43
  15.3 15.5 %collective-permute-start.7 = (bf16[8,128,256]{2,1,0:T(8,128)(2,1)S(1)}, bf16[8,128,256]{2,1,0:T(8,128)(2,1)S(1)}, u32[]{:S(2)}, u32[]{:S(2)}) collective-permute-start(bf16[8,128,256]{2,1,0:T(8,128)(2,1)S(1)} %get-tuple-element.85), channel_id=1, source_target_pairs={{0,12},{1,13},{2,14},{3,15},{4,0},{5,1},{6,2},{7,3},{8,4},{9,5},{1... | collective-permute-start | bytes 1572872 | tf_op jit(solution)/shard_map/ppermute | solution.py:43
  25.7 14.4 %collective-permute-start.1 = (bf16[8,128,256]{2,1,0:T(8,128)(2,1)S(1)}, bf16[8,128,256]{2,1,0:T(8,128)(2,1)S(1)}, u32[]{:S(2)}, u32[]{:S(2)}) collective-permute-start(bf16[8,128,256]{2,1,0:T(8,128)(2,1)S(1)} %add_convert_fusion.3), channel_id=1, source_target_pairs={{0,1},{1,2},{2,3},{3,0},{4,5},{5,6},{6,7},{7,4},{8,9},{9,10},{10,1... | collective-permute-start | bytes 1572872 | tf_op jit(solution)/shard_map/ppermute | solution.py:43
  26.3 14.1 %collective-permute-start.4 = (bf16[8,128,256]{2,1,0:T(8,128)(2,1)S(1)}, bf16[8,128,256]{2,1,0:T(8,128)(2,1)S(1)}, u32[]{:S(2)}, u32[]{:S(2)}) collective-permute-start(bf16[8,128,256]{2,1,0:T(8,128)(2,1)S(1)} %add_convert_fusion.2), channel_id=1, source_target_pairs={{0,4},{1,5},{2,6},{3,7},{4,8},{5,9},{6,10},{7,11},{8,12},{9,13},{1... | collective-permute-start | bytes 1572872 | tf_op jit(solution)/shard_map/ppermute | solution.py:43
  27.6 14.7 %collective-permute-start.13 = (bf16[8,128,256]{2,1,0:T(8,128)(2,1)S(1)}, bf16[8,128,256]{2,1,0:T(8,128)(2,1)S(1)}, u32[]{:S(2)}, u32[]{:S(2)}) collective-permute-start(bf16[8,128,256]{2,1,0:T(8,128)(2,1)S(1)} %get-tuple-element.95), channel_id=1, source_target_pairs={{0,3},{1,0},{2,1},{3,2},{4,7},{5,4},{6,5},{7,6},{8,11},{9,8},{10,9... | collective-permute-start | bytes 1572872 | tf_op jit(solution)/shard_map/ppermute | solution.py:43
  30.8 18.8 %collective-permute-start.8 = (bf16[8,128,256]{2,1,0:T(8,128)(2,1)S(1)}, bf16[8,128,256]{2,1,0:T(8,128)(2,1)S(1)}, u32[]{:S(2)}, u32[]{:S(2)}) collective-permute-start(bf16[8,128,256]{2,1,0:T(8,128)(2,1)S(1)} %get-tuple-element.86), channel_id=1, source_target_pairs={{0,12},{1,13},{2,14},{3,15},{4,0},{5,1},{6,2},{7,3},{8,4},{9,5},{1... | collective-permute-start | bytes 1572872 | tf_op jit(solution)/shard_map/ppermute | solution.py:43
  42.4 19.5 %collective-permute-start.14 = (bf16[8,128,256]{2,1,0:T(8,128)(2,1)S(1)}, bf16[8,128,256]{2,1,0:T(8,128)(2,1)S(1)}, u32[]{:S(2)}, u32[]{:S(2)}) collective-permute-start(bf16[8,128,256]{2,1,0:T(8,128)(2,1)S(1)} %add_convert_fusion), channel_id=1, source_target_pairs={{0,3},{1,0},{2,1},{3,2},{4,7},{5,4},{6,5},{7,6},{8,11},{9,8},{10,9... | collective-permute-start | bytes 1572872 | tf_op jit(solution)/shard_map/ppermute | solution.py:43
  48.1 12.4 %collective-permute-start.6 = (bf16[8,128,256]{2,1,0:T(8,128)(2,1)S(1)}, bf16[8,128,256]{2,1,0:T(8,128)(2,1)S(1)}, u32[]{:S(2)}, u32[]{:S(2)}) collective-permute-start(bf16[8,128,256]{2,1,0:T(8,128)(2,1)S(1)} %get-tuple-element.82), channel_id=1, source_target_pairs={{0,4},{1,5},{2,6},{3,7},{4,8},{5,9},{6,10},{7,11},{8,12},{9,13},{1... | collective-permute-start | bytes 1572872 | tf_op jit(solution)/shard_map/ppermute | solution.py:43
  49.6 12.3 %collective-permute-start.11 = (bf16[8,128,256]{2,1,0:T(8,128)(2,1)S(1)}, bf16[8,128,256]{2,1,0:T(8,128)(2,1)S(1)}, u32[]{:S(2)}, u32[]{:S(2)}) collective-permute-start(bf16[8,128,256]{2,1,0:T(8,128)(2,1)S(1)} %get-tuple-element.91), channel_id=1, source_target_pairs={{0,1},{1,2},{2,3},{3,0},{4,5},{5,6},{6,7},{7,4},{8,9},{9,10},{10,1... | collective-permute-start | bytes 1572872 | tf_op jit(solution)/shard_map/ppermute | solution.py:43
  49.8 12.2 %collective-permute-start.9 = (bf16[8,128,256]{2,1,0:T(8,128)(2,1)S(1)}, bf16[8,128,256]{2,1,0:T(8,128)(2,1)S(1)}, u32[]{:S(2)}, u32[]{:S(2)}) collective-permute-start(bf16[8,128,256]{2,1,0:T(8,128)(2,1)S(1)} %add_convert_fusion.1), channel_id=1, source_target_pairs={{0,12},{1,13},{2,14},{3,15},{4,0},{5,1},{6,2},{7,3},{8,4},{9,5},{1... | collective-permute-start | bytes 1572872 | tf_op jit(solution)/shard_map/ppermute | solution.py:43
  73.6 8.5 %collective-permute-start.20 = (bf16[2,128,512]{2,1,0:T(8,128)(2,1)S(1)}, bf16[2,128,512]{2,1,0:T(8,128)(2,1)S(1)}, u32[]{:S(2)}, u32[]{:S(2)}) collective-permute-start(bf16[2,128,512]{2,1,0:T(8,128)(2,1)S(1)} %get-tuple-element.105), channel_id=1, source_target_pairs={{0,16},{32,48},{64,80},{96,112},{16,0},{48,32},{80,64},{112,96},{1... | collective-permute-start | bytes 786440 | tf_op jit(solution)/shard_map/ppermute | solution.py:304
  89.2 10.9 %collective-permute-start.24 = (bf16[2,128,512]{2,1,0:T(8,128)(2,1)S(1)}, bf16[2,128,512]{2,1,0:T(8,128)(2,1)S(1)}, u32[]{:S(2)}, u32[]{:S(2)}) collective-permute-start(bf16[2,128,512]{2,1,0:T(8,128)(2,1)S(1)} %get-tuple-element.111), channel_id=1, source_target_pairs={{0,1},{2,3},{4,5},{6,7},{8,9},{10,11},{12,13},{14,15},{1,0},{3,2},... | collective-permute-start | bytes 786440 | tf_op jit(solution)/shard_map/ppermute | solution.py:304
  110.0 14.4 %collective-permute-start.30 = (bf16[4,128,256]{2,1,0:T(8,128)(2,1)S(1)}, bf16[4,128,256]{2,1,0:T(8,128)(2,1)S(1)}, u32[]{:S(2)}, u32[]{:S(2)}) collective-permute-start(bf16[4,128,256]{2,1,0:T(8,128)(2,1)S(1)} %get-tuple-element.115), channel_id=1, source_target_pairs={{0,1},{1,2},{2,3},{3,0},{4,5},{5,6},{6,7},{7,4},{8,9},{9,10},{10,1... | collective-permute-start | bytes 786440 | tf_op jit(solution)/shard_map/ppermute | solution.py:43
  114.7 11.3 %collective-permute-start.33 = (bf16[4,128,256]{2,1,0:T(8,128)(2,1)S(1)}, bf16[4,128,256]{2,1,0:T(8,128)(2,1)S(1)}, u32[]{:S(2)}, u32[]{:S(2)}) collective-permute-start(bf16[4,128,256]{2,1,0:T(8,128)(2,1)S(1)} %get-tuple-element.117), channel_id=1, source_target_pairs={{0,4},{1,5},{2,6},{3,7},{4,8},{5,9},{6,10},{7,11},{8,12},{9,13},{1... | collective-permute-start | bytes 786440 | tf_op jit(solution)/shard_map/ppermute | solution.py:43
  117.3 9.9 %collective-permute-start.32 = (bf16[4,128,256]{2,1,0:T(8,128)(2,1)S(1)}, bf16[4,128,256]{2,1,0:T(8,128)(2,1)S(1)}, u32[]{:S(2)}, u32[]{:S(2)}) collective-permute-start(bf16[4,128,256]{2,1,0:T(8,128)(2,1)S(1)} %get-tuple-element.115), channel_id=1, source_target_pairs={{0,3},{1,0},{2,1},{3,2},{4,7},{5,4},{6,5},{7,6},{8,11},{9,8},{10,9... | collective-permute-start | bytes 786440 | tf_op jit(solution)/shard_map/ppermute | solution.py:43
  120.5 10.1 %collective-permute-start.38 = (bf16[4,128,256]{2,1,0:T(8,128)(2,1)S(1)}, bf16[4,128,256]{2,1,0:T(8,128)(2,1)S(1)}, u32[]{:S(2)}, u32[]{:S(2)}) collective-permute-start(bf16[4,128,256]{2,1,0:T(8,128)(2,1)S(1)} %get-tuple-element.117), channel_id=1, source_target_pairs={{0,12},{1,13},{2,14},{3,15},{4,0},{5,1},{6,2},{7,3},{8,4},{9,5},{1... | collective-permute-start | bytes 786440 | tf_op jit(solution)/shard_map/ppermute | solution.py:43
  124.4 9.3 %collective-permute-start.31 = (bf16[4,128,256]{2,1,0:T(8,128)(2,1)S(1)}, bf16[4,128,256]{2,1,0:T(8,128)(2,1)S(1)}, u32[]{:S(2)}, u32[]{:S(2)}) collective-permute-start(bf16[4,128,256]{2,1,0:T(8,128)(2,1)S(1)} %collective-permute-done.30), channel_id=1, source_target_pairs={{0,1},{1,2},{2,3},{3,0},{4,5},{5,6},{6,7},{7,4},{8,9},{9,10},{10,1... | collective-permute-start | bytes 786440 | tf_op jit(solution)/shard_map/ppermute | solution.py:43
  126.0 9.3 %collective-permute-start.34 = (bf16[4,128,256]{2,1,0:T(8,128)(2,1)S(1)}, bf16[4,128,256]{2,1,0:T(8,128)(2,1)S(1)}, u32[]{:S(2)}, u32[]{:S(2)}) collective-permute-start(bf16[4,128,256]{2,1,0:T(8,128)(2,1)S(1)} %collective-permute-done.33), channel_id=1, source_target_pairs={{0,4},{1,5},{2,6},{3,7},{4,8},{5,9},{6,10},{7,11},{8,12},{9,13},{1... | collective-permute-start | bytes 786440 | tf_op jit(solution)/shard_map/ppermute | solution.py:43
  127.2 13.8 %collective-permute-start.45 = (bf16[8,128,256]{2,1,0:T(8,128)(2,1)S(1)}, bf16[8,128,256]{2,1,0:T(8,128)(2,1)S(1)}, u32[]{:S(2)}, u32[]{:S(2)}) collective-permute-start(bf16[8,128,256]{2,1,0:T(8,128)(2,1)S(1)} %constant_dynamic-update-slice_fusion.4.rest_8_), channel_id=1, source_target_pairs={{0,3},{1,0},{2,1},{3,2},{4,7},{5,4},{6,5},{7,6},{8,11},{9,8},{10,9... | collective-permute-start | bytes 1572872 | tf_op jit(solution)/shard_map/ppermute | solution.py:43
  130.6 14.2 %collective-permute-start.39 = (bf16[8,128,256]{2,1,0:T(8,128)(2,1)S(1)}, bf16[8,128,256]{2,1,0:T(8,128)(2,1)S(1)}, u32[]{:S(2)}, u32[]{:S(2)}) collective-permute-start(bf16[8,128,256]{2,1,0:T(8,128)(2,1)S(1)} %constant_dynamic-update-slice_fusion.rest_0_), channel_id=1, source_target_pairs={{0,12},{1,13},{2,14},{3,15},{4,0},{5,1},{6,2},{7,3},{8,4},{9,5},{1... | collective-permute-start | bytes 1572872 | tf_op jit(solution)/shard_map/ppermute | solution.py:43
  133.7 14.1 %collective-permute-start.42 = (bf16[8,128,256]{2,1,0:T(8,128)(2,1)S(1)}, bf16[8,128,256]{2,1,0:T(8,128)(2,1)S(1)}, u32[]{:S(2)}, u32[]{:S(2)}) collective-permute-start(bf16[8,128,256]{2,1,0:T(8,128)(2,1)S(1)} %constant_dynamic-update-slice_fusion.4.rest_8_), channel_id=1, source_target_pairs={{0,1},{1,2},{2,3},{3,0},{4,5},{5,6},{6,7},{7,4},{8,9},{9,10},{10,1... | collective-permute-start | bytes 1572872 | tf_op jit(solution)/shard_map/ppermute | solution.py:43
  135.3 14.1 %collective-permute-start.35 = (bf16[8,128,256]{2,1,0:T(8,128)(2,1)S(1)}, bf16[8,128,256]{2,1,0:T(8,128)(2,1)S(1)}, u32[]{:S(2)}, u32[]{:S(2)}) collective-permute-start(bf16[8,128,256]{2,1,0:T(8,128)(2,1)S(1)} %constant_dynamic-update-slice_fusion.rest_0_), channel_id=1, source_target_pairs={{0,4},{1,5},{2,6},{3,7},{4,8},{5,9},{6,10},{7,11},{8,12},{9,13},{1... | collective-permute-start | bytes 1572872 | tf_op jit(solution)/shard_map/ppermute | solution.py:43
  141.0 13.3 %collective-permute-start.46 = (bf16[8,128,256]{2,1,0:T(8,128)(2,1)S(1)}, bf16[8,128,256]{2,1,0:T(8,128)(2,1)S(1)}, u32[]{:S(2)}, u32[]{:S(2)}) collective-permute-start(bf16[8,128,256]{2,1,0:T(8,128)(2,1)S(1)} %constant_dynamic-update-slice_fusion.6.rest_9_), channel_id=1, source_target_pairs={{0,3},{1,0},{2,1},{3,2},{4,7},{5,4},{6,5},{7,6},{8,11},{9,8},{10,9... | collective-permute-start | bytes 1572872 | tf_op jit(solution)/shard_map/ppermute | solution.py:43
  144.7 13.3 %collective-permute-start.40 = (bf16[8,128,256]{2,1,0:T(8,128)(2,1)S(1)}, bf16[8,128,256]{2,1,0:T(8,128)(2,1)S(1)}, u32[]{:S(2)}, u32[]{:S(2)}) collective-permute-start(bf16[8,128,256]{2,1,0:T(8,128)(2,1)S(1)} %constant_dynamic-update-slice_fusion.2.rest_1_), channel_id=1, source_target_pairs={{0,12},{1,13},{2,14},{3,15},{4,0},{5,1},{6,2},{7,3},{8,4},{9,5},{1... | collective-permute-start | bytes 1572872 | tf_op jit(solution)/shard_map/ppermute | solution.py:43
  147.8 13.2 %collective-permute-start.43 = (bf16[8,128,256]{2,1,0:T(8,128)(2,1)S(1)}, bf16[8,128,256]{2,1,0:T(8,128)(2,1)S(1)}, u32[]{:S(2)}, u32[]{:S(2)}) collective-permute-start(bf16[8,128,256]{2,1,0:T(8,128)(2,1)S(1)} %constant_dynamic-update-slice_fusion.6.rest_9_), channel_id=1, source_target_pairs={{0,1},{1,2},{2,3},{3,0},{4,5},{5,6},{6,7},{7,4},{8,9},{9,10},{10,1... | collective-permute-start | bytes 1572872 | tf_op jit(solution)/shard_map/ppermute | solution.py:43
  149.4 13.2 %collective-permute-start.36 = (bf16[8,128,256]{2,1,0:T(8,128)(2,1)S(1)}, bf16[8,128,256]{2,1,0:T(8,128)(2,1)S(1)}, u32[]{:S(2)}, u32[]{:S(2)}) collective-permute-start(bf16[8,128,256]{2,1,0:T(8,128)(2,1)S(1)} %constant_dynamic-update-slice_fusion.2.rest_1_), channel_id=1, source_target_pairs={{0,4},{1,5},{2,6},{3,7},{4,8},{5,9},{6,10},{7,11},{8,12},{9,13},{1... | collective-permute-start | bytes 1572872 | tf_op jit(solution)/shard_map/ppermute | solution.py:43
  154.3 12.3 %collective-permute-start.47 = (bf16[8,128,256]{2,1,0:T(8,128)(2,1)S(1)}, bf16[8,128,256]{2,1,0:T(8,128)(2,1)S(1)}, u32[]{:S(2)}, u32[]{:S(2)}) collective-permute-start(bf16[8,128,256]{2,1,0:T(8,128)(2,1)S(1)} %collective-permute-done.46.rest_15_), channel_id=1, source_target_pairs={{0,3},{1,0},{2,1},{3,2},{4,7},{5,4},{6,5},{7,6},{8,11},{9,8},{10,9... | collective-permute-start | bytes 1572872 | tf_op jit(solution)/shard_map/ppermute | solution.py:43
  158.0 10.9 %collective-permute-start.41 = (bf16[8,128,256]{2,1,0:T(8,128)(2,1)S(1)}, bf16[8,128,256]{2,1,0:T(8,128)(2,1)S(1)}, u32[]{:S(2)}, u32[]{:S(2)}) collective-permute-start(bf16[8,128,256]{2,1,0:T(8,128)(2,1)S(1)} %collective-permute-done.40.rest_7_), channel_id=1, source_target_pairs={{0,12},{1,13},{2,14},{3,15},{4,0},{5,1},{6,2},{7,3},{8,4},{9,5},{1... | collective-permute-start | bytes 1572872 | tf_op jit(solution)/shard_map/ppermute | solution.py:43
  161.0 12.3 %collective-permute-start.44 = (bf16[8,128,256]{2,1,0:T(8,128)(2,1)S(1)}, bf16[8,128,256]{2,1,0:T(8,128)(2,1)S(1)}, u32[]{:S(2)}, u32[]{:S(2)}) collective-permute-start(bf16[8,128,256]{2,1,0:T(8,128)(2,1)S(1)} %collective-permute-done.42.rest_10_), channel_id=1, source_target_pairs={{0,1},{1,2},{2,3},{3,0},{4,5},{5,6},{6,7},{7,4},{8,9},{9,10},{10,1... | collective-permute-start | bytes 1572872 | tf_op jit(solution)/shard_map/ppermute | solution.py:43
  162.6 12.2 %collective-permute-start.37 = (bf16[8,128,256]{2,1,0:T(8,128)(2,1)S(1)}, bf16[8,128,256]{2,1,0:T(8,128)(2,1)S(1)}, u32[]{:S(2)}, u32[]{:S(2)}) collective-permute-start(bf16[8,128,256]{2,1,0:T(8,128)(2,1)S(1)} %collective-permute-done.35.rest_2_), channel_id=1, source_target_pairs={{0,4},{1,5},{2,6},{3,7},{4,8},{5,9},{6,10},{7,11},{8,12},{9,13},{1... | collective-permute-start | bytes 1572872 | tf_op jit(solution)/shard_map/ppermute | solution.py:43
  (27 other events, 565.1 us)
